TPU v7x, 32 devices: a whole 2x2x4 slice. The times are simulated.
32 devices in a mesh: dp: 8 (over z, core), tensor: 4 (over y, x).
Axes of the slice: x: 2, y: 2, z: 4, core: 2. Of those that a mesh axis runs over, the one named last changes fastest.
Arguments:
- hidden_in: bfloat16 [8192, 2048], P('dp'), may hold values from -6 to 6
- self_out: bfloat16 [8192, 2048], P('dp'), may hold values from -6 to 6
- out_grad: bfloat16 [8192, 2048], P('dp'), may hold values from -6 to 6
- lengths: int32 [8], P('dp'), may hold values from 256 to 1024, as said below
- w_query: bfloat16 [2048, 2048], P('dp', 'tensor'), may hold values from -0.125 to 0.125
- w_key: bfloat16 [2048, 2048], P('dp', 'tensor'), may hold values from -0.125 to 0.125
- w_value: bfloat16 [2048, 2048], P('dp', 'tensor'), may hold values from -0.125 to 0.125
- w_output: bfloat16 [2048, 2048], P('tensor', 'dp'), may hold values from -0.5 to 0.5
- w_gate: bfloat16 [2048, 5504], P('dp', 'tensor'), may hold values from -0.125 to 0.125
- w_up: bfloat16 [2048, 5504], P('dp', 'tensor'), may hold values from -0.125 to 0.125
- w_down: bfloat16 [5504, 2048], P('tensor', 'dp'), may hold values from -0.078125 to 0.078125
- attn_gain: bfloat16 [2048], P('dp'), may hold values from 0.099609375 to 1.8984375
- ffn_gain: bfloat16 [2048], P('dp'), may hold values from 0.099609375 to 1.8984375
- kv_gain: bfloat16 [2048], P('dp'), may hold values from 0.099609375 to 1.8984375
Outputs:
- layer_out: bfloat16 [8192, 2048], P('dp')
- input_grad: float32 [8192, 2048], P('dp')
- self_grad: float32 [8192, 2048], P('dp')
- grad_query: float32 [2048, 2048], P('dp', 'tensor')
- grad_key: float32 [2048, 2048], P('dp', 'tensor')
- grad_value: float32 [2048, 2048], P('dp', 'tensor')
- grad_output: float32 [2048, 2048], P('tensor', 'dp')
- grad_gate: float32 [2048, 5504], P('dp', 'tensor')
- grad_up: float32 [2048, 5504], P('dp', 'tensor')
- grad_down: float32 [5504, 2048], P('tensor', 'dp')
- grad_attn_gain: float32 [2048], P('dp')
- grad_ffn_gain: float32 [2048], P('dp')
- grad_kv_gain: float32 [2048], P('dp')
Inputs may be any that keep to these rules, and one draw needn't show every extreme that they name: `lengths`: each sequence has 256 to 1024 live tokens; in every draw one sequence is exactly 1024 long.
All inputs are finite; a program needn't handle non-finite values.
Results may differ from a plain program's by a relative error of at most 0.023.
Values may be sent and summed in bfloat16 or wider, within the bound.
No kernel may reach another device: no remote copies, remote signals or barrier semaphores. Data moves between devices by JAX's collectives and lax.ppermute only.
A program may use at most 256 MiB of HBM per device.

v0:
```python
import jax
import jax.numpy as jnp
from jax import lax
from jax.sharding import PartitionSpec as P

HD = 128
QBLOCK = 512


epsilon = 1e-06


def plain_dot(left, right):
    return jnp.dot(left, right, preferred_element_type=jnp.float32)


def first_dims(left, right):
    return lax.dot_general(
        left, right, (((0,), (0,)), ((), ())), preferred_element_type=jnp.float32
    )


def last_dims(left, right):
    return lax.dot_general(
        left, right, (((1,), (1,)), ((), ())), preferred_element_type=jnp.float32
    )


def rms_scale(values, gain):
    inverse = lax.rsqrt(jnp.mean(values * values, axis=-1, keepdims=True) + epsilon)
    return (inverse, values * inverse * gain)


def norm_back(grad, values, inverse, gain):
    scaled = grad * gain
    inner = jnp.mean(scaled * values, axis=-1, keepdims=True)
    return (
        inverse * scaled - values * inverse**3 * inner,
        jnp.sum(grad * values * inverse, axis=0),
    )


def rotary_tables(length, head_size):
    position = jnp.arange(length, dtype=jnp.float32)
    freqs = jnp.exp(
        -jnp.log(10000.0) * jnp.arange(head_size // 2, dtype=jnp.float32) * 2.0 / head_size
    )
    angle = position[:, None] * freqs[None, :]
    return (jnp.cos(angle)[:, None, :], jnp.sin(angle)[:, None, :])


def rotate(values, cosine, sine):
    middle = values.shape[-1] // 2
    front = values[..., :middle]
    behind = values[..., middle:]
    return jnp.concatenate(
        [front * cosine - behind * sine, front * sine + behind * cosine], axis=-1
    )


def block_scores(start, queries, keys_rot, valid):
    length = keys_rot.shape[0]
    rows = lax.dynamic_slice_in_dim(queries, start, QBLOCK, 0)
    scores = jnp.einsum(
        "qhd,khd->hqk", rows, keys_rot, preferred_element_type=jnp.float32
    ) * queries.shape[2] ** (-0.5)
    places = start + jnp.arange(QBLOCK, dtype=jnp.int32)
    allowed = (jnp.arange(length, dtype=jnp.int32)[None, :] <= places[:, None]) & valid[None, :]
    return (rows, jnp.where(allowed[None], scores, -1e30), allowed)


def attend_forward(queries, keys_rot, values_in, valid):
    length, heads, size = queries.shape
    starts = jnp.arange(length // QBLOCK, dtype=jnp.int32) * QBLOCK

    def one_block(start):
        rows, scores, allowed = block_scores(start, queries, keys_rot, valid)
        largest = jnp.max(scores, axis=-1, keepdims=True)
        expo = jnp.exp(scores - largest)
        totals = jnp.sum(expo, axis=-1, keepdims=True)
        probs = (expo / totals).astype(jnp.bfloat16)
        result = jnp.einsum("hqk,khd->qhd", probs, values_in, preferred_element_type=jnp.float32)
        return (result, (largest + jnp.log(totals))[..., 0])

    results, log_sums = lax.map(one_block, starts)
    return (results.reshape(length, heads, size), log_sums)


def attend_backward(queries, keys_rot, values_in, valid, log_sums, grad_attended):
    length, heads, size = queries.shape
    scale = size ** (-0.5)
    starts = jnp.arange(length // QBLOCK, dtype=jnp.int32) * QBLOCK

    def one_block(carry, entry):
        start, block_sums = entry
        rows, scores, allowed = block_scores(start, queries, keys_rot, valid)
        grad_rows = lax.dynamic_slice_in_dim(grad_attended, start, QBLOCK, 0)
        probs = jnp.where(allowed[None], jnp.exp(scores - block_sums[:, :, None]), 0.0)
        grad_probs = jnp.einsum(
            "qhd,khd->hqk", grad_rows, values_in, preferred_element_type=jnp.float32
        )
        inner = jnp.sum(probs * grad_probs, axis=-1, keepdims=True)
        grad_scores = (probs * (grad_probs - inner)).astype(jnp.bfloat16)
        query_grad = (
            jnp.einsum("hqk,khd->qhd", grad_scores, keys_rot, preferred_element_type=jnp.float32)
            * scale
        )
        key_grad = (
            carry[0]
            + jnp.einsum("hqk,qhd->khd", grad_scores, rows, preferred_element_type=jnp.float32)
            * scale
        )
        value_grad = carry[1] + jnp.einsum(
            "hqk,qhd->khd",
            probs.astype(jnp.bfloat16),
            grad_rows,
            preferred_element_type=jnp.float32,
        )
        return ((key_grad, value_grad), query_grad)

    empty = jnp.zeros(keys_rot.shape, jnp.float32)
    (key_grad, value_grad), query_grad = lax.scan(one_block, (empty, empty), (starts, log_sums))
    return (query_grad.reshape(length, heads, size), key_grad, value_grad)


def local(
    hidden_in,
    self_out,
    out_grad,
    lengths,
    w_query,
    w_key,
    w_value,
    w_output,
    w_gate,
    w_up,
    w_down,
    attn_gain,
    ffn_gain,
    kv_gain,
):
    fetched = (
        lax.all_gather(w_query, "dp", axis=0, tiled=True),
        lax.all_gather(w_key, "dp", axis=0, tiled=True),
        lax.all_gather(w_value, "dp", axis=0, tiled=True),
        lax.all_gather(w_output, "dp", axis=1, tiled=True),
        lax.all_gather(w_gate, "dp", axis=0, tiled=True),
        lax.all_gather(w_up, "dp", axis=0, tiled=True),
        lax.all_gather(w_down, "dp", axis=1, tiled=True),
        lax.all_gather(attn_gain, "dp", axis=0, tiled=True),
        lax.all_gather(ffn_gain, "dp", axis=0, tiled=True),
        lax.all_gather(kv_gain, "dp", axis=0, tiled=True),
    )
    hidden = hidden_in.astype(jnp.float32)
    selfout = self_out.astype(jnp.float32)
    length = hidden.shape[0]
    valid = jnp.arange(length, dtype=jnp.int32) < lengths[0]
    heads_here = fetched[0].shape[1] // HD
    x_inverse, x_normed = rms_scale(hidden, fetched[7].astype(jnp.float32))
    normed = x_normed.astype(jnp.bfloat16)
    s_inverse, s_normed = rms_scale(selfout, fetched[9].astype(jnp.float32))
    kv_normed = s_normed.astype(jnp.bfloat16)
    cosine, sine = rotary_tables(length, HD)
    queries = rotate(
        plain_dot(normed, fetched[0]).reshape(length, heads_here, HD), cosine, sine
    ).astype(jnp.bfloat16)
    keys_rot = rotate(
        plain_dot(kv_normed, fetched[1]).reshape(length, heads_here, HD), cosine, sine
    ).astype(jnp.bfloat16)
    values_in = (
        plain_dot(kv_normed, fetched[2]).astype(jnp.bfloat16).reshape(length, heads_here, HD)
    )
    attended, log_sums = attend_forward(queries, keys_rot, values_in, valid)
    attended_low = attended.reshape(length, -1).astype(jnp.bfloat16)
    mid = hidden + lax.psum(plain_dot(attended_low, fetched[3]), "tensor")
    m_inverse, m_normed = rms_scale(mid, fetched[8].astype(jnp.float32))
    ffn_in = m_normed.astype(jnp.bfloat16)
    gate_pre = plain_dot(ffn_in, fetched[4])
    up_pre = plain_dot(ffn_in, fetched[5])
    sigma = jax.nn.sigmoid(gate_pre)
    activated = (gate_pre * sigma * up_pre).astype(jnp.bfloat16)
    layer_out = (
        mid
        + lax.psum(plain_dot(activated, fetched[6]).astype(jnp.bfloat16), "tensor").astype(
            jnp.float32
        )
    ).astype(jnp.bfloat16)
    weights = (
        lax.all_gather(w_query, "dp", axis=0, tiled=True),
        lax.all_gather(w_key, "dp", axis=0, tiled=True),
        lax.all_gather(w_value, "dp", axis=0, tiled=True),
        lax.all_gather(w_output, "dp", axis=1, tiled=True),
        lax.all_gather(w_gate, "dp", axis=0, tiled=True),
        lax.all_gather(w_up, "dp", axis=0, tiled=True),
        lax.all_gather(w_down, "dp", axis=1, tiled=True),
        lax.all_gather(attn_gain, "dp", axis=0, tiled=True),
        lax.all_gather(ffn_gain, "dp", axis=0, tiled=True),
        lax.all_gather(kv_gain, "dp", axis=0, tiled=True),
    )
    attn_scale = weights[7].astype(jnp.float32)
    ffn_scale = weights[8].astype(jnp.float32)
    kv_scale = weights[9].astype(jnp.float32)
    grad_y = out_grad.astype(jnp.float32) * valid[:, None].astype(jnp.float32)
    grad_y_low = grad_y.astype(jnp.bfloat16)
    grad_down = first_dims(activated, grad_y_low)
    grad_act = last_dims(grad_y_low, weights[6])
    grad_gate_pre = (grad_act * up_pre * sigma * (1.0 + gate_pre * (1.0 - sigma))).astype(
        jnp.bfloat16
    )
    grad_up_pre = (grad_act * gate_pre * sigma).astype(jnp.bfloat16)
    grad_gate = first_dims(ffn_in, grad_gate_pre)
    grad_up = first_dims(ffn_in, grad_up_pre)
    grad_ffn_in = lax.psum(
        (last_dims(grad_gate_pre, weights[4]) + last_dims(grad_up_pre, weights[5])).astype(
            jnp.bfloat16
        ),
        "tensor",
    ).astype(jnp.float32)
    mid_part, grad_ffn_gain = norm_back(grad_ffn_in, mid, m_inverse, ffn_scale)
    grad_mid = grad_y + mid_part
    grad_mid_low = grad_mid.astype(jnp.bfloat16)
    grad_output = first_dims(attended_low, grad_mid_low)
    grad_attended = (
        last_dims(grad_mid_low, weights[3]).astype(jnp.bfloat16).reshape(length, heads_here, HD)
    )
    query_grad, key_grad, value_grad = attend_backward(
        queries, keys_rot, values_in, valid, log_sums, grad_attended
    )
    grad_q_pre = rotate(query_grad, cosine, -sine).reshape(length, -1).astype(jnp.bfloat16)
    grad_k_pre = rotate(key_grad, cosine, -sine).reshape(length, -1).astype(jnp.bfloat16)
    grad_v_pre = value_grad.reshape(length, -1).astype(jnp.bfloat16)
    grad_query = first_dims(normed, grad_q_pre)
    grad_key = first_dims(kv_normed, grad_k_pre)
    grad_value = first_dims(kv_normed, grad_v_pre)
    grad_normed, grad_kv_normed = (
        lax.psum(last_dims(grad_q_pre, weights[0]).astype(jnp.bfloat16), "tensor").astype(
            jnp.float32
        ),
        lax.psum(
            (last_dims(grad_k_pre, weights[1]) + last_dims(grad_v_pre, weights[2])).astype(
                jnp.bfloat16
            ),
            "tensor",
        ).astype(jnp.float32),
    )
    x_part, grad_attn_gain = norm_back(grad_normed, hidden, x_inverse, attn_scale)
    s_part, grad_kv_gain = norm_back(grad_kv_normed, selfout, s_inverse, kv_scale)
    input_grad = grad_mid + x_part
    summed = (
        lax.psum_scatter(
            grad_query.astype(jnp.bfloat16), "dp", scatter_dimension=0, tiled=True
        ).astype(jnp.float32),
        lax.psum_scatter(
            grad_key.astype(jnp.bfloat16), "dp", scatter_dimension=0, tiled=True
        ).astype(jnp.float32),
        lax.psum_scatter(
            grad_value.astype(jnp.bfloat16), "dp", scatter_dimension=0, tiled=True
        ).astype(jnp.float32),
        lax.psum_scatter(
            grad_output.astype(jnp.bfloat16), "dp", scatter_dimension=1, tiled=True
        ).astype(jnp.float32),
        lax.psum_scatter(
            grad_gate.astype(jnp.bfloat16), "dp", scatter_dimension=0, tiled=True
        ).astype(jnp.float32),
        lax.psum_scatter(
            grad_up.astype(jnp.bfloat16), "dp", scatter_dimension=0, tiled=True
        ).astype(jnp.float32),
        lax.psum_scatter(
            grad_down.astype(jnp.bfloat16), "dp", scatter_dimension=1, tiled=True
        ).astype(jnp.float32),
        lax.psum_scatter(
            grad_attn_gain.astype(jnp.bfloat16), "dp", scatter_dimension=0, tiled=True
        ).astype(jnp.float32),
        lax.psum_scatter(
            grad_ffn_gain.astype(jnp.bfloat16), "dp", scatter_dimension=0, tiled=True
        ).astype(jnp.float32),
        lax.psum_scatter(
            grad_kv_gain.astype(jnp.bfloat16), "dp", scatter_dimension=0, tiled=True
        ).astype(jnp.float32),
    )
    gain_attn = summed[7]
    gain_ffn = summed[8]
    gain_kv = summed[9]
    return (
        layer_out,
        input_grad,
        s_part,
        summed[0],
        summed[1],
        summed[2],
        summed[3],
        summed[4],
        summed[5],
        summed[6],
        gain_attn,
        gain_ffn,
        gain_kv,
    )


def solution(mesh):
    placed = (
        P("dp", None),
        P("dp", None),
        P("dp", None),
        P("dp"),
        P("dp", "tensor"),
        P("dp", "tensor"),
        P("dp", "tensor"),
        P("tensor", "dp"),
        P("dp", "tensor"),
        P("dp", "tensor"),
        P("tensor", "dp"),
        P("dp"),
        P("dp"),
        P("dp"),
    )
    return jax.shard_map(
        local,
        mesh=mesh,
        in_specs=placed,
        out_specs=(
            P("dp", None),
            P("dp", None),
            P("dp", None),
            P("dp", "tensor"),
            P("dp", "tensor"),
            P("dp", "tensor"),
            P("tensor", "dp"),
            P("dp", "tensor"),
            P("dp", "tensor"),
            P("tensor", "dp"),
            P("dp"),
            P("dp"),
            P("dp"),
        ),
        check_vma=False,
    )
```

profile of v0, /device:TPU:0, one launch (start us, length us, event | category | flops | bytes accessed | tf_op | source)
XLA Modules:
  0.0 1340.2 jit_solution(16218594319938436078)
XLA Ops:
  16.9 13.5 %all-gather.1 = bf16[8,1,256]{2,1,0:T(2,128)(2,1)S(1)} all-gather(bf16[1,1,256]{2,1,0:T(2,128)(2,1)S(1)} %reshape.278), channel_id=1, replica_groups=mesh['dp'=8,'tensor'=4] {'dp'}, dimensions={0}, use_global_device_ids=true | all-gather | bytes 4608 | tf_op jit(solution)/shard_map/all_gather | solution.py:152
  48.4 23.4 %all-gather.11.cloned.1.call-done = bf16[2048,512]{1,0:T(8,128)(2,1)} async-done(((bf16[256,512]{1,0:T(8,128)(2,1)}), bf16[2048,512]{1,0:T(8,128)(2,1)}) %all-gather.11.cloned.1.call-update) | async-done | bytes 2097168 | tf_op jit(solution)/shard_map/all_gather | solution.py:143
  83.8 18.2 %all-gather.13.cloned.1.call-done = bf16[2048,512]{1,0:T(8,128)(2,1)} async-done(((bf16[256,512]{1,0:T(8,128)(2,1)}), bf16[2048,512]{1,0:T(8,128)(2,1)}) %all-gather.13.cloned.1.call-update) | async-done | bytes 2097168 | tf_op jit(solution)/shard_map/all_gather | solution.py:144
  120.8 25.9 %while.28 = (s32[]{:T(128)}, bf16[2,512,4,128]{3,1,2,0:T(8,128)(2,1)}, f32[2,4,512]{2,1,0:T(4,128)S(1)}, s32[2]{0:T(128)S(1)}, bf16[1024,4,128]{2,0,1:T(8,128)(2...) while((s32[]{:T(128)}, ...), condition=%wide.region_5.6_spmd.clone, body=%wide.region_2.5_spmd.clone.sunk | while | flops 1099955712 | bytes 39393520 | solution.py:85
  160.9 10.3 all-gather.2
  171.3 158.6 %all-reduce.9.cloned.1.call-done = f32[1024,2048]{1,0:T(8,128)} async-done(((f32[1024,2048]{1,0:T(8,128)}), f32[1024,2048]{1,0:T(8,128)}) %all-reduce.9.cloned.1.call-update) | async-done | bytes 8388624 | tf_op jit(solution)/shard_map/psum | solution.py:175
  341.8 50.1 %all-gather.21.cloned.1.call-done = bf16[2048,1376]{0,1:T(8,128)(2,1)} async-done(((bf16[256,1376]{0,1:T(8,128)(2,1)}), bf16[2048,1376]{0,1:T(8,128)(2,1)}) %all-gather.21.cloned.1.call-update) | async-done | bytes 5636112 | tf_op jit(solution)/shard_map/all_gather | solution.py:148
  391.9 11.2 fusion.87
  403.1 48.4 %all-gather.19.cloned.1.call-done = bf16[2048,1376]{0,1:T(8,128)(2,1)} async-done(((bf16[256,1376]{0,1:T(8,128)(2,1)}), bf16[2048,1376]{0,1:T(8,128)(2,1)}) %all-gather.19.cloned.1.call-update) | async-done | bytes 5636112 | tf_op jit(solution)/shard_map/all_gather | solution.py:147
  451.6 10.8 fusion.86
  462.4 48.8 %all-gather.23.cloned.1.call-done = bf16[1376,2048]{1,0:T(8,128)(2,1)} async-done(((bf16[1376,256]{1,0:T(8,128)(2,1)}), bf16[1376,2048]{1,0:T(8,128)(2,1)}) %all-gather.23.cloned.1.call-update) | async-done | bytes 5636112 | tf_op jit(solution)/shard_map/all_gather | solution.py:149
  511.2 16.9 %multiply_convert_fusion.2 = (bf16[1024,1376]{0,1:T(8,128)(2,1)S(1)}, bf16[1024,1376]{0,1:T(8,128)(2,1)S(1)}, bf16[1024,1376]{0,1:T(8,128)(2,1)}) fusion(f32[1024,1376]{0,1:T(8,128)} %fusion.86, f32[1024,1376]{0,1:T(8,128)} %fusion.87, bf16[1376,2048]{1,0:T(8,128)(2,1)} %all-gather.23.cloned.1.call-done, bf16[1024,2048]{1,0:T(8,128)(2,1)} %param.20, ...), kind=kOutput, calls=%fused_computation.95 | convolution fusion | flops 5800198144 | bytes 29560832 | tf_op jit(solution)/shard_map/dot_general | solution.py:24
  535.2 11.2 add_convert_fusion.1
  546.5 102.1 %all-reduce.11.cloned.1.call-done = bf16[1024,2048]{1,0:T(8,128)(2,1)} async-done(((bf16[1024,2048]{1,0:T(8,128)(2,1)}), bf16[1024,2048]{1,0:T(8,128)(2,1)}) %all-reduce.11.cloned.1.call-update) | async-done | bytes 4194320 | tf_op jit(solution)/shard_map/psum | solution.py:213
  677.2 38.6 %while.29 = (s32[]{:T(128)}, f32[1024,4,128]{0,2,1:T(8,128)S(1)}, f32[1024,4,128]{0,2,1:T(8,128)}, f32[2,512,4,128]{3,1,0,2:T(8,128)}, s32[2]{0:T(128)S(1)}, /*i...) while((s32[]{:T(128)}, f32[1024,4,128]{0,2,1:T(8,128)S(1)}, ...), condition=%wide.region_13.14_spmd.clone, body=%wide.region_11.13_spmd.clone.sunk | while | flops 2709257728 | bytes 124828080 | solution.py:122
  749.3 10.3 convolution_convert_fusion
  770.6 10.5 convolution_convert_fusion.2
  781.2 11.4 convolution_convert_fusion.4
  811.3 23.1 %reduce-scatter.10.cloned.1.call-done = bf16[256,512]{1,0:T(8,128)(2,1)} async-done(((bf16[2048,512]{1,0:T(8,128)(2,1)}), bf16[256,512]{1,0:T(8,128)(2,1)}) %reduce-scatter.10.cloned.1.call-update) | async-done | bytes 262160 | tf_op jit(solution)/shard_map/reduce_scatter | solution.py:253
  836.2 62.7 %reduce-scatter.18.cloned.1.call-done = bf16[256,1376]{0,1:T(8,128)(2,1)} async-done(((bf16[2048,1376]{0,1:T(8,128)(2,1)}), bf16[256,1376]{0,1:T(8,128)(2,1)}) %reduce-scatter.18.cloned.1.call-update) | async-done | bytes 704528 | tf_op jit(solution)/shard_map/reduce_scatter | solution.py:265
  901.2 62.0 %reduce-scatter.16.cloned.1.call-done = bf16[256,1376]{0,1:T(8,128)(2,1)} async-done(((bf16[2048,1376]{0,1:T(8,128)(2,1)}), bf16[256,1376]{0,1:T(8,128)(2,1)}) %reduce-scatter.16.cloned.1.call-update) | async-done | bytes 704528 | tf_op jit(solution)/shard_map/reduce_scatter | solution.py:262
  965.5 61.9 %reduce-scatter.20.cloned.1.call-done = bf16[1376,256]{1,0:T(8,128)(2,1)} async-done(((bf16[1376,2048]{1,0:T(8,128)(2,1)}), bf16[1376,256]{1,0:T(8,128)(2,1)}) %reduce-scatter.20.cloned.1.call-update) | async-done | bytes 704528 | tf_op jit(solution)/shard_map/reduce_scatter | solution.py:268
  1029.7 241.8 %all-reduce.13.cloned.1.call-done = (bf16[1024,2048]{1,0:T(8,128)(2,1)}, bf16[1024,2048]{1,0:T(8,128)(2,1)}, bf16[1024,2048]{1,0:T(8,128)(2,1)}) async-done(((bf16[1024,2048]{1,0:T(8,128)(2,1)}, bf16[1024,2048]{1,0:T(8,128)(2,1)}, bf16[1024,2048]{1,0:T(8,128)(2,1)}), (bf16[1024,2048]{1,0:T(8,128)(2,1)}, bf16[1024,2048]{1,0:T(8,128)(2,1)}, bf16[1024,2048]{1,0:T(8,128)(2,1)})) %all-reduce.13.cloned.1.call-update) | async-done | bytes 12582928 | tf_op jit(solution)/shard_map/psum | solution.py:184
  1287.1 28.5 %all-reduce.3 = (bf16[2048]{0:T(1024)(128)(2,1)S(1)}, bf16[2048]{0:T(1024)(128)(2,1)S(1)}, bf16[2048]{0:T(1024)(128)(2,1)S(1)}) all-reduce(bf16[2048]{0:T(1024)(128)(2,1)S(1)} %get-tuple-element.258, bf16[2048]{0:T(1024)(128)(2,1)S(1)} %copy-done.38, ...), channel_id=9, replica_groups=mesh['dp'=8,'tensor'=4] {'dp'}, use_global_device_ids=true, to_apply=%region_26.27.clone | all-reduce | flops 6144 | bytes 24576
  (270 shorter events, 279.0 us)
Async XLA Ops:
  7.2 35.2 %all-gather.15.cloned.1.call-start = ((), (), s32[]{:S(2)}) async-start(), calls=%async_computation.9 | async-start | bytes 2359296 | tf_op jit(solution)/shard_map/all_gather | solution.py:145
  7.9 63.9 %all-gather.11.cloned.1.call-start = ((), (), s32[]{:S(2)}) async-start(), calls=%async_computation.7 | async-start | bytes 2359296 | tf_op jit(solution)/shard_map/all_gather | solution.py:143
  8.7 93.4 %all-gather.13.cloned.1.call-start = ((), (), s32[]{:S(2)}) async-start(), calls=%async_computation.8 | async-start | bytes 2359296 | tf_op jit(solution)/shard_map/all_gather | solution.py:144
  9.4 141.0 %all-gather.17.cloned.1.call-start = ((), (), s32[]{:S(2)}) async-start(), calls=%async_computation.10 | async-start | bytes 2359296 | tf_op jit(solution)/shard_map/all_gather | solution.py:146
  10.0 319.9 %all-reduce.9.cloned.1.call-start = ((), (), s32[]{:S(2)}) async-start(), calls=%async_computation.11 | async-start | bytes 16777216 | tf_op jit(solution)/shard_map/psum | solution.py:175
  16.3 85.7 %copy-start.35 = (f32[1024]{0:T(1024)}, f32[1024]{0:T(1024)S(1)}, u32[]{:S(2)}) copy-start(f32[1024]{0:T(1024)S(1)} %get-tuple-element.330) | copy-start | bytes 12292
  16.9 54.9 %copy-start.33 = (f32[1024]{0:T(1024)}, f32[1024]{0:T(1024)S(1)}, u32[]{:S(2)}) copy-start(f32[1024]{0:T(1024)S(1)} %get-tuple-element.332) | copy-start | bytes 12292
  30.5 71.6 %copy-start.29 = (f32[8,1,256]{2,1,0:T(1,128)}, f32[8,1,256]{2,1,0:T(1,128)S(1)}, u32[]{:S(2)}) copy-start(f32[8,1,256]{2,1,0:T(1,128)S(1)} %convert_element_type.230) | copy-start | bytes 24580
  158.1 233.8 %all-gather.21.cloned.1.call-start = ((), (), s32[]{:S(2)}) async-start(), calls=%async_computation.13 | async-start | bytes 6340608 | tf_op jit(solution)/shard_map/all_gather | solution.py:148
  158.7 292.9 %all-gather.19.cloned.1.call-start = ((), (), s32[]{:S(2)}) async-start(), calls=%async_computation.12 | async-start | bytes 6340608 | tf_op jit(solution)/shard_map/all_gather | solution.py:147
  159.4 351.8 %all-gather.23.cloned.1.call-start = ((), (), s32[]{:S(2)}) async-start(), calls=%async_computation.14 | async-start | bytes 6340608 | tf_op jit(solution)/shard_map/all_gather | solution.py:149
  160.2 488.4 %all-reduce.11.cloned.1.call-start = ((), (), s32[]{:S(2)}) async-start(), calls=%async_computation.15 | async-start | bytes 8388608 | tf_op jit(solution)/shard_map/psum | solution.py:213
  171.3 485.2 %copy-start.39 = (f32[1024]{0:T(1024)}, f32[1024]{0:T(1024)S(1)}, u32[]{:S(2)}) copy-start(f32[1024]{0:T(1024)S(1)} %fusion.78) | copy-start | bytes 12292
  546.4 259.5 %reduce-scatter.14.cloned.1.call-start = ((), (), s32[]{:S(2)}) async-start(), calls=%async_computation.19 | async-start | bytes 2359296 | tf_op jit(solution)/shard_map/reduce_scatter | solution.py:259
  669.9 137.8 %reduce-scatter.12.cloned.1.call-start = ((), (), s32[]{:S(2)}) async-start(), calls=%async_computation.18 | async-start | bytes 2359296 | tf_op jit(solution)/shard_map/reduce_scatter | solution.py:256
  677.2 41.3 %copy-start.30 = (f32[8,1,256]{2,1,0:T(1,128)S(1)}, f32[8,1,256]{2,1,0:T(1,128)}, u32[]{:S(2)}) copy-start(f32[8,1,256]{2,1,0:T(1,128)} %copy-done.29) | copy-start | bytes 24580
  677.2 41.3 %copy-start.36 = (f32[1024]{0:T(1024)S(1)}, f32[1024]{0:T(1024)}, u32[]{:S(2)}) copy-start(f32[1024]{0:T(1024)} %copy-done.35) | copy-start | bytes 12292
  724.9 84.6 %reduce-scatter.8.cloned.1.call-start = ((), (), s32[]{:S(2)}) async-start(), calls=%async_computation.16 | async-start | bytes 2359296 | tf_op jit(solution)/shard_map/reduce_scatter | solution.py:250
  741.4 92.9 %reduce-scatter.10.cloned.1.call-start = ((), (), s32[]{:S(2)}) async-start(), calls=%async_computation.17 | async-start | bytes 2359296 | tf_op jit(solution)/shard_map/reduce_scatter | solution.py:253
  749.2 149.7 %reduce-scatter.18.cloned.1.call-start = ((), (), s32[]{:S(2)}) async-start(), calls=%async_computation.21 | async-start | bytes 6340608 | tf_op jit(solution)/shard_map/reduce_scatter | solution.py:265
  759.6 203.6 %reduce-scatter.16.cloned.1.call-start = ((), (), s32[]{:S(2)}) async-start(), calls=%async_computation.20 | async-start | bytes 6340608 | tf_op jit(solution)/shard_map/reduce_scatter | solution.py:262
  769.9 257.4 %reduce-scatter.20.cloned.1.call-start = ((), (), s32[]{:S(2)}) async-start(), calls=%async_computation.22 | async-start | bytes 6340608 | tf_op jit(solution)/shard_map/reduce_scatter | solution.py:268
  781.1 490.4 %all-reduce.13.cloned.1.call-start = ((), (), s32[]{:S(2)}) async-start(), calls=%async_computation.23 | async-start | bytes 25165824 | tf_op jit(solution)/shard_map/psum | solution.py:184
  1283.5 34.1 %copy-start.37 = (f32[1024]{0:T(1024)S(1)}, f32[1024]{0:T(1024)}, u32[]{:S(2)}) copy-start(f32[1024]{0:T(1024)} %get-tuple-element.331) | copy-start | bytes 12292
  (52 other events, 270.5 us)
Sparse Core Ops, SparseCore 0:
  9.6 31.8 all-gather.14
  43.2 28.5 all-gather.10
  73.4 28.5 all-gather.12
  103.5 30.3 all-gather.16
  158.2 171.6 all-reduce.8
  331.4 60.4 all-gather.20
  393.6 57.9 all-gather.18
  453.2 57.9 all-gather.22
  546.5 102.0 all-reduce.10
  670.0 35.7 reduce-scatter.13
  725.0 35.8 reduce-scatter.11
  763.1 34.4 reduce-scatter.7
  799.9 34.3 reduce-scatter.9
  836.5 62.3 reduce-scatter.17
  901.2 61.9 reduce-scatter.15
  965.4 61.9 reduce-scatter.19
  1032.2 239.2 all-reduce.12
where the time goes:
time: 1340 us
  waiting for transfers between devices  906 us (68%)
  matrix products  196 us (15%)
  other arithmetic  104 us (8%)
  blocking collectives  61.2 us (5%)
  local copies, waits for them, and re-layouts  46.5 us (3%)
  between operations  16 us (1%)
    psum x1, waiting for transfers between devices, local(): lax.psum(plain_dot(activated, fetched[6]).astype(jnp.bfloat16), 'tensor')  242 us
    psum x1, waiting for transfers between devices, local(): mid = hidden + lax.psum(plain_dot(attended_low, fetched[3]), 'tensor')  159 us
    psum x1, waiting for transfers between devices, local(): lax.psum((last_dims(grad_gate_pre, weights[4]) + last_dims(grad_up_pre, w...  102 us
    reduce_scatter x1, waiting for transfers between devices, local(): lax.psum_scatter(grad_up.astype(jnp.bfloat16), 'dp', scatter_dimension=0,...  62.7 us
    reduce_scatter x1, waiting for transfers between devices, local(): lax.psum_scatter(grad_gate.astype(jnp.bfloat16), 'dp', scatter_dimension=...  62 us
    reduce_scatter x1, waiting for transfers between devices, local(): lax.psum_scatter(grad_down.astype(jnp.bfloat16), 'dp', scatter_dimension=...  61.9 us
    dot_general x7, matrix products, plain_dot(): return jnp.dot(left, right, preferred_element_type=jnp.float32)  57.1 us
    dot_general x7, matrix products, first_dims(): lax.dot_general(left, right, (((0,), (0,)), ((), ())), preferred_element_...  54.4 us
  transfers between devices with their start and end apart: 17, of which 12 were waited for; matrix products, arithmetic and copies ran while one was open for 18% of the time, Pallas kernels for 0%

commit v1 on v0

v1 whole, which is shorter than its diff:
```python
import jax
import jax.numpy as jnp
from jax import lax
from jax.sharding import PartitionSpec as P

HD = 128
QBLOCK = 512
BF = jnp.bfloat16
F32 = jnp.float32


epsilon = 1e-06


def plain_dot(left, right):
    return jnp.dot(left, right, preferred_element_type=jnp.float32)


def first_dims(left, right):
    return lax.dot_general(
        left, right, (((0,), (0,)), ((), ())), preferred_element_type=jnp.float32
    )


def last_dims(left, right):
    return lax.dot_general(
        left, right, (((1,), (1,)), ((), ())), preferred_element_type=jnp.float32
    )


def rms_scale(values, gain):
    inverse = lax.rsqrt(jnp.mean(values * values, axis=-1, keepdims=True) + epsilon)
    return (inverse, values * inverse * gain)


def norm_back(grad, values, inverse, gain):
    scaled = grad * gain
    inner = jnp.mean(scaled * values, axis=-1, keepdims=True)
    return (
        inverse * scaled - values * inverse**3 * inner,
        jnp.sum(grad * values * inverse, axis=0),
    )


def rotary_tables(length, head_size):
    position = jnp.arange(length, dtype=jnp.float32)
    freqs = jnp.exp(
        -jnp.log(10000.0) * jnp.arange(head_size // 2, dtype=jnp.float32) * 2.0 / head_size
    )
    angle = position[:, None] * freqs[None, :]
    return (jnp.cos(angle)[:, None, :], jnp.sin(angle)[:, None, :])


def rotate(values, cosine, sine):
    middle = values.shape[-1] // 2
    front = values[..., :middle]
    behind = values[..., middle:]
    return jnp.concatenate(
        [front * cosine - behind * sine, front * sine + behind * cosine], axis=-1
    )


def block_scores(start, queries, keys_rot, valid):
    length = keys_rot.shape[0]
    rows = lax.dynamic_slice_in_dim(queries, start, QBLOCK, 0)
    scores = jnp.einsum(
        "qhd,khd->hqk", rows, keys_rot, preferred_element_type=jnp.float32
    ) * queries.shape[2] ** (-0.5)
    places = start + jnp.arange(QBLOCK, dtype=jnp.int32)
    allowed = (jnp.arange(length, dtype=jnp.int32)[None, :] <= places[:, None]) & valid[None, :]
    return (rows, jnp.where(allowed[None], scores, -1e30), allowed)


def attend_forward(queries, keys_rot, values_in, valid):
    length, heads, size = queries.shape
    starts = jnp.arange(length // QBLOCK, dtype=jnp.int32) * QBLOCK

    def one_block(start):
        rows, scores, allowed = block_scores(start, queries, keys_rot, valid)
        largest = jnp.max(scores, axis=-1, keepdims=True)
        expo = jnp.exp(scores - largest)
        totals = jnp.sum(expo, axis=-1, keepdims=True)
        probs = (expo / totals).astype(jnp.bfloat16)
        result = jnp.einsum("hqk,khd->qhd", probs, values_in, preferred_element_type=jnp.float32)
        return (result, (largest + jnp.log(totals))[..., 0])

    results, log_sums = lax.map(one_block, starts)
    return (results.reshape(length, heads, size), log_sums)


def attend_backward(queries, keys_rot, values_in, valid, log_sums, grad_attended):
    length, heads, size = queries.shape
    scale = size ** (-0.5)
    starts = jnp.arange(length // QBLOCK, dtype=jnp.int32) * QBLOCK

    def one_block(carry, entry):
        start, block_sums = entry
        rows, scores, allowed = block_scores(start, queries, keys_rot, valid)
        grad_rows = lax.dynamic_slice_in_dim(grad_attended, start, QBLOCK, 0)
        probs = jnp.where(allowed[None], jnp.exp(scores - block_sums[:, :, None]), 0.0)
        grad_probs = jnp.einsum(
            "qhd,khd->hqk", grad_rows, values_in, preferred_element_type=jnp.float32
        )
        inner = jnp.sum(probs * grad_probs, axis=-1, keepdims=True)
        grad_scores = (probs * (grad_probs - inner)).astype(jnp.bfloat16)
        query_grad = (
            jnp.einsum("hqk,khd->qhd", grad_scores, keys_rot, preferred_element_type=jnp.float32)
            * scale
        )
        key_grad = (
            carry[0]
            + jnp.einsum("hqk,qhd->khd", grad_scores, rows, preferred_element_type=jnp.float32)
            * scale
        )
        value_grad = carry[1] + jnp.einsum(
            "hqk,qhd->khd",
            probs.astype(jnp.bfloat16),
            grad_rows,
            preferred_element_type=jnp.float32,
        )
        return ((key_grad, value_grad), query_grad)

    empty = jnp.zeros(keys_rot.shape, jnp.float32)
    (key_grad, value_grad), query_grad = lax.scan(one_block, (empty, empty), (starts, log_sums))
    return (query_grad.reshape(length, heads, size), key_grad, value_grad)


def swap(array, bit, size):
    return lax.ppermute(array, "tensor", [(t, t ^ bit) for t in range(size)])


def bit_orders(size):
    bits = [1 << step for step in range(size.bit_length() - 1)]
    return (bits, bits[1:] + bits[:1])


def relative(array, me, size):
    part = array.shape[0] // size
    return jnp.stack(
        [lax.dynamic_slice_in_dim(array, (me ^ step) * part, part, 0) for step in range(size)]
    )


def absolute(blocks, me):
    parts = [
        lax.dynamic_index_in_dim(blocks, me ^ step, 0, keepdims=False)
        for step in range(blocks.shape[0])
    ]
    return jnp.concatenate(parts, axis=0)


def scatter_sum(blocks):
    size = blocks.shape[0]
    half = blocks.shape[2] // 2
    sums = []
    for group, order in enumerate(bit_orders(size)):
        held = {
            place: blocks[place, :, group * half : (group + 1) * half].astype(F32)
            for place in range(size)
        }
        for bit in order:
            sent = [place for place in held if place & bit]
            got = swap(jnp.stack([held[place].astype(BF) for place in sent]), bit, size)
            held = {
                place ^ bit: held[place ^ bit] + got[at].astype(F32)
                for at, place in enumerate(sent)
            }
        sums.append(held[0])
    return jnp.concatenate(sums, axis=1)


def gather_rows(own, size):
    half = own.shape[1] // 2
    parts = []
    for group, order in enumerate(bit_orders(size)):
        held = {0: own[:, group * half : (group + 1) * half]}
        for bit in order[::-1]:
            places = list(held)
            got = swap(jnp.stack([held[place] for place in places]), bit, size)
            for at, place in enumerate(places):
                held[place ^ bit] = got[at]
        parts.append(held)
    return jnp.stack(
        [jnp.concatenate([held[place] for held in parts], axis=1) for place in range(size)]
    )


def local(
    hidden_in,
    self_out,
    out_grad,
    lengths,
    w_query,
    w_key,
    w_value,
    w_output,
    w_gate,
    w_up,
    w_down,
    attn_gain,
    ffn_gain,
    kv_gain,
):
    me = lax.axis_index("tensor")
    size = lax.axis_size("tensor")
    dp_size = lax.axis_size("dp")
    gains = lax.all_gather(jnp.stack([attn_gain, ffn_gain, kv_gain]), "dp", axis=1, tiled=True)
    gains = gains.astype(F32)
    attn_scale, ffn_scale, kv_scale = gains[0], gains[1], gains[2]
    wide = w_query.shape[1]
    qkv = lax.all_gather(
        jnp.concatenate([w_query, w_key, w_value], axis=1), "dp", axis=0, tiled=True
    )
    f_query, f_key, f_value = qkv[:, :wide], qkv[:, wide : 2 * wide], qkv[:, 2 * wide :]
    f_output = lax.all_gather(w_output, "dp", axis=1, tiled=True)
    f_gate = lax.all_gather(w_gate, "dp", axis=0, tiled=True)
    f_up = lax.all_gather(w_up, "dp", axis=0, tiled=True)
    f_down = lax.all_gather(w_down, "dp", axis=1, tiled=True)

    hidden = hidden_in.astype(F32)
    selfout = self_out.astype(F32)
    length, width = hidden.shape
    quarter = length // size
    valid = jnp.arange(length, dtype=jnp.int32) < lengths[0]
    heads_here = wide // HD
    x_inverse, x_normed = rms_scale(hidden, attn_scale)
    normed = x_normed.astype(BF)
    s_inverse, s_normed = rms_scale(selfout, kv_scale)
    kv_normed = s_normed.astype(BF)
    cosine, sine = rotary_tables(length, HD)
    queries = rotate(
        plain_dot(normed, f_query).reshape(length, heads_here, HD), cosine, sine
    ).astype(BF)
    keys_rot = rotate(
        plain_dot(kv_normed, f_key).reshape(length, heads_here, HD), cosine, sine
    ).astype(BF)
    values_in = plain_dot(kv_normed, f_value).astype(BF).reshape(length, heads_here, HD)
    attended, log_sums = attend_forward(queries, keys_rot, values_in, valid)
    attended_low = relative(attended.reshape(length, -1).astype(BF), me, size).reshape(length, -1)

    def own_rows(array):
        return lax.dynamic_slice_in_dim(array, me * quarter, quarter, 0)

    hidden_own = own_rows(hidden_in).astype(F32)
    self_own = own_rows(self_out).astype(F32)
    mid_sum = scatter_sum(plain_dot(attended_low, f_output).reshape(size, quarter, width))
    mid = hidden_own + mid_sum
    m_inverse, m_normed = rms_scale(mid, ffn_scale)
    ffn_in = gather_rows(m_normed.astype(BF), size).reshape(length, width)

    grad_y_low = relative(jnp.where(valid[:, None], out_grad, jnp.zeros((), BF)), me, size)
    grad_y = grad_y_low[0].astype(F32)
    grad_y_low = grad_y_low.reshape(length, width)

    gate_pre = plain_dot(ffn_in, f_gate)
    up_pre = plain_dot(ffn_in, f_up)
    sigma = jax.nn.sigmoid(gate_pre)
    activated = (gate_pre * sigma * up_pre).astype(BF)
    grad_down = first_dims(activated, grad_y_low)
    sum_down = lax.psum_scatter(grad_down.astype(BF), "dp", scatter_dimension=1, tiled=True)
    grad_act = last_dims(grad_y_low, f_down)
    grad_gate_pre = (grad_act * up_pre * sigma * (1.0 + gate_pre * (1.0 - sigma))).astype(BF)
    grad_up_pre = (grad_act * gate_pre * sigma).astype(BF)
    back_sum = scatter_sum(
        (last_dims(grad_gate_pre, f_gate) + last_dims(grad_up_pre, f_up)).reshape(
            size, quarter, width
        )
    )
    grad_gate = first_dims(ffn_in, grad_gate_pre)
    sum_gate = lax.psum_scatter(grad_gate.astype(BF), "dp", scatter_dimension=0, tiled=True)
    grad_up = first_dims(ffn_in, grad_up_pre)
    sum_up = lax.psum_scatter(grad_up.astype(BF), "dp", scatter_dimension=0, tiled=True)

    mid_part, grad_ffn_gain = norm_back(back_sum, mid, m_inverse, ffn_scale)
    grad_mid = grad_y + mid_part
    grad_mid_low = gather_rows(grad_mid.astype(BF), size).reshape(length, width)

    out_sum = scatter_sum(plain_dot(activated, f_down).reshape(size, quarter, width))
    layer_out = absolute(gather_rows((mid + out_sum).astype(BF), size), me)

    grad_output = first_dims(attended_low, grad_mid_low)
    sum_output = lax.psum_scatter(grad_output.astype(BF), "dp", scatter_dimension=1, tiled=True)
    grad_attended = absolute(
        last_dims(grad_mid_low, f_output).astype(BF).reshape(size, quarter, -1), me
    ).reshape(length, heads_here, HD)
    query_grad, key_grad, value_grad = attend_backward(
        queries, keys_rot, values_in, valid, log_sums, grad_attended
    )
    grad_q_pre = rotate(query_grad, cosine, -sine).reshape(length, -1).astype(BF)
    grad_k_pre = rotate(key_grad, cosine, -sine).reshape(length, -1).astype(BF)
    grad_v_pre = value_grad.reshape(length, -1).astype(BF)
    rel_q = relative(grad_q_pre, me, size).reshape(length, -1)
    rel_k = relative(grad_k_pre, me, size).reshape(length, -1)
    rel_v = relative(grad_v_pre, me, size).reshape(length, -1)
    grad_normed = scatter_sum(last_dims(rel_q, f_query).reshape(size, quarter, width))
    grad_kv_normed = scatter_sum(
        (last_dims(rel_k, f_key) + last_dims(rel_v, f_value)).reshape(size, quarter, width)
    )
    grad_qkv = jnp.concatenate(
        [
            first_dims(normed, grad_q_pre).astype(BF),
            first_dims(kv_normed, grad_k_pre).astype(BF),
            first_dims(kv_normed, grad_v_pre).astype(BF),
        ],
        axis=1,
    )
    sum_qkv = lax.psum_scatter(grad_qkv, "dp", scatter_dimension=0, tiled=True).astype(F32)
    x_part, grad_attn_gain = norm_back(grad_normed, hidden_own, own_rows(x_inverse), attn_scale)
    s_part, grad_kv_gain = norm_back(grad_kv_normed, self_own, own_rows(s_inverse), kv_scale)
    input_grad = absolute(gather_rows((grad_mid + x_part).astype(BF), size), me).astype(F32)
    self_grad = absolute(gather_rows(s_part.astype(BF), size), me).astype(F32)

    gain_grads = jnp.stack([grad_attn_gain, grad_ffn_gain, grad_kv_gain])
    for bit in bit_orders(size)[0]:
        gain_grads = gain_grads + swap(gain_grads, bit, size)
    place = lax.axis_index("dp")
    piece = width // dp_size

    def gain_piece(step):
        return lax.dynamic_slice_in_dim(gain_grads, ((place + step) % dp_size) * piece, piece, 1)

    total = gain_piece(0)
    for step in range(1, dp_size):
        total = total + lax.ppermute(
            gain_piece(step), "dp", [(i, (i + step) % dp_size) for i in range(dp_size)]
        )
    return (
        layer_out,
        input_grad,
        self_grad,
        sum_qkv[:, :wide],
        sum_qkv[:, wide : 2 * wide],
        sum_qkv[:, 2 * wide :],
        sum_output.astype(F32),
        sum_gate.astype(F32),
        sum_up.astype(F32),
        sum_down.astype(F32),
        total[0],
        total[1],
        total[2],
    )


def solution(mesh):
    placed = (
        P("dp", None),
        P("dp", None),
        P("dp", None),
        P("dp"),
        P("dp", "tensor"),
        P("dp", "tensor"),
        P("dp", "tensor"),
        P("tensor", "dp"),
        P("dp", "tensor"),
        P("dp", "tensor"),
        P("tensor", "dp"),
        P("dp"),
        P("dp"),
        P("dp"),
    )
    return jax.shard_map(
        local,
        mesh=mesh,
        in_specs=placed,
        out_specs=(
            P("dp", None),
            P("dp", None),
            P("dp", None),
            P("dp", "tensor"),
            P("dp", "tensor"),
            P("dp", "tensor"),
            P("tensor", "dp"),
            P("dp", "tensor"),
            P("dp", "tensor"),
            P("tensor", "dp"),
            P("dp"),
            P("dp"),
            P("dp"),
        ),
        check_vma=False,
    )
```

time: 1340 us -> 832 us (0.62)
  waiting for transfers between devices: 906 us -> 334 us
  starting transfers between devices: 0.68 us -> 55 us
  blocking collectives: 61.2 us -> 14.5 us
  local copies, waits for them, and re-layouts: 46.5 us -> 78.6 us
  other arithmetic: 104 us -> 128 us
    psum x3 -> x0, waiting for transfers between devices: 503 us -> none  [the longest x1 242 us: local(): lax.psum(plain_dot(activated, fetched[6]).astype(jnp.bfloat16), 'tensor')]
    ppermute x0 -> x49, waiting for transfers between devices: none -> 261 us  [the longest x42 260 us: swap(): return lax.ppermute(array, 'tensor', [(t, t ^ bit) for t in range(size)])]
    reduce_scatter x7 -> x5, waiting for transfers between devices: 210 us -> 0.01 us  [the longest x1 0.01 us: local(): lax.psum_scatter(grad_output.astype(BF), 'dp', scatter_dimension=1, tiled...]
    all_gather x7 -> x5, waiting for transfers between devices: 189 us -> 70.5 us  [the longest x1 42.2 us: local(): lax.all_gather(jnp.concatenate([w_query, w_key, w_value], axis=1), 'dp',...]
    ppermute x0 -> x49, starting transfers between devices: none -> 54.6 us  [the longest x42 48.3 us: swap(): return lax.ppermute(array, 'tensor', [(t, t ^ bit) for t in range(size)])]
    unnamed x1 -> x0, blocking collectives: 28.5 us -> none
    another operation x4 -> x48, other arithmetic: 10.2 us -> 35.7 us
    concatenate x0 -> x4, other arithmetic: none -> 18.5 us  [the longest x1 11.6 us: local(): jnp.concatenate([first_dims(normed, grad_q_pre).astype(BF), first_dims(kv...]
  transfers between devices with their start and end apart: 17 -> 59, of which waited for: 12 -> 28; matrix products, arithmetic and copies ran while one was open for 18% -> 41% of each run, Pallas kernels for 0% -> 0%
where the time goes in v1:
time: 832 us; the launch traced here: 828 us
  waiting for transfers between devices  334 us (40%)
  matrix products  193 us (23%)
  other arithmetic  128 us (15%)
  local copies, waits for them, and re-layouts  78.6 us (9%)
  starting transfers between devices  55 us (7%)
  between operations  17.2 us (2%)
  blocking collectives  14.5 us (2%)
    ppermute x42, waiting for transfers between devices, swap(): return lax.ppermute(array, 'tensor', [(t, t ^ bit) for t in range(size)])  260 us
    dot_general x7, matrix products, plain_dot(): return jnp.dot(left, right, preferred_element_type=jnp.float32)  57.7 us
    ppermute x42, starting transfers between devices, swap(): return lax.ppermute(array, 'tensor', [(t, t ^ bit) for t in range(size)])  48.3 us
    dot_general x7, matrix products, last_dims(): lax.dot_general(left, right, (((1,), (1,)), ((), ())), preferred_element_...  46.4 us
    all_gather x1, waiting for transfers between devices, local(): lax.all_gather(jnp.concatenate([w_query, w_key, w_value], axis=1), 'dp',...  42.2 us
    dot_general x7, matrix products, first_dims(): lax.dot_general(left, right, (((0,), (0,)), ((), ())), preferred_element_...  42.2 us
    unnamed x151, local copies, waits for them, and re-layouts  35.8 us
    all_gather x1, waiting for transfers between devices, local(): f_gate = lax.all_gather(w_gate, 'dp', axis=0, tiled=True)  28.3 us
  transfers between devices with their start and end apart: 59, of which 28 were waited for; matrix products, arithmetic and copies ran while one was open for 41% of the time, Pallas kernels for 0%

profile of v1, /device:TPU:0, one launch (start us, length us, event | category | flops | bytes accessed | tf_op | source)
XLA Modules:
  0.0 828.1 jit_solution(16205445262796048960)
XLA Ops:
  13.8 14.5 %all_gather.18 = bf16[3,2048]{1,0:T(4,128)(2,1)S(1)} all-gather(bf16[3,256]{1,0:T(4,128)(2,1)S(1)} %pad_maximum_fusion.38), channel_id=1, replica_groups=mesh['dp'=8,'tensor'=4] {'dp'}, dimensions={1}, use_global_device_ids=true | all-gather | bytes 13824 | tf_op jit(solution)/shard_map/all_gather | solution.py:207
  35.6 42.2 %all-gather.6.cloned.1.call-done = bf16[2048,1536]{1,0:T(8,128)(2,1)} async-done(((bf16[256,1536]{1,0:T(8,128)(2,1)}), bf16[2048,1536]{1,0:T(8,128)(2,1)}) %all-gather.6.cloned.1.call-update) | async-done | bytes 6291472 | tf_op jit(solution)/shard_map/all_gather | solution.py:211
  117.5 24.3 %while.28 = (s32[]{:T(128)}, bf16[2,512,4,128]{3,1,2,0:T(8,128)(2,1)}, f32[2,4,512]{2,1,0:T(4,128)S(1)}, s32[2]{0:T(128)S(1)}, bf16[1024,4,128]{2,0,1:T(8,128)(2...) while((s32[]{:T(128)}, ...), condition=%wide.region_5.6_spmd.clone, body=%wide.region_2.5_spmd.clone.sunk | while | flops 1099955712 | bytes 31005356 | solution.py:87
  153.4 22.3 %collective-permute-done = bf16[2,256,1024]{2,1,0:T(8,128)(2,1)S(1)} collective-permute-done((bf16[2,256,1024]{2,1,0:T(8,128)(2,1)S(1)}, bf16[2,256,1024]{2,1,0:T(8,128)(2,1)S(1)}, u32[]{:S(2)}, u32[]{:S(2)}) %collective-permute-start) | collective-permute-done | bytes 1048608 | tf_op jit(solution)/shard_map/ppermute | solution.py:129
  179.0 11.3 %collective-permute-done.1 = bf16[1,256,1024]{2,1,0:T(8,128)(2,1)} collective-permute-done((bf16[1,256,1024]{2,1,0:T(8,128)(2,1)}, bf16[1,256,1024]{2,1,0:T(8,128)(2,1)}, u32[]{:S(2)}, u32[]{:S(2)}) %collective-permute-start.1) | collective-permute-done | bytes 524320 | tf_op jit(solution)/shard_map/ppermute | solution.py:129
  194.2 10.6 %collective-permute-done.3 = bf16[1,256,1024]{2,1,0:T(8,128)(2,1)S(1)} collective-permute-done((bf16[1,256,1024]{2,1,0:T(8,128)(2,1)S(1)}, bf16[1,256,1024]{2,1,0:T(8,128)(2,1)S(1)}, u32[]{:S(2)}, u32[]{:S(2)}) %collective-permute-start.3) | collective-permute-done | bytes 524320 | tf_op jit(solution)/shard_map/ppermute | solution.py:129
  224.7 10.8 %fusion.140 = f32[1024,1376]{0,1:T(8,128)} fusion(bf16[1024,2048]{1,0:T(8,128)(2,1)} %bitcast.346, bf16[1376,2048]{1,0:T(8,128)(2,1)} %all-gather.14.cloned.1.call-done), kind=kOutput, calls=%fused_computation.347 | convolution fusion | flops 5771362304 | bytes 15466496 | tf_op jit(solution)/shard_map/dot_general | solution.py:26
  249.0 10.9 %fusion.138 = f32[1024,1376]{0,1:T(8,128)} fusion(bf16[1024,2048]{1,0:T(8,128)(2,1)} %bitcast.348, bf16[2048,1376]{0,1:T(8,128)(2,1)} %all-gather.12.cloned.1.call-done), kind=kOutput, calls=%fused_computation.345 | convolution fusion | flops 5771362304 | bytes 15466496 | tf_op jit(solution)/shard_map/dot_general | solution.py:16
  259.9 28.3 %all-gather.10.cloned.1.call-done = bf16[2048,1376]{0,1:T(8,128)(2,1)} async-done(((bf16[256,1376]{0,1:T(8,128)(2,1)}), bf16[2048,1376]{0,1:T(8,128)(2,1)}) %all-gather.10.cloned.1.call-update) | async-done | bytes 5636112 | tf_op jit(solution)/shard_map/all_gather | solution.py:216
  288.2 16.4 %multiply_convert_fusion.1 = (bf16[1024,1376]{0,1:T(8,128)(2,1)}, bf16[1024,1376]{0,1:T(8,128)(2,1)}, bf16[1024,1376]{0,1:T(8,128)(2,1)}) fusion(f32[1024,1376]{0,1:T(8,128)} %fusion.140, f32[1024,1376]{0,1:T(8,128)} %fusion.138, bf16[1024,2048]{1,0:T(8,128)(2,1)} %bitcast.349, bf16[2048,1376]{0,1:T(8,128)(2,1)} %all-gather.10.cloned.1.call-done), kind=kOutput, calls=%fused_computation.58 | convolution fusion | flops 5793906688 | bytes 29556736 | tf_op jit(solution)/shard_map/dot_general | solution.py:16
  313.5 9.0 %convolution_add_fusion.1 = f32[1024,2048]{1,0:T(8,128)S(1)} fusion(f32[1024,2048]{1,0:T(8,128)S(1)} %fusion.141, bf16[1024,1376]{0,1:T(8,128)(2,1)} %get-tuple-element.358, bf16[2048,1376]{0,1:T(8,128)(2,1)S(1)} %copy-done.26), kind=kOutput, calls=%fused_computation.74 | convolution fusion | flops 5773459456 | bytes 25231360 | tf_op jit(solution)/shard_map/dot_general | solution.py:26
  326.8 8.9 %fusion.139 = f32[1024,2048]{1,0:T(8,128)S(1)} fusion(bf16[1024,1376]{0,1:T(8,128)(2,1)S(1)} %copy-done.69, bf16[1376,2048]{1,0:T(8,128)(2,1)} %all-gather.14.cloned.1.call-done), kind=kOutput, calls=%fused_computation.346 | convolution fusion | flops 5771362304 | bytes 16842752 | tf_op jit(solution)/shard_map/dot_general | solution.py:16
  353.4 18.9 %collective-permute-done.8 = bf16[2,256,1024]{2,1,0:T(8,128)(2,1)S(1)} collective-permute-done((bf16[2,256,1024]{2,1,0:T(8,128)(2,1)S(1)}, bf16[2,256,1024]{2,1,0:T(8,128)(2,1)S(1)}, u32[]{:S(2)}, u32[]{:S(2)}) %collective-permute-start.8) | collective-permute-done | bytes 1048608 | tf_op jit(solution)/shard_map/ppermute | solution.py:129
  374.0 28.4 %collective-permute-done.17 = bf16[1,256,1024]{2,1,0:T(8,128)(2,1)S(1)} collective-permute-done((bf16[1,256,1024]{2,1,0:T(8,128)(2,1)S(1)}, bf16[1,256,1024]{2,1,0:T(8,128)(2,1)S(1)}, u32[]{:S(2)}, u32[]{:S(2)}) %collective-permute-start.17) | collective-permute-done | bytes 524320 | tf_op jit(solution)/shard_map/ppermute | solution.py:129
  433.2 10.9 %collective-permute-done.20 = bf16[1,256,1024]{2,1,0:T(8,128)(2,1)S(1)} collective-permute-done((bf16[1,256,1024]{2,1,0:T(8,128)(2,1)S(1)}, bf16[1,256,1024]{2,1,0:T(8,128)(2,1)S(1)}, u32[]{:S(2)}, u32[]{:S(2)}) %collective-permute-start.20) | collective-permute-done | bytes 524320 | tf_op jit(solution)/shard_map/ppermute | solution.py:129
  446.4 21.3 %collective-permute-done.21 = bf16[2,256,1024]{2,1,0:T(8,128)(2,1)S(1)} collective-permute-done((bf16[2,256,1024]{2,1,0:T(8,128)(2,1)S(1)}, bf16[2,256,1024]{2,1,0:T(8,128)(2,1)S(1)}, u32[]{:S(2)}, u32[]{:S(2)}) %collective-permute-start.21) | collective-permute-done | bytes 1048608 | tf_op jit(solution)/shard_map/ppermute | solution.py:129
  473.5 10.4 %convolution_convert_fusion.1 = bf16[2048,1376]{0,1:T(8,128)(2,1)} fusion(bf16[1024,1376]{0,1:T(8,128)(2,1)} %get-tuple-element.359, bf16[1024,2048]{1,0:T(8,128)(2,1)} %bitcast.350), kind=kOutput, calls=%fused_computation.55 | convolution fusion | flops 5774180352 | bytes 12648448 | tf_op jit(solution)/shard_map/dot_general | solution.py:20
  484.1 10.3 %convolution_convert_fusion = bf16[2048,1376]{0,1:T(8,128)(2,1)} fusion(bf16[1024,1376]{0,1:T(8,128)(2,1)} %get-tuple-element.358, bf16[1024,2048]{1,0:T(8,128)(2,1)} %bitcast.351), kind=kOutput, calls=%fused_computation.54 | convolution fusion | flops 5774180352 | bytes 12648448 | tf_op jit(solution)/shard_map/dot_general | solution.py:20
  500.6 10.3 %convolution_convert_fusion.2 = bf16[1376,2048]{1,0:T(8,128)(2,1)} fusion(bf16[1024,1376]{0,1:T(8,128)(2,1)} %get-tuple-element.360, bf16[1024,2048]{1,0:T(8,128)(2,1)} %bitcast.347), kind=kOutput, calls=%fused_computation.56 | convolution fusion | flops 5774180352 | bytes 12648448 | tf_op jit(solution)/shard_map/dot_general | solution.py:20
  530.4 56.3 %while.29 = (s32[]{:T(128)}, f32[1024,4,128]{0,2,1:T(8,128)S(1)}, f32[1024,4,128]{0,2,1:T(8,128)}, f32[2,512,4,128]{3,1,0,2:T(8,128)}, s32[2]{0:T(128)S(1)}, /*i...) while((s32[]{:T(128)}, f32[1024,4,128]{0,2,1:T(8,128)S(1)}, ...), condition=%wide.region_10.11_spmd.clone, body=%wide.region_8.10_spmd.clone.sunk | while | flops 2709257728 | bytes 166771616 | solution.py:124
  643.0 11.6 %pad_maximum_fusion = bf16[2048,1536]{0,1:T(8,128)(2,1)} fusion(bf16[2048,512]{0,1:T(8,128)(2,1)S(1)} %convolution_convert_fusion.3, bf16[2048,512]{0,1:T(8,128)(2,1)S(1)} %convolution_convert_fusion.4, bf16[2048,512]{0,1:T(8,128)(2,1)S(1)} %convolution_convert_fusion.5), kind=kLoop, calls=%fused_computation.57 | loop fusion | flops 18874368 | bytes 12582912 | tf_op jit(solution)/shard_map/concatenate | solution.py:299
  666.5 24.7 %collective-permute-done.33 = bf16[1,256,1024]{2,1,0:T(8,128)(2,1)S(1)} collective-permute-done((bf16[1,256,1024]{2,1,0:T(8,128)(2,1)S(1)}, bf16[1,256,1024]{2,1,0:T(8,128)(2,1)S(1)}, u32[]{:S(2)}, u32[]{:S(2)}) %collective-permute-start.33) | collective-permute-done | bytes 524320 | tf_op jit(solution)/shard_map/ppermute | solution.py:129
  746.1 26.9 %collective-permute-done.30 = bf16[1,256,1024]{2,1,0:T(8,128)(2,1)S(1)} collective-permute-done((bf16[1,256,1024]{2,1,0:T(8,128)(2,1)S(1)}, bf16[1,256,1024]{2,1,0:T(8,128)(2,1)S(1)}, u32[]{:S(2)}, u32[]{:S(2)}) %collective-permute-start.30) | collective-permute-done | bytes 524320 | tf_op jit(solution)/shard_map/ppermute | solution.py:129
  773.8 21.2 %collective-permute-done.29 = bf16[2,256,1024]{2,1,0:T(8,128)(2,1)S(1)} collective-permute-done((bf16[2,256,1024]{2,1,0:T(8,128)(2,1)S(1)}, bf16[2,256,1024]{2,1,0:T(8,128)(2,1)S(1)}, u32[]{:S(2)}, u32[]{:S(2)}) %collective-permute-start.29) | collective-permute-done | bytes 1048608 | tf_op jit(solution)/shard_map/ppermute | solution.py:129
  (511 shorter events, 422.5 us)
Async XLA Ops:
  7.2 70.6 %all-gather.6.cloned.1.call-start = ((), (), s32[]{:S(2)}) async-start(), calls=%async_computation.5 | async-start | bytes 7077888 | tf_op jit(solution)/shard_map/all_gather | solution.py:211
  9.3 136.5 %all-gather.8.cloned.1.call-start = ((), (), s32[]{:S(2)}) async-start(), calls=%async_computation.6 | async-start | bytes 2359296 | tf_op jit(solution)/shard_map/all_gather | solution.py:215
  10.0 214.7 %all-gather.14.cloned.1.call-start = ((), (), s32[]{:S(2)}) async-start(), calls=%async_computation.9 | async-start | bytes 6340608 | tf_op jit(solution)/shard_map/all_gather | solution.py:218
  10.8 238.2 %all-gather.12.cloned.1.call-start = ((), (), s32[]{:S(2)}) async-start(), calls=%async_computation.8 | async-start | bytes 6340608 | tf_op jit(solution)/shard_map/all_gather | solution.py:217
  11.4 276.8 %all-gather.10.cloned.1.call-start = ((), (), s32[]{:S(2)}) async-start(), calls=%async_computation.7 | async-start | bytes 6340608 | tf_op jit(solution)/shard_map/all_gather | solution.py:216
  178.1 629.8 %reduce-scatter.8.cloned.1.call-start = ((), (), s32[]{:S(2)}) async-start(), calls=%async_computation.11 | async-start | bytes 2359296 | tf_op jit(solution)/shard_map/reduce_scatter | solution.py:282
  339.8 32.5 %collective-permute-start.8 = (bf16[2,256,1024]{2,1,0:T(8,128)(2,1)S(1)}, bf16[2,256,1024]{2,1,0:T(8,128)(2,1)S(1)}, u32[]{:S(2)}, u32[]{:S(2)}) collective-permute-start(bf16[2,256,1024]{2,1,0:T(8,128)(2,1)S(1)} %pad_maximum_fusion.17), channel_id=1, source_target_pairs={{0,1},{1,0},{2,3},{3,2},{4,5},{5,4},{6,7},{7,6},{8,9},{9,8},{10,11... | collective-permute-start | bytes 3145736 | tf_op jit(solution)/shard_map/ppermute | solution.py:129
  342.6 31.4 %collective-permute-start.18 = (bf16[2,256,1024]{2,1,0:T(8,128)(2,1)S(1)}, bf16[2,256,1024]{2,1,0:T(8,128)(2,1)S(1)}, u32[]{:S(2)}, u32[]{:S(2)}) collective-permute-start(bf16[2,256,1024]{2,1,0:T(8,128)(2,1)S(1)} %slice.521), channel_id=1, source_target_pairs={{0,2},{1,3},{2,0},{3,1},{4,6},{5,7},{6,4},{7,5},{8,10},{9,11},{10,... | collective-permute-start | bytes 3145736 | tf_op jit(solution)/shard_map/ppermute | solution.py:129
  345.5 59.1 %collective-permute-start.10 = (bf16[2,256,1024]{2,1,0:T(8,128)(2,1)S(1)}, bf16[2,256,1024]{2,1,0:T(8,128)(2,1)S(1)}, u32[]{:S(2)}, u32[]{:S(2)}) collective-permute-start(bf16[2,256,1024]{2,1,0:T(8,128)(2,1)S(1)} %slice.504), channel_id=1, source_target_pairs={{0,2},{1,3},{2,0},{3,1},{4,6},{5,7},{6,4},{7,5},{8,10},{9,11},{10,... | collective-permute-start | bytes 3145736 | tf_op jit(solution)/shard_map/ppermute | solution.py:129
  351.8 50.6 %collective-permute-start.17 = (bf16[1,256,1024]{2,1,0:T(8,128)(2,1)S(1)}, bf16[1,256,1024]{2,1,0:T(8,128)(2,1)S(1)}, u32[]{:S(2)}, u32[]{:S(2)}) collective-permute-start(bf16[1,256,1024]{2,1,0:T(8,128)(2,1)S(1)} %fusion.85), channel_id=1, source_target_pairs={{0,2},{1,3},{2,0},{3,1},{4,6},{5,7},{6,4},{7,5},{8,10},{9,11},{10,... | collective-permute-start | bytes 1572872 | tf_op jit(solution)/shard_map/ppermute | solution.py:129
  372.5 40.2 %collective-permute-start.9 = (bf16[1,256,1024]{2,1,0:T(8,128)(2,1)S(1)}, bf16[1,256,1024]{2,1,0:T(8,128)(2,1)S(1)}, u32[]{:S(2)}, u32[]{:S(2)}) collective-permute-start(bf16[1,256,1024]{2,1,0:T(8,128)(2,1)S(1)} %fusion.91), channel_id=1, source_target_pairs={{0,2},{1,3},{2,0},{3,1},{4,6},{5,7},{6,4},{7,5},{8,10},{9,11},{10,... | collective-permute-start | bytes 1572872 | tf_op jit(solution)/shard_map/ppermute | solution.py:129
  473.5 336.1 %reduce-scatter.10.cloned.1.call-start = ((), (), s32[]{:S(2)}) async-start(), calls=%async_computation.12 | async-start | bytes 6340608 | tf_op jit(solution)/shard_map/reduce_scatter | solution.py:270
  484.0 327.9 %reduce-scatter.12.cloned.1.call-start = ((), (), s32[]{:S(2)}) async-start(), calls=%async_computation.13 | async-start | bytes 6340608 | tf_op jit(solution)/shard_map/reduce_scatter | solution.py:272
  494.4 319.9 %reduce-scatter.14.cloned.1.call-start = ((), (), s32[]{:S(2)}) async-start(), calls=%async_computation.14 | async-start | bytes 6340608 | tf_op jit(solution)/shard_map/reduce_scatter | solution.py:260
  510.9 305.6 %reduce-scatter.6.cloned.1.call-start = ((), (), s32[]{:S(2)}) async-start(), calls=%async_computation.10 | async-start | bytes 7077888 | tf_op jit(solution)/shard_map/reduce_scatter | solution.py:307
  513.4 141.1 %collective-permute-start.13 = (bf16[2,256,1024]{2,1,0:T(8,128)(2,1)}, bf16[2,256,1024]{2,1,0:T(8,128)(2,1)}, u32[]{:S(2)}, u32[]{:S(2)}) collective-permute-start(bf16[2,256,1024]{2,1,0:T(8,128)(2,1)} %pad_maximum_fusion.18), channel_id=1, source_target_pairs={{0,1},{1,0},{2,3},{3,2},{4,5},{5,4},{6,7},{7,6},{8,9},{9,8},{10,11... | collective-permute-start | bytes 3145736 | tf_op jit(solution)/shard_map/ppermute | solution.py:129
  516.4 141.3 %collective-permute-start.15 = (bf16[2,256,1024]{2,1,0:T(8,128)(2,1)}, bf16[2,256,1024]{2,1,0:T(8,128)(2,1)}, u32[]{:S(2)}, u32[]{:S(2)}) collective-permute-start(bf16[2,256,1024]{2,1,0:T(8,128)(2,1)} %pad_maximum_fusion.19), channel_id=1, source_target_pairs={{0,2},{1,3},{2,0},{3,1},{4,6},{5,7},{6,4},{7,5},{8,10},{9,11},{10,... | collective-permute-start | bytes 3145736 | tf_op jit(solution)/shard_map/ppermute | solution.py:129
  620.7 40.1 %collective-permute-start.32 = (bf16[2,256,1024]{2,1,0:T(8,128)(2,1)}, bf16[2,256,1024]{2,1,0:T(8,128)(2,1)}, u32[]{:S(2)}, u32[]{:S(2)}) collective-permute-start(bf16[2,256,1024]{2,1,0:T(8,128)(2,1)} %pad_maximum_fusion.31), channel_id=1, source_target_pairs={{0,1},{1,0},{2,3},{3,2},{4,5},{5,4},{6,7},{7,6},{8,9},{9,8},{10,11... | collective-permute-start | bytes 3145736 | tf_op jit(solution)/shard_map/ppermute | solution.py:129
  621.8 44.6 %collective-permute-start.34 = (bf16[2,256,1024]{2,1,0:T(8,128)(2,1)}, bf16[2,256,1024]{2,1,0:T(8,128)(2,1)}, u32[]{:S(2)}, u32[]{:S(2)}) collective-permute-start(bf16[2,256,1024]{2,1,0:T(8,128)(2,1)} %slice.559), channel_id=1, source_target_pairs={{0,2},{1,3},{2,0},{3,1},{4,6},{5,7},{6,4},{7,5},{8,10},{9,11},{10,... | collective-permute-start | bytes 3145736 | tf_op jit(solution)/shard_map/ppermute | solution.py:129
  654.5 40.5 %collective-permute-start.26 = (bf16[2,256,1024]{2,1,0:T(8,128)(2,1)S(1)}, bf16[2,256,1024]{2,1,0:T(8,128)(2,1)S(1)}, u32[]{:S(2)}, u32[]{:S(2)}) collective-permute-start(bf16[2,256,1024]{2,1,0:T(8,128)(2,1)S(1)} %slice.540), channel_id=1, source_target_pairs={{0,2},{1,3},{2,0},{3,1},{4,6},{5,7},{6,4},{7,5},{8,10},{9,11},{10,... | collective-permute-start | bytes 3145736 | tf_op jit(solution)/shard_map/ppermute | solution.py:129
  735.7 37.7 %collective-permute-start.37 = (bf16[2,256,1024]{2,1,0:T(8,128)(2,1)S(1)}, bf16[2,256,1024]{2,1,0:T(8,128)(2,1)S(1)}, u32[]{:S(2)}, u32[]{:S(2)}) collective-permute-start(bf16[2,256,1024]{2,1,0:T(8,128)(2,1)S(1)} %pad_maximum_fusion.32), channel_id=1, source_target_pairs={{0,1},{1,0},{2,3},{3,2},{4,5},{5,4},{6,7},{7,6},{8,9},{9,8},{10,11... | collective-permute-start | bytes 3145736 | tf_op jit(solution)/shard_map/ppermute | solution.py:129
  736.8 36.7 %collective-permute-start.39 = (bf16[2,256,1024]{2,1,0:T(8,128)(2,1)S(1)}, bf16[2,256,1024]{2,1,0:T(8,128)(2,1)S(1)}, u32[]{:S(2)}, u32[]{:S(2)}) collective-permute-start(bf16[2,256,1024]{2,1,0:T(8,128)(2,1)S(1)} %pad_maximum_fusion.33), channel_id=1, source_target_pairs={{0,2},{1,3},{2,0},{3,1},{4,6},{5,7},{6,4},{7,5},{8,10},{9,11},{10,... | collective-permute-start | bytes 3145736 | tf_op jit(solution)/shard_map/ppermute | solution.py:129
  739.5 33.5 %collective-permute-start.30 = (bf16[1,256,1024]{2,1,0:T(8,128)(2,1)S(1)}, bf16[1,256,1024]{2,1,0:T(8,128)(2,1)S(1)}, u32[]{:S(2)}, u32[]{:S(2)}) collective-permute-start(bf16[1,256,1024]{2,1,0:T(8,128)(2,1)S(1)} %get-tuple-element.431), channel_id=1, source_target_pairs={{0,1},{1,0},{2,3},{3,2},{4,5},{5,4},{6,7},{7,6},{8,9},{9,8},{10,11... | collective-permute-start | bytes 1572872 | tf_op jit(solution)/shard_map/ppermute | solution.py:129
  745.1 50.0 %collective-permute-start.29 = (bf16[2,256,1024]{2,1,0:T(8,128)(2,1)S(1)}, bf16[2,256,1024]{2,1,0:T(8,128)(2,1)S(1)}, u32[]{:S(2)}, u32[]{:S(2)}) collective-permute-start(bf16[2,256,1024]{2,1,0:T(8,128)(2,1)S(1)} %pad_maximum_fusion.26), channel_id=1, source_target_pairs={{0,1},{1,0},{2,3},{3,2},{4,5},{5,4},{6,7},{7,6},{8,9},{9,8},{10,11... | collective-permute-start | bytes 3145736 | tf_op jit(solution)/shard_map/ppermute | solution.py:129
  (116 other events, 1475.2 us)
Sparse Core Ops, SparseCore 0:
  10.2 67.5 all-gather.5
  79.4 29.4 all-gather.7
  110.5 58.8 all-gather.13
  170.8 57.9 all-gather.11
  230.2 57.9 all-gather.9
  473.6 33.5 reduce-scatter.7
  509.5 62.2 reduce-scatter.9
  574.3 61.9 reduce-scatter.11
  638.6 61.9 reduce-scatter.13
  702.9 68.6 reduce-scatter.5

commit v2 on v1

v2 whole, which is shorter than its diff:
```python
import functools

import jax
import jax.numpy as jnp
from jax import lax
from jax.experimental import pallas as pl
from jax.experimental.pallas import tpu as pltpu
from jax.sharding import PartitionSpec as P

HD = 128
QROWS = 256
BF = jnp.bfloat16
F32 = jnp.float32
epsilon = 1e-06
VMEM_LIMIT = 60 * 1024 * 1024


def plain_dot(left, right):
    return jnp.dot(left, right, preferred_element_type=jnp.float32)


def last_dims(left, right):
    return lax.dot_general(
        left, right, (((1,), (1,)), ((), ())), preferred_element_type=jnp.float32
    )


def round_up(number, unit):
    return (number + unit - 1) // unit * unit


def head_group(wide):
    return 2 * HD if wide % (2 * HD) == 0 else HD


def limits():
    return pltpu.CompilerParams(vmem_limit_bytes=VMEM_LIMIT)


def turn(values, cosine, sine):
    return values * cosine + pltpu.roll(values, HD // 2, 1) * sine


def forward_kernel(
    size,
    place_ref,
    normed_ref,
    kv_ref,
    wq_ref,
    wk_ref,
    wv_ref,
    cos_ref,
    sin_ref,
    q_ref,
    k_ref,
    v_ref,
    out_ref,
    flip_ref,
):
    me, live = place_ref[0], place_ref[1]
    length = normed_ref.shape[0]
    group = wq_ref.shape[1]
    part = length // size
    cosine, sine = cos_ref[...], sin_ref[...]
    q_pre = plain_dot(normed_ref[...], wq_ref[...])
    for at in range(0, group, HD):
        q_ref[:, at : at + HD] = turn(q_pre[:, at : at + HD], cosine, sine).astype(BF)
    k_pre = plain_dot(kv_ref[...], wk_ref[...])
    for at in range(0, group, HD):
        k_ref[:, at : at + HD] = turn(k_pre[:, at : at + HD], cosine, sine).astype(BF)
    v_ref[...] = plain_dot(kv_ref[...], wv_ref[...]).astype(BF)
    for at in range(0, group, HD):
        for start in range(0, length, QROWS):
            stop = start + QROWS
            scores = last_dims(q_ref[start:stop, at : at + HD], k_ref[:stop, at : at + HD])
            scores = scores * HD ** (-0.5)
            rows = start + lax.broadcasted_iota(jnp.int32, (QROWS, 1), 0)
            bound = jnp.minimum(rows, live - 1)
            columns = lax.broadcasted_iota(jnp.int32, (QROWS, stop), 1)
            scores = jnp.where(columns <= bound, scores, -1e30)
            largest = jnp.max(scores, axis=1, keepdims=True)
            expo = jnp.exp(scores - largest)
            probs = (expo / jnp.sum(expo, axis=1, keepdims=True)).astype(BF)
            result = plain_dot(probs, v_ref[:stop, at : at + HD])
            flipped = result.T.astype(BF)
            result = result.astype(BF)
            step = min(part, QROWS)
            for piece in range(0, QROWS, step):
                block = (start + piece) // part
                row = pl.multiple_of((block ^ me) * part, part) + (start + piece) % part
                rows_at = pl.ds(pl.multiple_of(row, 128), step)
                out_ref[rows_at, at : at + HD] = result[piece : piece + step]
                flip_ref[at : at + HD, rows_at] = flipped[:, piece : piece + step]


def attend_forward(place, normed, kv_normed, weights, cosine, sine, size):
    length, width = normed.shape
    wide = weights.shape[1] // 4
    group = head_group(wide)
    groups = wide // group
    whole = pl.BlockSpec((length, width), lambda g: (0, 0))
    table = pl.BlockSpec((length, HD), lambda g: (0, 0))
    heads = pl.BlockSpec((length, group), lambda g: (0, g))
    out = jax.ShapeDtypeStruct((length, wide), BF)
    return pl.pallas_call(
        functools.partial(forward_kernel, size),
        grid=(groups,),
        in_specs=[
            pl.BlockSpec(memory_space=pltpu.SMEM),
            whole,
            whole,
            pl.BlockSpec((width, group), lambda g: (0, g)),
            pl.BlockSpec((width, group), lambda g: (0, g + groups)),
            pl.BlockSpec((width, group), lambda g: (0, g + 2 * groups)),
            table,
            table,
        ],
        out_specs=[heads] * 4 + [pl.BlockSpec((group, length), lambda g: (g, 0))],
        out_shape=[out] * 4 + [jax.ShapeDtypeStruct((wide, length), BF)],
        compiler_params=limits(),
        cost_estimate=pl.CostEstimate(
            flops=6 * length * width * wide + 3 * length * length * wide,
            bytes_accessed=4 * length * width + 6 * width * wide + 8 * length * wide,
            transcendentals=length * length * wide // HD,
        ),
    )(place, normed, kv_normed, weights, weights, weights, cosine, sine)


def backward_kernel(
    size,
    place_ref,
    grad_ref,
    wo_ref,
    q_ref,
    k_ref,
    v_ref,
    cos_ref,
    sin_ref,
    rq_ref,
    rk_ref,
    rv_ref,
    flip_ref,
    ga_ref,
    kt_ref,
    sum_k,
    sum_v,
):
    me, live = place_ref[0], place_ref[1]
    length = grad_ref.shape[0]
    group = wo_ref.shape[1]
    part = length // size
    scale = HD ** (-0.5)
    cosine, sine = cos_ref[...], -sin_ref[...]

    def home(row):
        block = row // part
        return pl.multiple_of(pl.multiple_of((block ^ me) * part, part) + row % part, 128)

    for block in range(size):
        ga_ref[pl.ds(home(block * part), part), :] = plain_dot(
            grad_ref[block * part : (block + 1) * part, :], wo_ref[...]
        ).astype(BF)
    step = min(part, QROWS)
    for at in range(0, group, HD):
        kt_ref[...] = k_ref[:, at : at + HD].T
        for start in reversed(range(0, length, QROWS)):
            stop = start + QROWS
            queries = q_ref[start:stop, at : at + HD]
            grads = ga_ref[start:stop, at : at + HD]
            scores = last_dims(k_ref[:stop, at : at + HD], queries) * scale
            columns = start + lax.broadcasted_iota(jnp.int32, (1, QROWS), 1)
            bound = jnp.minimum(columns, live - 1)
            rows = lax.broadcasted_iota(jnp.int32, (stop, QROWS), 0)
            scores = jnp.where(rows <= bound, scores, -1e30)
            largest = jnp.max(scores, axis=0, keepdims=True)
            expo = jnp.exp(scores - largest)
            probs = expo * (1.0 / jnp.sum(expo, axis=0, keepdims=True))
            grad_probs = last_dims(v_ref[:stop, at : at + HD], grads)
            inner = jnp.sum(probs * grad_probs, axis=0, keepdims=True)
            grad_scores = (probs * (grad_probs - inner)).astype(BF)
            add_k = plain_dot(grad_scores, queries)
            add_v = plain_dot(probs.astype(BF), grads)
            if stop == length:
                sum_k[...] = add_k
                sum_v[...] = add_v
            else:
                sum_k[:stop] += add_k
                sum_v[:stop] += add_v
            grad_q = plain_dot(kt_ref[:, :stop], grad_scores).T * scale
            grad_q = turn(grad_q, cosine[start:stop], sine[start:stop])
            flip_ref[0, at : at + HD, start:stop] = grad_q.T.astype(BF)
            grad_q = grad_q.astype(BF)
            for piece in range(0, QROWS, step):
                rq_ref[pl.ds(home(start + piece), step), at : at + HD] = grad_q[
                    piece : piece + step
                ]
        grad_k = turn(sum_k[...] * scale, cosine, sine)
        grad_v = sum_v[...]
        flip_ref[1, at : at + HD, :] = grad_k.T.astype(BF)
        flip_ref[2, at : at + HD, :] = grad_v.T.astype(BF)
        grad_k, grad_v = grad_k.astype(BF), grad_v.astype(BF)
        for block in range(size):
            rows = slice(block * part, (block + 1) * part)
            rk_ref[pl.ds(home(block * part), part), at : at + HD] = grad_k[rows]
            rv_ref[pl.ds(home(block * part), part), at : at + HD] = grad_v[rows]


def attend_backward(place, grad_mid_low, weights, queries, keys, values, cosine, sine, size):
    length, width = grad_mid_low.shape
    wide = queries.shape[1]
    group = head_group(wide)
    groups = wide // group
    table = pl.BlockSpec((length, HD), lambda g: (0, 0))
    heads = pl.BlockSpec((length, group), lambda g: (0, g))
    out = jax.ShapeDtypeStruct((length, wide), BF)
    return pl.pallas_call(
        functools.partial(backward_kernel, size),
        grid=(groups,),
        in_specs=[
            pl.BlockSpec(memory_space=pltpu.SMEM),
            pl.BlockSpec((length, width), lambda g: (0, 0)),
            pl.BlockSpec((width, group), lambda g: (0, g + 3 * groups)),
            heads,
            heads,
            heads,
            table,
            table,
        ],
        out_specs=[heads] * 3 + [pl.BlockSpec((3, group, length), lambda g: (0, g, 0))],
        out_shape=[out] * 3 + [jax.ShapeDtypeStruct((3, wide, length), BF)],
        scratch_shapes=[
            pltpu.VMEM((length, group), BF),
            pltpu.VMEM((HD, length), BF),
            pltpu.VMEM((length, HD), F32),
            pltpu.VMEM((length, HD), F32),
        ],
        compiler_params=limits(),
        cost_estimate=pl.CostEstimate(
            flops=2 * length * width * wide + 10 * length * length * wide,
            bytes_accessed=2 * length * width + 2 * width * wide + 18 * length * wide,
            transcendentals=length * length * wide // HD,
        ),
    )(place, grad_mid_low, weights, queries, keys, values, cosine, sine)


def feed_kernel(x_ref, g_ref, wg_ref, wu_ref, wd_ref, act_ref, gate_ref, up_ref, flip_ref):
    gate = plain_dot(x_ref[...], wg_ref[...])
    up = plain_dot(x_ref[...], wu_ref[...])
    grad = plain_dot(g_ref[...], wd_ref[...])
    sigma = 1.0 / (1.0 + jnp.exp(-gate))
    silu = gate * sigma
    act = silu * up
    grad_up = grad * silu
    grad_gate = grad * up * (sigma + silu * (1.0 - sigma))
    act_ref[...] = act.astype(BF)
    up_ref[...] = grad_up.astype(BF)
    gate_ref[...] = grad_gate.astype(BF)
    flip_ref[0] = grad_gate.T.astype(BF)
    flip_ref[1] = grad_up.T.astype(BF)
    flip_ref[2] = act.T.astype(BF)


def feed_forward(ffn_in, grad_low, weights):
    length, width = ffn_in.shape
    units = weights.shape[1] // 3
    step = 256 if units % 256 == 0 else 128
    steps = units // step
    whole = pl.BlockSpec((length, width), lambda f: (0, 0))
    out = pl.BlockSpec((length, step), lambda f: (0, f))
    return pl.pallas_call(
        feed_kernel,
        grid=(steps,),
        in_specs=[
            whole,
            whole,
            pl.BlockSpec((width, step), lambda f: (0, f)),
            pl.BlockSpec((width, step), lambda f: (0, f + steps)),
            pl.BlockSpec((width, step), lambda f: (0, f + 2 * steps)),
        ],
        out_specs=[out] * 3 + [pl.BlockSpec((3, step, length), lambda f: (0, f, 0))],
        out_shape=[jax.ShapeDtypeStruct((length, units), BF)] * 3
        + [jax.ShapeDtypeStruct((3, units, length), BF)],
        compiler_params=limits(),
        cost_estimate=pl.CostEstimate(
            flops=6 * length * width * units,
            bytes_accessed=4 * length * width + 6 * width * units + 12 * length * units,
            transcendentals=2 * length * units,
        ),
    )(ffn_in, grad_low, weights, weights, weights)


def products_kernel(counts, *refs):
    step = pl.program_id(0)
    lefts, rights, out_ref = refs[: len(counts)], refs[len(counts) : -1], refs[-1]
    first = 0
    for (steps, right), left in zip(counts, lefts):

        @pl.when((step >= first) & (step < first + steps))
        def _(left=left, right=right):
            out_ref[...] = plain_dot(left[...], rights[right][...]).astype(BF)

        first += steps


def products(terms, rights):
    length, width = rights[0].shape
    step = 256 if all(left.shape[1] % 256 == 0 for left, _, _ in terms) else 128
    counts = tuple((left.shape[1] // step, at) for left, _, at in terms)
    total = sum(steps for steps, _ in counts)
    left_specs = []
    first = 0
    for (steps, _), (_, lead, _) in zip(counts, terms):

        def block(i, first=first, last=steps - 1, lead=lead):
            return (lead, lax.max(lax.min(i - first, last), 0), 0)

        left_specs.append(pl.BlockSpec((None, step, length), block))
        first += steps
    return pl.pallas_call(
        functools.partial(products_kernel, counts),
        grid=(total,),
        in_specs=left_specs + [pl.BlockSpec((length, width), lambda i: (0, 0))] * len(rights),
        out_specs=pl.BlockSpec((step, width), lambda i: (i, 0)),
        out_shape=jax.ShapeDtypeStruct((total * step, width), BF),
        compiler_params=limits(),
        cost_estimate=pl.CostEstimate(
            flops=2 * total * step * length * width,
            bytes_accessed=2 * (total * step * (length + width) + len(rights) * length * width),
            transcendentals=0,
        ),
    )(*[left for left, _, _ in terms], *rights)


def rows_kernel(count, *refs):
    out_ref = refs[-1]
    total = None
    for left, right in zip(refs[:count], refs[count:-1]):
        rows = left[...].reshape(-1, left.shape[-1])
        part = last_dims(rows, right[...])
        total = part if total is None else total + part
    out_ref[...] = total.astype(BF).reshape(out_ref.shape)


def row_products(terms, bit, side, half, width):
    columns = width // 2
    step = 512 if columns % 512 == 0 else columns
    left_specs, right_specs, lefts, rights = [], [], [], []
    flops = nbytes = 0
    for left, right, at in terms:
        rows, depth = left.shape[0] // 4, left.shape[1]
        lefts.append(left.reshape(2, 2, rows, depth))
        if bit == 1:
            left_specs.append(pl.BlockSpec((2, 1, rows, depth), lambda j: (0, side, 0, 0)))
        else:
            left_specs.append(pl.BlockSpec((1, 2, rows, depth), lambda j: (side, 0, 0, 0)))
        right_specs.append(
            pl.BlockSpec(
                (step, depth), lambda j, at=at: (half * (columns // step) + j, at)
            )
        )
        rights.append(right)
        flops += 4 * rows * depth * columns
        nbytes += 2 * depth * (2 * rows + columns)
    return pl.pallas_call(
        functools.partial(rows_kernel, len(terms)),
        grid=(columns // step,),
        in_specs=left_specs + right_specs,
        out_specs=pl.BlockSpec((2, rows, step), lambda j: (0, 0, j)),
        out_shape=jax.ShapeDtypeStruct((2, rows, columns), BF),
        compiler_params=limits(),
        cost_estimate=pl.CostEstimate(
            flops=flops, bytes_accessed=nbytes + 4 * rows * columns, transcendentals=0
        ),
    )(*lefts, *rights)


def rms_scale(values, gain):
    inverse = lax.rsqrt(jnp.mean(values * values, axis=-1, keepdims=True) + epsilon)
    return (inverse, values * inverse * gain)


def norm_back(grad, values, inverse, gain):
    scaled = grad * gain
    inner = jnp.mean(scaled * values, axis=-1, keepdims=True)
    return (
        inverse * scaled - values * inverse**3 * inner,
        jnp.sum(grad * values * inverse, axis=0),
    )


def rotary_tables(length):
    position = jnp.arange(length, dtype=jnp.float32)
    freqs = jnp.exp(-jnp.log(10000.0) * jnp.arange(HD // 2, dtype=jnp.float32) * 2.0 / HD)
    angle = position[:, None] * freqs[None, :]
    cosine, sine = jnp.cos(angle), jnp.sin(angle)
    return (jnp.concatenate([cosine, cosine], 1), jnp.concatenate([-sine, sine], 1))


def after(value, *earlier):
    return lax.optimization_barrier((value, *earlier))[0]


def swap(array, bit, size):
    return lax.ppermute(array, "tensor", [(t, t ^ bit) for t in range(size)])


def bit_orders(size):
    bits = [1 << step for step in range(size.bit_length() - 1)]
    return (bits, bits[1:] + bits[:1])


def relative(array, me, size):
    part = array.shape[0] // size
    return jnp.stack(
        [lax.dynamic_slice_in_dim(array, (me ^ step) * part, part, 0) for step in range(size)]
    )


def absolute(blocks, me):
    parts = [
        lax.dynamic_index_in_dim(blocks, me ^ step, 0, keepdims=False)
        for step in range(blocks.shape[0])
    ]
    return jnp.concatenate(parts, axis=0)


def scatter_sum(blocks):
    size = blocks.shape[0]
    half = blocks.shape[2] // 2
    sums = []
    for group, order in enumerate(bit_orders(size)):
        held = {
            place: blocks[place, :, group * half : (group + 1) * half].astype(F32)
            for place in range(size)
        }
        for bit in order:
            sent = [place for place in held if place & bit]
            got = swap(jnp.stack([held[place].astype(BF) for place in sent]), bit, size)
            held = {
                place ^ bit: held[place ^ bit] + got[at].astype(F32)
                for at, place in enumerate(sent)
            }
        sums.append(held[0])
    return jnp.concatenate(sums, axis=1)


def gather_rows(own, size):
    half = own.shape[1] // 2
    parts = []
    for group, order in enumerate(bit_orders(size)):
        held = {0: own[:, group * half : (group + 1) * half]}
        for bit in order[::-1]:
            places = list(held)
            got = swap(jnp.stack([held[place] for place in places]), bit, size)
            for at, place in enumerate(places):
                held[place ^ bit] = got[at]
        parts.append(held)
    return jnp.stack(
        [jnp.concatenate([held[place] for held in parts], axis=1) for place in range(size)]
    )


def product_scatter(terms, size, width):
    if size != 4:
        total = 0.0
        for left, right, at in terms:
            depth = left.shape[1]
            total = total + last_dims(left, right[:, at * depth : (at + 1) * depth])
        return scatter_sum(total.reshape(size, -1, width))
    sent = [row_products(terms, 1 + half, 1, half, width) for half in range(2)]
    got = [swap(sent[half], 1 + half, size).astype(F32) for half in range(2)]
    lefts = after([left for left, _, _ in terms], *sent)
    terms = [(left, right, at) for left, (_, right, at) in zip(lefts, terms)]
    kept = [row_products(terms, 1 + half, 0, half, width).astype(F32) for half in range(2)]
    more = [
        swap((kept[half][1] + got[half][1]).astype(BF), 2 - half, size).astype(F32)
        for half in range(2)
    ]
    return jnp.concatenate([kept[half][0] + got[half][0] + more[half] for half in range(2)], axis=1)


def local(
    hidden_in,
    self_out,
    out_grad,
    lengths,
    w_query,
    w_key,
    w_value,
    w_output,
    w_gate,
    w_up,
    w_down,
    attn_gain,
    ffn_gain,
    kv_gain,
):
    me = lax.axis_index("tensor")
    size = lax.axis_size("tensor")
    dp_size = lax.axis_size("dp")
    length, width = hidden_in.shape
    quarter = length // size
    wide, units = w_query.shape[1], w_gate.shape[1]
    early = round_up(units // 2, 128)
    late = round_up(units - early, 128)

    def columns(array, start, count):
        kept = array[:, start : start + count]
        return jnp.pad(kept, ((0, 0), (0, count - kept.shape[1])))

    w_flip = w_down.T
    mine = [jnp.concatenate([w_query, w_key, w_value, w_output.T], axis=1)]
    for start, count in ((0, early), (early, late)):
        mine.append(
            jnp.concatenate([columns(w, start, count) for w in (w_gate, w_up, w_flip)], axis=1)
        )
    w_heads, w_early, w_late = [lax.all_gather(w, "dp", axis=0, tiled=True) for w in mine]
    gains = lax.all_gather(jnp.stack([attn_gain, ffn_gain, kv_gain]), "dp", axis=1, tiled=True)
    gains = gains.astype(F32)
    attn_scale, ffn_scale, kv_scale = gains[0], gains[1], gains[2]

    place = jnp.stack([me, lengths[0]])
    valid = jnp.arange(length, dtype=jnp.int32) < lengths[0]
    cosine, sine = rotary_tables(length)
    hidden = hidden_in.astype(F32)
    selfout = self_out.astype(F32)
    x_inverse, x_normed = rms_scale(hidden, attn_scale)
    normed = x_normed.astype(BF)
    s_inverse, s_normed = rms_scale(selfout, kv_scale)
    kv_normed = s_normed.astype(BF)

    def own_rows(array):
        return lax.dynamic_slice_in_dim(array, me * quarter, quarter, 0)

    hidden_own = own_rows(hidden_in).astype(F32)
    self_own = own_rows(self_out).astype(F32)
    grad_y_low = relative(jnp.where(valid[:, None], out_grad, jnp.zeros((), BF)), me, size)
    grad_y = grad_y_low[0].astype(F32)
    grad_y_low = grad_y_low.reshape(length, width)

    queries, keys, values, attended_low, attended_flip = attend_forward(
        place, normed, kv_normed, w_heads, cosine, sine, size
    )
    mid_sum = product_scatter([(attended_low, w_heads, 3)], size, width)
    mid = hidden_own + mid_sum
    m_inverse, m_normed = rms_scale(mid, ffn_scale)
    ffn_in = gather_rows(m_normed.astype(BF), size).reshape(length, width)

    act_early, gate_early, up_early, flip_early = feed_forward(ffn_in, grad_y_low, w_early)

    def unit_grads(flip):
        return products([(flip, 0, 0), (flip, 1, 0), (flip, 2, 1)], [ffn_in, grad_y_low])

    grads_early = unit_grads(flip_early)
    sum_early = lax.psum_scatter(grads_early, "dp", scatter_dimension=1, tiled=True)
    act_late, gate_late, up_late, flip_late = feed_forward(
        after(ffn_in, grads_early), grad_y_low, w_late
    )
    back_sum = product_scatter(
        [
            (gate_early, w_early, 0),
            (up_early, w_early, 1),
            (gate_late, w_late, 0),
            (up_late, w_late, 1),
        ],
        size,
        width,
    )
    grads_late = unit_grads(flip_late)
    sum_late = lax.psum_scatter(grads_late, "dp", scatter_dimension=1, tiled=True)

    mid_part, grad_ffn_gain = norm_back(back_sum, mid, m_inverse, ffn_scale)
    grad_mid = grad_y + mid_part
    grad_mid_low = gather_rows(grad_mid.astype(BF), size).reshape(length, width)

    out_sum = product_scatter([(act_early, w_early, 2), (act_late, w_late, 2)], size, width)
    layer_out = absolute(gather_rows((mid + out_sum).astype(BF), size), me)

    rel_q, rel_k, rel_v, flip_heads = attend_backward(
        place, grad_mid_low, w_heads, queries, keys, values, cosine, sine, size
    )
    grad_kv_normed = product_scatter([(rel_k, w_heads, 1), (rel_v, w_heads, 2)], size, width)
    grad_normed = product_scatter([(rel_q, w_heads, 0)], size, width)
    grads_heads = products(
        [(flip_heads, 0, 0), (flip_heads, 1, 1), (flip_heads, 2, 1), (attended_flip[None], 0, 2)],
        [normed, kv_normed, after(grad_mid_low, sum_early)],
    )
    sum_heads = lax.psum_scatter(grads_heads, "dp", scatter_dimension=1, tiled=True).astype(F32)
    x_part, grad_attn_gain = norm_back(grad_normed, hidden_own, own_rows(x_inverse), attn_scale)
    s_part, grad_kv_gain = norm_back(grad_kv_normed, self_own, own_rows(s_inverse), kv_scale)
    self_grad = absolute(gather_rows(s_part.astype(BF), size), me).astype(F32)
    input_grad = absolute(gather_rows((grad_mid + x_part).astype(BF), size), me).astype(F32)

    gain_grads = jnp.stack([grad_attn_gain, grad_ffn_gain, grad_kv_gain])
    for bit in bit_orders(size)[0]:
        gain_grads = gain_grads + swap(gain_grads, bit, size)
    place = lax.axis_index("dp")
    piece = width // dp_size

    def gain_piece(step):
        return lax.dynamic_slice_in_dim(gain_grads, ((place + step) % dp_size) * piece, piece, 1)

    total = gain_piece(0)
    for step in range(1, dp_size):
        total = total + lax.ppermute(
            gain_piece(step), "dp", [(i, (i + step) % dp_size) for i in range(dp_size)]
        )
    def unit_sums(at):
        early_rows = sum_early[at * early : (at + 1) * early]
        late_rows = sum_late[at * late : at * late + units - early]
        return jnp.concatenate([early_rows, late_rows], axis=0).astype(F32)

    return (
        layer_out,
        input_grad,
        self_grad,
        sum_heads[:wide].T,
        sum_heads[wide : 2 * wide].T,
        sum_heads[2 * wide : 3 * wide].T,
        sum_heads[3 * wide :],
        unit_sums(0).T,
        unit_sums(1).T,
        unit_sums(2),
        total[0],
        total[1],
        total[2],
    )


def solution(mesh):
    placed = (
        P("dp", None),
        P("dp", None),
        P("dp", None),
        P("dp"),
        P("dp", "tensor"),
        P("dp", "tensor"),
        P("dp", "tensor"),
        P("tensor", "dp"),
        P("dp", "tensor"),
        P("dp", "tensor"),
        P("tensor", "dp"),
        P("dp"),
        P("dp"),
        P("dp"),
    )
    return jax.shard_map(
        local,
        mesh=mesh,
        in_specs=placed,
        out_specs=(
            P("dp", None),
            P("dp", None),
            P("dp", None),
            P("dp", "tensor"),
            P("dp", "tensor"),
            P("dp", "tensor"),
            P("tensor", "dp"),
            P("dp", "tensor"),
            P("dp", "tensor"),
            P("tensor", "dp"),
            P("dp"),
            P("dp"),
            P("dp"),
        ),
        check_vma=False,
    )
```

time: 832 us -> 699 us (0.84)
  Pallas kernels: 0 us -> 229 us
  matrix products: 193 us -> 0 us
  waiting for transfers between devices: 334 us -> 258 us
  local copies, waits for them, and re-layouts: 78.6 us -> 28.8 us
  other arithmetic: 128 us -> 94.5 us
    pallas_call x0 -> x27, Pallas kernels: none -> 229 us  [the longest x20 89 us: row_products(): pl.pallas_call(functools.partial(rows_kernel, len(terms)), grid=(columns...]
    dot_general x35 -> x0, matrix products: 193 us -> none  [the longest x7 57.7 us: plain_dot(): return jnp.dot(left, right, preferred_element_type=jnp.float32)]
    ppermute x42, waiting for transfers between devices: 260 us -> 197 us  [swap(): return lax.ppermute(array, 'tensor', [(t, t ^ bit) for t in range(size)])]
    unnamed x151 -> x71, local copies, waits for them, and re-layouts: 35.8 us -> 11.1 us
    convert_element_type x12 -> x33, other arithmetic: 20.5 us -> 38.9 us  [the longest x10 16.6 us: product_scatter(): row_products(terms, 1 + half, 0, half, width).astype(F32)]
    another operation x12 -> x1, other arithmetic: 16.4 us -> 0.59 us  [local(): place = jnp.stack([me, lengths[0]])]
    concatenate x5 -> x4, other arithmetic: 18.2 us -> 5.68 us  [the longest x1 2.26 us: local(): mine = [jnp.concatenate([w_query, w_key, w_value, w_output.T], axis=1)]]
    all_gather x5 -> x3, waiting for transfers between devices: 70.5 us -> 60.4 us  [local(): lax.all_gather(w, 'dp', axis=0, tiled=True)]
  transfers between devices with their start and end apart: 59 -> 55, of which waited for: 28 -> 27; matrix products, arithmetic and copies ran while one was open for 41% -> 15% of each run, Pallas kernels for 0% -> 33%
where the time goes in v2:
time: 699 us; the launch traced here: 693 us
  waiting for transfers between devices  258 us (37%)
  Pallas kernels  229 us (33%)
  other arithmetic  94.5 us (14%)
  starting transfers between devices  52 us (7%)
  local copies, waits for them, and re-layouts  28.8 us (4%)
  between operations  16.4 us (2%)
  blocking collectives  14.6 us (2%)
    ppermute x42, waiting for transfers between devices, swap(): return lax.ppermute(array, 'tensor', [(t, t ^ bit) for t in range(size)])  197 us
    pallas_call x20, Pallas kernels, row_products(): pl.pallas_call(functools.partial(rows_kernel, len(terms)), grid=(columns...  89 us
    all_gather x3, waiting for transfers between devices, local(): lax.all_gather(w, 'dp', axis=0, tiled=True)  60.4 us
    pallas_call x3, Pallas kernels, products(): pl.pallas_call(functools.partial(products_kernel, counts), grid=(total,),...  52.4 us
    ppermute x42, starting transfers between devices, swap(): return lax.ppermute(array, 'tensor', [(t, t ^ bit) for t in range(size)])  44.5 us
    pallas_call x2, Pallas kernels, feed_forward(): pl.pallas_call(feed_kernel, grid=(steps,), in_specs=[whole, whole, pl.Blo...  41.3 us
    pallas_call x1, Pallas kernels, attend_forward(): pl.pallas_call(functools.partial(forward_kernel, size), grid=(groups,), i...  24.8 us
    pallas_call x1, Pallas kernels, attend_backward(): pl.pallas_call(functools.partial(backward_kernel, size), grid=(groups,),...  21.2 us
  transfers between devices with their start and end apart: 55, of which 27 were waited for; matrix products, arithmetic and copies ran while one was open for 15% of the time, Pallas kernels for 33%

profile of v2, /device:TPU:0, one launch (start us, length us, event | category | flops | bytes accessed | tf_op | source)
XLA Modules:
  0.0 692.7 jit_solution(5825640073811246568)
XLA Ops:
  16.5 14.6 %all_gather.12 = bf16[3,2048]{1,0:T(4,128)(2,1)S(1)} all-gather(bf16[3,256]{1,0:T(4,128)(2,1)S(1)} %pad_maximum_fusion.25), channel_id=1, replica_groups=mesh['dp'=8,'tensor'=4] {'dp'}, dimensions={1}, use_global_device_ids=true | all-gather | bytes 13824 | tf_op jit(solution)/shard_map/all_gather | solution.py:518
  43.3 52.3 %all-gather.4.cloned.1.call-done.wq_ref.wk_ref.wv_ref.refs_1_.wo_ref.refs_2_.refs_3_ = bf16[2048,2048]{1,0:T(8,128)(2,1)} async-done(((bf16[256,2048]{1,0:T(8,128)(2,1)}), bf16[2048,2048]{1,0:T(8,128)(2,1)}) %all-gather.4.cloned.1.call-update) | async-done | bytes 8388624 | tf_op jit(solution)/shard_map/all_gather | solution.py:517
  95.6 24.8 %shard_map.237 = (bf16[1024,512]{1,0:T(8,128)(2,1)}, bf16[1024,512]{1,0:T(8,128)(2,1)}, bf16[1024,512]{1,0:T(8,128)(2,1)}, bf16[1024,512]{1,0:T(8,128)(2,1)}, bf16[512,1024]{1,0:T(8,128)(2,1)}) custom-call(s32[2]{0:T(128)} %pad_add_fusion.place_ref, bf16[1024,2048]{1,0:T(8,128)(2,1)} %get-tuple-element.183.normed_ref.refs_4_, ...), custom_call_target="tpu_custom_call" | custom-call | flops 8053063680 | bytes 18874368 | tf_op jit(solution)/shard_map/pallas_call | solution.py:105
  133.8 15.2 %collective-permute-done = bf16[2,256,1024]{2,1,0:T(8,128)(2,1)} collective-permute-done((bf16[2,256,1024]{2,1,0:T(8,128)(2,1)}, bf16[2,256,1024]{2,1,0:T(8,128)(2,1)}, u32[]{:S(2)}, u32[]{:S(2)}) %collective-permute-start) | collective-permute-done | bytes 1048608 | tf_op jit(solution)/shard_map/ppermute | solution.py:404
  182.9 8.2 %collective-permute-done.6 = bf16[1,256,1024]{2,1,0:T(8,128)(2,1)S(1)} collective-permute-done((bf16[1,256,1024]{2,1,0:T(8,128)(2,1)}, bf16[1,256,1024]{2,1,0:T(8,128)(2,1)S(1)}, u32[]{:S(2)}, u32[]{:S(2)}) %collective-permute-start.6) | collective-permute-done | bytes 524320 | tf_op jit(solution)/shard_map/ppermute | solution.py:404
  202.1 12.4 %collective-permute-done.7 = bf16[2,256,1024]{2,1,0:T(8,128)(2,1)S(1)} collective-permute-done((bf16[2,256,1024]{2,1,0:T(8,128)(2,1)S(1)}, bf16[2,256,1024]{2,1,0:T(8,128)(2,1)S(1)}, u32[]{:S(2)}, u32[]{:S(2)}) %collective-permute-start.7) | collective-permute-done | bytes 1048608 | tf_op jit(solution)/shard_map/ppermute | solution.py:404
  222.1 17.7 %shard_map.242 = (bf16[1024,768]{1,0:T(8,128)(2,1)}, bf16[1024,768]{1,0:T(8,128)(2,1)}, bf16[1024,768]{1,0:T(8,128)(2,1)}, bf16[3,768,1024]{2,1,0:T(8,128)(2,1)}) custom-call(bf16[1024,2048]{1,0:T(8,128)(2,1)} %bitcast.254, bf16[1024,2048]{1,0:T(8,128)(2,1)} %bitcast.250, ...), custom_call_target="tpu_custom_call" | custom-call | flops 9663676416 | bytes 27262976 | tf_op jit(solution)/shard_map/pallas_call | solution.py:270
  239.8 17.0 %shard_map.243 = bf16[2304,2048]{1,0:T(8,128)(2,1)} custom-call(bf16[3,768,1024]{2,1,0:T(8,128)(2,1)} %get-tuple-element.45.refs_0_.refs_1_.refs_2_, bf16[3,768,1024]{2,1,0:T(8,128)(2,1)} %get-tuple-element.45.refs_0_.refs_1_.refs_2_, bf16[3,768,1024]{2,1,0:T(8,128)(2,1)} %get-tuple-element.45.refs_0_.refs_1_.refs_2_, bf16[1024,2048]{1,0:T(8,128)(2,1)} %bitcast.255, ...), custom_call_target="tpu_custom_call" | custom-call | flops 9663676416 | bytes 22544384 | tf_op jit(solution)/shard_map/pallas_call | solution.py:319
  256.9 8.1 %all-gather.8.cloned.1.call-done.wg_ref.wu_ref.wd_ref.refs_3_.refs_6_.refs_7_ = bf16[2048,1920]{1,0:T(8,128)(2,1)} async-done(((bf16[256,1920]{1,0:T(8,128)(2,1)}), bf16[2048,1920]{1,0:T(8,128)(2,1)}) %all-gather.8.cloned.1.call-update) | async-done | bytes 7864336 | tf_op jit(solution)/shard_map/all_gather | solution.py:517
  265.0 23.5 %shard_map.244 = (bf16[1024,640]{1,0:T(8,128)(2,1)}, bf16[1024,640]{1,0:T(8,128)(2,1)}, bf16[1024,640]{1,0:T(8,128)(2,1)}, bf16[3,640,1024]{2,1,0:T(8,128)(2,1)}) custom-call(bf16[1024,2048]{1,0:T(8,128)(2,1)} %bitcast.256, bf16[1024,2048]{1,0:T(8,128)(2,1)} %bitcast.252, ...), custom_call_target="tpu_custom_call" | custom-call | flops 8053063680 | bytes 24117248 | tf_op jit(solution)/shard_map/pallas_call | solution.py:270
  288.5 18.4 %shard_map.263 = bf16[1920,2048]{1,0:T(8,128)(2,1)} custom-call(bf16[3,640,1024]{2,1,0:T(8,128)(2,1)} %get-tuple-element.70.refs_0_.refs_1_.refs_2_, bf16[3,640,1024]{2,1,0:T(8,128)(2,1)} %get-tuple-element.70.refs_0_.refs_1_.refs_2_, bf16[3,640,1024]{2,1,0:T(8,128)(2,1)} %get-tuple-element.70.refs_0_.refs_1_.refs_2_, bf16[1024,2048]{1,0:T(8,128)(2,1)} %bitcast.257, ...), custom_call_target="tpu_custom_call" | custom-call | flops 8053063680 | bytes 20185088 | tf_op jit(solution)/shard_map/pallas_call | solution.py:319
  307.0 7.4 %shard_map.249 = bf16[2,256,1024]{2,1,0:T(8,128)(2,1)} custom-call(bf16[2,2,256,768]{3,2,1,0:T(8,128)(2,1)} %bitcast.258, bf16[2,2,256,768]{3,2,1,0:T(8,128)(2,1)} %bitcast.262, bf16[2,2,256,640]{3,2,1,0:T(8,128)(2,1)} %bitcast.270, bf16[2,2,256,640]{3,2,1,0:T(8,128)(2,1)} %bitcast.274, ...), custom_call_target="tpu_custom_call" | custom-call | flops 2952790016 | bytes 9699328 | tf_op jit(solution)/shard_map/pallas_call | solution.py:364
  315.9 7.5 %shard_map.250 = bf16[2,256,1024]{2,1,0:T(8,128)(2,1)} custom-call(bf16[2,2,256,768]{3,2,1,0:T(8,128)(2,1)} %bitcast.259, bf16[2,2,256,768]{3,2,1,0:T(8,128)(2,1)} %bitcast.263, bf16[2,2,256,640]{3,2,1,0:T(8,128)(2,1)} %bitcast.271, bf16[2,2,256,640]{3,2,1,0:T(8,128)(2,1)} %bitcast.275, ...), custom_call_target="tpu_custom_call" | custom-call | flops 2952790016 | bytes 9699328 | tf_op jit(solution)/shard_map/pallas_call | solution.py:364
  335.3 7.5 %shard_map.252 = bf16[2,256,1024]{2,1,0:T(8,128)(2,1)} custom-call(bf16[2,2,256,768]{3,2,1,0:T(8,128)(2,1)} %bitcast.260, bf16[2,2,256,768]{3,2,1,0:T(8,128)(2,1)} %bitcast.264, bf16[2,2,256,640]{3,2,1,0:T(8,128)(2,1)} %bitcast.272, bf16[2,2,256,640]{3,2,1,0:T(8,128)(2,1)} %bitcast.276, ...), custom_call_target="tpu_custom_call" | custom-call | flops 2952790016 | bytes 9699328 | tf_op jit(solution)/shard_map/pallas_call | solution.py:364
  342.7 7.3 %shard_map.251 = bf16[2,256,1024]{2,1,0:T(8,128)(2,1)} custom-call(bf16[2,2,256,768]{3,2,1,0:T(8,128)(2,1)} %bitcast.261, bf16[2,2,256,768]{3,2,1,0:T(8,128)(2,1)} %bitcast.265, bf16[2,2,256,640]{3,2,1,0:T(8,128)(2,1)} %bitcast.273, bf16[2,2,256,640]{3,2,1,0:T(8,128)(2,1)} %bitcast.277, ...), custom_call_target="tpu_custom_call" | custom-call | flops 2952790016 | bytes 9699328 | tf_op jit(solution)/shard_map/pallas_call | solution.py:364
  401.4 9.5 %collective-permute-done.22 = bf16[1,256,1024]{2,1,0:T(8,128)(2,1)S(1)} collective-permute-done((bf16[1,256,1024]{2,1,0:T(8,128)(2,1)S(1)}, bf16[1,256,1024]{2,1,0:T(8,128)(2,1)S(1)}, u32[]{:S(2)}, u32[]{:S(2)}) %collective-permute-start.22) | collective-permute-done | bytes 524320 | tf_op jit(solution)/shard_map/ppermute | solution.py:404
  416.2 11.2 %collective-permute-done.14 = bf16[1,256,1024]{2,1,0:T(8,128)(2,1)S(1)} collective-permute-done((bf16[1,256,1024]{2,1,0:T(8,128)(2,1)S(1)}, bf16[1,256,1024]{2,1,0:T(8,128)(2,1)S(1)}, u32[]{:S(2)}, u32[]{:S(2)}) %collective-permute-start.14) | collective-permute-done | bytes 524320 | tf_op jit(solution)/shard_map/ppermute | solution.py:404
  429.2 8.0 %collective-permute-done.23 = bf16[2,256,1024]{2,1,0:T(8,128)(2,1)S(1)} collective-permute-done((bf16[2,256,1024]{2,1,0:T(8,128)(2,1)S(1)}, bf16[2,256,1024]{2,1,0:T(8,128)(2,1)S(1)}, u32[]{:S(2)}, u32[]{:S(2)}) %collective-permute-start.23) | collective-permute-done | bytes 1048608 | tf_op jit(solution)/shard_map/ppermute | solution.py:404
  437.3 8.9 %collective-permute-done.21 = bf16[2,256,1024]{2,1,0:T(8,128)(2,1)S(1)} collective-permute-done((bf16[2,256,1024]{2,1,0:T(8,128)(2,1)S(1)}, bf16[2,256,1024]{2,1,0:T(8,128)(2,1)S(1)}, u32[]{:S(2)}, u32[]{:S(2)}) %collective-permute-start.21) | collective-permute-done | bytes 1048608 | tf_op jit(solution)/shard_map/ppermute | solution.py:404
  448.7 21.2 %shard_map.253 = (bf16[1024,512]{1,0:T(8,128)(2,1)}, bf16[1024,512]{1,0:T(8,128)(2,1)}, bf16[1024,512]{1,0:T(8,128)(2,1)}, bf16[3,512,1024]{2,1,0:T(8,128)(2,1)}) custom-call(s32[2]{0:T(128)} %pad_add_fusion.place_ref, bf16[1024,2048]{1,0:T(8,128)(2,1)} %bitcast.302, ...), custom_call_target="tpu_custom_call" | custom-call | flops 7516192768 | bytes 15728640 | tf_op jit(solution)/shard_map/pallas_call | solution.py:216
  469.9 17.1 %shard_map.262 = bf16[2048,2048]{1,0:T(8,128)(2,1)} custom-call(bf16[3,512,1024]{2,1,0:T(8,128)(2,1)} %get-tuple-element.67.refs_0_.refs_1_.refs_2_, bf16[3,512,1024]{2,1,0:T(8,128)(2,1)} %get-tuple-element.67.refs_0_.refs_1_.refs_2_, bf16[3,512,1024]{2,1,0:T(8,128)(2,1)} %get-tuple-element.67.refs_0_.refs_1_.refs_2_, bf16[1,512,1024]{2,1,0:T(8,128)(2,1)} %bitcast.343, ...), custom_call_target="tpu_custom_call" | custom-call | flops 8589934592 | bytes 25165824 | tf_op jit(solution)/shard_map/pallas_call | solution.py:319
  547.7 11.7 %collective-permute-done.24 = bf16[2,256,1024]{2,1,0:T(8,128)(2,1)} collective-permute-done((bf16[2,256,1024]{2,1,0:T(8,128)(2,1)}, bf16[2,256,1024]{2,1,0:T(8,128)(2,1)}, u32[]{:S(2)}, u32[]{:S(2)}) %collective-permute-start.24) | collective-permute-done | bytes 1048608 | tf_op jit(solution)/shard_map/ppermute | solution.py:404
  614.9 23.8 %collective-permute-done.28 = bf16[1,256,1024]{2,1,0:T(8,128)(2,1)S(1)} collective-permute-done((bf16[1,256,1024]{2,1,0:T(8,128)(2,1)S(1)}, bf16[1,256,1024]{2,1,0:T(8,128)(2,1)S(1)}, u32[]{:S(2)}, u32[]{:S(2)}) %collective-permute-start.28) | collective-permute-done | bytes 524320 | tf_op jit(solution)/shard_map/ppermute | solution.py:404
  641.1 20.1 %collective-permute-done.31 = bf16[2,256,1024]{2,1,0:T(8,128)(2,1)S(1)} collective-permute-done((bf16[2,256,1024]{2,1,0:T(8,128)(2,1)S(1)}, bf16[2,256,1024]{2,1,0:T(8,128)(2,1)S(1)}, u32[]{:S(2)}, u32[]{:S(2)}) %collective-permute-start.31) | collective-permute-done | bytes 1048608 | tf_op jit(solution)/shard_map/ppermute | solution.py:404
  (344 shorter events, 303.0 us)
Async XLA Ops:
  7.2 88.4 %all-gather.4.cloned.1.call-start = ((), (), s32[]{:S(2)}) async-start(), calls=%async_computation.3 | async-start | bytes 9437184 | tf_op jit(solution)/shard_map/all_gather | solution.py:517
  10.6 211.5 %all-gather.6.cloned.1.call-start = ((), (), s32[]{:S(2)}) async-start(), calls=%async_computation.4 | async-start | bytes 10616832 | tf_op jit(solution)/shard_map/all_gather | solution.py:517
  13.3 251.7 %all-gather.8.cloned.1.call-start = ((), (), s32[]{:S(2)}) async-start(), calls=%async_computation.5 | async-start | bytes 8847360 | tf_op jit(solution)/shard_map/all_gather | solution.py:517
  15.7 454.2 %reduce-scatter.4.cloned.1.call-start = ((), (), s32[]{:S(2)}) async-start(), calls=%async_computation.6 | async-start | bytes 10616832 | tf_op jit(solution)/shard_map/reduce_scatter | solution.py:555
  127.9 31.1 %collective-permute-start.2 = (bf16[2,256,1024]{2,1,0:T(8,128)(2,1)}, bf16[2,256,1024]{2,1,0:T(8,128)(2,1)S(1)}, u32[]{:S(2)}, u32[]{:S(2)}) collective-permute-start(bf16[2,256,1024]{2,1,0:T(8,128)(2,1)} %shard_map.239), channel_id=1, source_target_pairs={{0,2},{1,3},{2,0},{3,1},{4,6},{5,7},{6,4},{7,5},{8,10},{9,11},{10,... | collective-permute-start | bytes 3145736 | tf_op jit(solution)/shard_map/ppermute | solution.py:404
  256.8 418.0 %reduce-scatter.8.cloned.1.call-start = ((), (), s32[]{:S(2)}) async-start(), calls=%async_computation.8 | async-start | bytes 8847360 | tf_op jit(solution)/shard_map/reduce_scatter | solution.py:570
  306.9 373.1 %reduce-scatter.6.cloned.1.call-start = ((), (), s32[]{:S(2)}) async-start(), calls=%async_computation.7 | async-start | bytes 9437184 | tf_op jit(solution)/shard_map/reduce_scatter | solution.py:588
  314.4 51.5 %collective-permute-start.16 = (bf16[2,256,1024]{2,1,0:T(8,128)(2,1)}, bf16[2,256,1024]{2,1,0:T(8,128)(2,1)}, u32[]{:S(2)}, u32[]{:S(2)}) collective-permute-start(bf16[2,256,1024]{2,1,0:T(8,128)(2,1)} %shard_map.249), channel_id=1, source_target_pairs={{0,1},{1,0},{2,3},{3,2},{4,5},{5,4},{6,7},{7,6},{8,9},{9,8},{10,11... | collective-permute-start | bytes 3145736 | tf_op jit(solution)/shard_map/ppermute | solution.py:404
  323.4 46.1 %collective-permute-start.18 = (bf16[2,256,1024]{2,1,0:T(8,128)(2,1)}, bf16[2,256,1024]{2,1,0:T(8,128)(2,1)}, u32[]{:S(2)}, u32[]{:S(2)}) collective-permute-start(bf16[2,256,1024]{2,1,0:T(8,128)(2,1)} %shard_map.250), channel_id=1, source_target_pairs={{0,2},{1,3},{2,0},{3,1},{4,6},{5,7},{6,4},{7,5},{8,10},{9,11},{10,... | collective-permute-start | bytes 3145736 | tf_op jit(solution)/shard_map/ppermute | solution.py:404
  329.5 43.2 %collective-permute-start.8 = (bf16[2,256,1024]{2,1,0:T(8,128)(2,1)}, bf16[2,256,1024]{2,1,0:T(8,128)(2,1)}, u32[]{:S(2)}, u32[]{:S(2)}) collective-permute-start(bf16[2,256,1024]{2,1,0:T(8,128)(2,1)} %shard_map.245), channel_id=1, source_target_pairs={{0,1},{1,0},{2,3},{3,2},{4,5},{5,4},{6,7},{7,6},{8,9},{9,8},{10,11... | collective-permute-start | bytes 3145736 | tf_op jit(solution)/shard_map/ppermute | solution.py:404
  334.7 40.5 %collective-permute-start.10 = (bf16[2,256,1024]{2,1,0:T(8,128)(2,1)}, bf16[2,256,1024]{2,1,0:T(8,128)(2,1)}, u32[]{:S(2)}, u32[]{:S(2)}) collective-permute-start(bf16[2,256,1024]{2,1,0:T(8,128)(2,1)} %shard_map.246), channel_id=1, source_target_pairs={{0,2},{1,3},{2,0},{3,1},{4,6},{5,7},{6,4},{7,5},{8,10},{9,11},{10,... | collective-permute-start | bytes 3145736 | tf_op jit(solution)/shard_map/ppermute | solution.py:404
  411.0 26.2 %collective-permute-start.23 = (bf16[2,256,1024]{2,1,0:T(8,128)(2,1)S(1)}, bf16[2,256,1024]{2,1,0:T(8,128)(2,1)S(1)}, u32[]{:S(2)}, u32[]{:S(2)}) collective-permute-start(bf16[2,256,1024]{2,1,0:T(8,128)(2,1)S(1)} %pad_maximum_fusion.17), channel_id=1, source_target_pairs={{0,2},{1,3},{2,0},{3,1},{4,6},{5,7},{6,4},{7,5},{8,10},{9,11},{10,... | collective-permute-start | bytes 3145736 | tf_op jit(solution)/shard_map/ppermute | solution.py:404
  413.8 32.3 %collective-permute-start.21 = (bf16[2,256,1024]{2,1,0:T(8,128)(2,1)S(1)}, bf16[2,256,1024]{2,1,0:T(8,128)(2,1)S(1)}, u32[]{:S(2)}, u32[]{:S(2)}) collective-permute-start(bf16[2,256,1024]{2,1,0:T(8,128)(2,1)S(1)} %pad_maximum_fusion.16), channel_id=1, source_target_pairs={{0,1},{1,0},{2,3},{3,2},{4,5},{5,4},{6,7},{7,6},{8,9},{9,8},{10,11... | collective-permute-start | bytes 3145736 | tf_op jit(solution)/shard_map/ppermute | solution.py:404
  415.5 71.5 %collective-permute-start.12 = (bf16[1,256,1024]{2,1,0:T(8,128)(2,1)S(1)}, bf16[1,256,1024]{2,1,0:T(8,128)(2,1)S(1)}, u32[]{:S(2)}, u32[]{:S(2)}) collective-permute-start(bf16[1,256,1024]{2,1,0:T(8,128)(2,1)S(1)} %get-tuple-element.152), channel_id=1, source_target_pairs={{0,2},{1,3},{2,0},{3,1},{4,6},{5,7},{6,4},{7,5},{8,10},{9,11},{10,... | collective-permute-start | bytes 1572872 | tf_op jit(solution)/shard_map/ppermute | solution.py:404
  428.4 78.2 %collective-permute-start.15 = (bf16[2,256,1024]{2,1,0:T(8,128)(2,1)}, bf16[2,256,1024]{2,1,0:T(8,128)(2,1)}, u32[]{:S(2)}, u32[]{:S(2)}) collective-permute-start(bf16[2,256,1024]{2,1,0:T(8,128)(2,1)} %pad_maximum_fusion.15), channel_id=1, source_target_pairs={{0,2},{1,3},{2,0},{3,1},{4,6},{5,7},{6,4},{7,5},{8,10},{9,11},{10,... | collective-permute-start | bytes 3145736 | tf_op jit(solution)/shard_map/ppermute | solution.py:404
  488.1 26.4 %collective-permute-start.13 = (bf16[2,256,1024]{2,1,0:T(8,128)(2,1)}, bf16[2,256,1024]{2,1,0:T(8,128)(2,1)}, u32[]{:S(2)}, u32[]{:S(2)}) collective-permute-start(bf16[2,256,1024]{2,1,0:T(8,128)(2,1)} %pad_maximum_fusion.14), channel_id=1, source_target_pairs={{0,1},{1,0},{2,3},{3,2},{4,5},{5,4},{6,7},{7,6},{8,9},{9,8},{10,11... | collective-permute-start | bytes 3145736 | tf_op jit(solution)/shard_map/ppermute | solution.py:404
  494.2 48.0 %collective-permute-start.32 = (bf16[2,256,1024]{2,1,0:T(8,128)(2,1)}, bf16[2,256,1024]{2,1,0:T(8,128)(2,1)}, u32[]{:S(2)}, u32[]{:S(2)}) collective-permute-start(bf16[2,256,1024]{2,1,0:T(8,128)(2,1)} %shard_map.258), channel_id=1, source_target_pairs={{0,1},{1,0},{2,3},{3,2},{4,5},{5,4},{6,7},{7,6},{8,9},{9,8},{10,11... | collective-permute-start | bytes 3145736 | tf_op jit(solution)/shard_map/ppermute | solution.py:404
  499.0 45.6 %collective-permute-start.34 = (bf16[2,256,1024]{2,1,0:T(8,128)(2,1)}, bf16[2,256,1024]{2,1,0:T(8,128)(2,1)}, u32[]{:S(2)}, u32[]{:S(2)}) collective-permute-start(bf16[2,256,1024]{2,1,0:T(8,128)(2,1)} %shard_map.259), channel_id=1, source_target_pairs={{0,2},{1,3},{2,0},{3,1},{4,6},{5,7},{6,4},{7,5},{8,10},{9,11},{10,... | collective-permute-start | bytes 3145736 | tf_op jit(solution)/shard_map/ppermute | solution.py:404
  502.2 57.2 %collective-permute-start.24 = (bf16[2,256,1024]{2,1,0:T(8,128)(2,1)}, bf16[2,256,1024]{2,1,0:T(8,128)(2,1)}, u32[]{:S(2)}, u32[]{:S(2)}) collective-permute-start(bf16[2,256,1024]{2,1,0:T(8,128)(2,1)} %shard_map.254), channel_id=1, source_target_pairs={{0,1},{1,0},{2,3},{3,2},{4,5},{5,4},{6,7},{7,6},{8,9},{9,8},{10,11... | collective-permute-start | bytes 3145736 | tf_op jit(solution)/shard_map/ppermute | solution.py:404
  506.7 54.8 %collective-permute-start.26 = (bf16[2,256,1024]{2,1,0:T(8,128)(2,1)}, bf16[2,256,1024]{2,1,0:T(8,128)(2,1)S(1)}, u32[]{:S(2)}, u32[]{:S(2)}) collective-permute-start(bf16[2,256,1024]{2,1,0:T(8,128)(2,1)} %shard_map.255), channel_id=1, source_target_pairs={{0,2},{1,3},{2,0},{3,1},{4,6},{5,7},{6,4},{7,5},{8,10},{9,11},{10,... | collective-permute-start | bytes 3145736 | tf_op jit(solution)/shard_map/ppermute | solution.py:404
  601.6 39.1 %collective-permute-start.39 = (bf16[2,256,1024]{2,1,0:T(8,128)(2,1)S(1)}, bf16[2,256,1024]{2,1,0:T(8,128)(2,1)S(1)}, u32[]{:S(2)}, u32[]{:S(2)}) collective-permute-start(bf16[2,256,1024]{2,1,0:T(8,128)(2,1)S(1)} %pad_maximum_fusion.21), channel_id=1, source_target_pairs={{0,2},{1,3},{2,0},{3,1},{4,6},{5,7},{6,4},{7,5},{8,10},{9,11},{10,... | collective-permute-start | bytes 3145736 | tf_op jit(solution)/shard_map/ppermute | solution.py:404
  602.1 38.7 %collective-permute-start.37 = (bf16[2,256,1024]{2,1,0:T(8,128)(2,1)S(1)}, bf16[2,256,1024]{2,1,0:T(8,128)(2,1)S(1)}, u32[]{:S(2)}, u32[]{:S(2)}) collective-permute-start(bf16[2,256,1024]{2,1,0:T(8,128)(2,1)S(1)} %pad_maximum_fusion.20), channel_id=1, source_target_pairs={{0,1},{1,0},{2,3},{3,2},{4,5},{5,4},{6,7},{7,6},{8,9},{9,8},{10,11... | collective-permute-start | bytes 3145736 | tf_op jit(solution)/shard_map/ppermute | solution.py:404
  605.9 32.8 %collective-permute-start.28 = (bf16[1,256,1024]{2,1,0:T(8,128)(2,1)S(1)}, bf16[1,256,1024]{2,1,0:T(8,128)(2,1)S(1)}, u32[]{:S(2)}, u32[]{:S(2)}) collective-permute-start(bf16[1,256,1024]{2,1,0:T(8,128)(2,1)S(1)} %get-tuple-element.140), channel_id=1, source_target_pairs={{0,2},{1,3},{2,0},{3,1},{4,6},{5,7},{6,4},{7,5},{8,10},{9,11},{10,... | collective-permute-start | bytes 1572872 | tf_op jit(solution)/shard_map/ppermute | solution.py:404
  614.8 46.3 %collective-permute-start.31 = (bf16[2,256,1024]{2,1,0:T(8,128)(2,1)S(1)}, bf16[2,256,1024]{2,1,0:T(8,128)(2,1)S(1)}, u32[]{:S(2)}, u32[]{:S(2)}) collective-permute-start(bf16[2,256,1024]{2,1,0:T(8,128)(2,1)S(1)} %pad_maximum_fusion.19), channel_id=1, source_target_pairs={{0,2},{1,3},{2,0},{3,1},{4,6},{5,7},{6,4},{7,5},{8,10},{9,11},{10,... | collective-permute-start | bytes 3145736 | tf_op jit(solution)/shard_map/ppermute | solution.py:404
  (66 other events, 550.0 us)
Sparse Core Ops, SparseCore 0:
  10.7 84.8 all-gather.3
  97.8 89.2 all-gather.5
  188.8 76.1 all-gather.7
  267.1 98.0 reduce-scatter.3
  367.4 82.9 reduce-scatter.7
  487.1 86.9 reduce-scatter.5

commit v3 on v2

--- a/solution.py
+++ b/solution.py
@@ -13,6 +13,7 @@
 F32 = jnp.float32
 epsilon = 1e-06
 VMEM_LIMIT = 60 * 1024 * 1024
+WEIGHT = 1
 
 
 def plain_dot(left, right):
@@ -35,6 +36,14 @@
 
 def limits():
     return pltpu.CompilerParams(vmem_limit_bytes=VMEM_LIMIT)
+
+
+def estimate(flops, bytes_accessed, transcendentals):
+    return pl.CostEstimate(
+        flops=flops // WEIGHT,
+        bytes_accessed=bytes_accessed // WEIGHT,
+        transcendentals=transcendentals // WEIGHT,
+    )
 
 
 def turn(values, cosine, sine):
@@ -118,7 +127,7 @@
         out_specs=[heads] * 4 + [pl.BlockSpec((group, length), lambda g: (g, 0))],
         out_shape=[out] * 4 + [jax.ShapeDtypeStruct((wide, length), BF)],
         compiler_params=limits(),
-        cost_estimate=pl.CostEstimate(
+        cost_estimate=estimate(
             flops=6 * length * width * wide + 3 * length * length * wide,
             bytes_accessed=4 * length * width + 6 * width * wide + 8 * length * wide,
             transcendentals=length * length * wide // HD,
@@ -136,7 +145,7 @@
     v_ref,
     cos_ref,
     sin_ref,
-    rq_ref,
+    gq_ref,
     rk_ref,
     rv_ref,
     flip_ref,
@@ -160,7 +169,6 @@
         ga_ref[pl.ds(home(block * part), part), :] = plain_dot(
             grad_ref[block * part : (block + 1) * part, :], wo_ref[...]
         ).astype(BF)
-    step = min(part, QROWS)
     for at in range(0, group, HD):
         kt_ref[...] = k_ref[:, at : at + HD].T
         for start in reversed(range(0, length, QROWS)):
@@ -189,11 +197,7 @@
             grad_q = plain_dot(kt_ref[:, :stop], grad_scores).T * scale
             grad_q = turn(grad_q, cosine[start:stop], sine[start:stop])
             flip_ref[0, at : at + HD, start:stop] = grad_q.T.astype(BF)
-            grad_q = grad_q.astype(BF)
-            for piece in range(0, QROWS, step):
-                rq_ref[pl.ds(home(start + piece), step), at : at + HD] = grad_q[
-                    piece : piece + step
-                ]
+            gq_ref[start:stop, at : at + HD] = grad_q.astype(BF)
         grad_k = turn(sum_k[...] * scale, cosine, sine)
         grad_v = sum_v[...]
         flip_ref[1, at : at + HD, :] = grad_k.T.astype(BF)
@@ -205,29 +209,30 @@
             rv_ref[pl.ds(home(block * part), part), at : at + HD] = grad_v[rows]
 
 
-def attend_backward(place, grad_mid_low, weights, queries, keys, values, cosine, sine, size):
+def attend_backward(place, grad_mid_low, weights, queries, keys, values, cosine, sine, size, at):
     length, width = grad_mid_low.shape
     wide = queries.shape[1]
     group = head_group(wide)
     groups = wide // group
     table = pl.BlockSpec((length, HD), lambda g: (0, 0))
-    heads = pl.BlockSpec((length, group), lambda g: (0, g))
-    out = jax.ShapeDtypeStruct((length, wide), BF)
+    heads = pl.BlockSpec((length, group), lambda g: (0, at))
+    outs = pl.BlockSpec((length, group), lambda g: (0, 0))
+    out = jax.ShapeDtypeStruct((length, group), BF)
     return pl.pallas_call(
         functools.partial(backward_kernel, size),
-        grid=(groups,),
+        grid=(1,),
         in_specs=[
             pl.BlockSpec(memory_space=pltpu.SMEM),
             pl.BlockSpec((length, width), lambda g: (0, 0)),
-            pl.BlockSpec((width, group), lambda g: (0, g + 3 * groups)),
+            pl.BlockSpec((width, group), lambda g: (0, at + 3 * groups)),
             heads,
             heads,
             heads,
             table,
             table,
         ],
-        out_specs=[heads] * 3 + [pl.BlockSpec((3, group, length), lambda g: (0, g, 0))],
-        out_shape=[out] * 3 + [jax.ShapeDtypeStruct((3, wide, length), BF)],
+        out_specs=[outs] * 3 + [pl.BlockSpec((3, group, length), lambda g: (0, 0, 0))],
+        out_shape=[out] * 3 + [jax.ShapeDtypeStruct((3, group, length), BF)],
         scratch_shapes=[
             pltpu.VMEM((length, group), BF),
             pltpu.VMEM((HD, length), BF),
@@ -235,10 +240,10 @@
             pltpu.VMEM((length, HD), F32),
         ],
         compiler_params=limits(),
-        cost_estimate=pl.CostEstimate(
-            flops=2 * length * width * wide + 10 * length * length * wide,
-            bytes_accessed=2 * length * width + 2 * width * wide + 18 * length * wide,
-            transcendentals=length * length * wide // HD,
+        cost_estimate=estimate(
+            flops=2 * length * width * group + 10 * length * length * group,
+            bytes_accessed=2 * length * width + 2 * width * group + 18 * length * group,
+            transcendentals=length * length * group // HD,
         ),
     )(place, grad_mid_low, weights, queries, keys, values, cosine, sine)
 
@@ -263,7 +268,7 @@
 def feed_forward(ffn_in, grad_low, weights):
     length, width = ffn_in.shape
     units = weights.shape[1] // 3
-    step = 256 if units % 256 == 0 else 128
+    step = 256 if units % 256 == 0 else units if units <= 512 else 128
     steps = units // step
     whole = pl.BlockSpec((length, width), lambda f: (0, 0))
     out = pl.BlockSpec((length, step), lambda f: (0, f))
@@ -281,7 +286,7 @@
         out_shape=[jax.ShapeDtypeStruct((length, units), BF)] * 3
         + [jax.ShapeDtypeStruct((3, units, length), BF)],
         compiler_params=limits(),
-        cost_estimate=pl.CostEstimate(
+        cost_estimate=estimate(
             flops=6 * length * width * units,
             bytes_accessed=4 * length * width + 6 * width * units + 12 * length * units,
             transcendentals=2 * length * units,
@@ -323,7 +328,7 @@
         out_specs=pl.BlockSpec((step, width), lambda i: (i, 0)),
         out_shape=jax.ShapeDtypeStruct((total * step, width), BF),
         compiler_params=limits(),
-        cost_estimate=pl.CostEstimate(
+        cost_estimate=estimate(
             flops=2 * total * step * length * width,
             bytes_accessed=2 * (total * step * (length + width) + len(rights) * length * width),
             transcendentals=0,
@@ -331,45 +336,47 @@
     )(*[left for left, _, _ in terms], *rights)
 
 
-def rows_kernel(count, *refs):
-    out_ref = refs[-1]
-    total = None
-    for left, right in zip(refs[:count], refs[count:-1]):
-        rows = left[...].reshape(-1, left.shape[-1])
-        part = last_dims(rows, right[...])
-        total = part if total is None else total + part
-    out_ref[...] = total.astype(BF).reshape(out_ref.shape)
-
-
-def row_products(terms, bit, side, half, width):
+def rows_kernel(count, side, steps, *refs):
+    lefts, rights, outs = refs[:count], refs[count:-2], refs[-2:]
+    for half in range(2):
+
+        @pl.when(pl.program_id(0) // steps == half)
+        def _(half=half):
+            for piece in range(2):
+                row = 2 * piece + side if half == 0 else 2 * side + piece
+                total = None
+                for left, right in zip(lefts, rights):
+                    part = last_dims(left[row], right[...])
+                    total = part if total is None else total + part
+                outs[half][piece] = total.astype(BF)
+
+
+def row_products(terms, side, width):
     columns = width // 2
     step = 512 if columns % 512 == 0 else columns
+    steps = columns // step
     left_specs, right_specs, lefts, rights = [], [], [], []
     flops = nbytes = 0
     for left, right, at in terms:
         rows, depth = left.shape[0] // 4, left.shape[1]
-        lefts.append(left.reshape(2, 2, rows, depth))
-        if bit == 1:
-            left_specs.append(pl.BlockSpec((2, 1, rows, depth), lambda j: (0, side, 0, 0)))
-        else:
-            left_specs.append(pl.BlockSpec((1, 2, rows, depth), lambda j: (side, 0, 0, 0)))
-        right_specs.append(
-            pl.BlockSpec(
-                (step, depth), lambda j, at=at: (half * (columns // step) + j, at)
-            )
-        )
+        lefts.append(left.reshape(4, rows, depth))
+        left_specs.append(pl.BlockSpec((4, rows, depth), lambda j: (0, 0, 0)))
+        right_specs.append(pl.BlockSpec((step, depth), lambda j, at=at: (j, at)))
         rights.append(right)
-        flops += 4 * rows * depth * columns
-        nbytes += 2 * depth * (2 * rows + columns)
+        flops += 8 * rows * depth * columns
+        nbytes += 4 * depth * (2 * rows + columns)
     return pl.pallas_call(
-        functools.partial(rows_kernel, len(terms)),
-        grid=(columns // step,),
+        functools.partial(rows_kernel, len(terms), side, steps),
+        grid=(2 * steps,),
         in_specs=left_specs + right_specs,
-        out_specs=pl.BlockSpec((2, rows, step), lambda j: (0, 0, j)),
-        out_shape=jax.ShapeDtypeStruct((2, rows, columns), BF),
+        out_specs=[
+            pl.BlockSpec((2, rows, step), lambda j: (0, 0, lax.min(j, steps - 1))),
+            pl.BlockSpec((2, rows, step), lambda j: (0, 0, lax.max(j - steps, 0))),
+        ],
+        out_shape=[jax.ShapeDtypeStruct((2, rows, columns), BF)] * 2,
         compiler_params=limits(),
-        cost_estimate=pl.CostEstimate(
-            flops=flops, bytes_accessed=nbytes + 4 * rows * columns, transcendentals=0
+        cost_estimate=estimate(
+            flops=flops, bytes_accessed=nbytes + 8 * rows * columns, transcendentals=0
         ),
     )(*lefts, *rights)
 
@@ -382,10 +389,7 @@
 def norm_back(grad, values, inverse, gain):
     scaled = grad * gain
     inner = jnp.mean(scaled * values, axis=-1, keepdims=True)
-    return (
-        inverse * scaled - values * inverse**3 * inner,
-        jnp.sum(grad * values * inverse, axis=0),
-    )
+    return inverse * scaled - values * inverse**3 * inner
 
 
 def rotary_tables(length):
@@ -444,39 +448,107 @@
     return jnp.concatenate(sums, axis=1)
 
 
-def gather_rows(own, size):
+def gather_part(own, size, group, earlier=()):
+    held, came = {0: own}, []
+    for bit in bit_orders(size)[group][::-1]:
+        places = list(held)
+        sent = jnp.stack([held[place] for place in places])
+        came.append(swap(after(sent, *earlier) if came else sent, bit, size))
+        for at, place in enumerate(places):
+            held[place ^ bit] = came[-1][at]
+    return [held[place] for place in range(size)], came[0], came[-1]
+
+
+def gather_rows(own, size, earlier=()):
     half = own.shape[1] // 2
-    parts = []
-    for group, order in enumerate(bit_orders(size)):
-        held = {0: own[:, group * half : (group + 1) * half]}
-        for bit in order[::-1]:
-            places = list(held)
-            got = swap(jnp.stack([held[place] for place in places]), bit, size)
-            for at, place in enumerate(places):
-                held[place ^ bit] = got[at]
-        parts.append(held)
-    return jnp.stack(
-        [jnp.concatenate([held[place] for held in parts], axis=1) for place in range(size)]
-    )
-
-
-def product_scatter(terms, size, width):
+    low, low_first, low_last = gather_part(own[:, :half], size, 0, earlier)
+    high, high_first, high_last = gather_part(own[:, half:], size, 1, earlier)
+    rows = jnp.stack([jnp.concatenate(pair, axis=1) for pair in zip(low, high)])
+    return rows, [low_first, high_first], [low_last, high_last]
+
+
+def product_scatter(terms, size, width, earlier=(), free=()):
     if size != 4:
         total = 0.0
         for left, right, at in terms:
             depth = left.shape[1]
             total = total + last_dims(left, right[:, at * depth : (at + 1) * depth])
-        return scatter_sum(total.reshape(size, -1, width))
-    sent = [row_products(terms, 1 + half, 1, half, width) for half in range(2)]
-    got = [swap(sent[half], 1 + half, size).astype(F32) for half in range(2)]
-    lefts = after([left for left, _, _ in terms], *sent)
+        return scatter_sum(total.reshape(size, -1, width)), [total], [total], total
+    sent = row_products(terms, 1, width)
+    first = [swap(after(sent[half], *free), 1 + half, size) for half in range(2)]
+    lefts = after([left for left, _, _ in terms], *sent, *earlier)
     terms = [(left, right, at) for left, (_, right, at) in zip(lefts, terms)]
-    kept = [row_products(terms, 1 + half, 0, half, width).astype(F32) for half in range(2)]
-    more = [
-        swap((kept[half][1] + got[half][1]).astype(BF), 2 - half, size).astype(F32)
-        for half in range(2)
-    ]
-    return jnp.concatenate([kept[half][0] + got[half][0] + more[half] for half in range(2)], axis=1)
+    kept = row_products(terms, 0, width)
+    held = [kept[half].astype(F32) + first[half].astype(F32) for half in range(2)]
+    last = [swap(held[half][1].astype(BF), 2 - half, size) for half in range(2)]
+    total = [held[half][0] + last[half].astype(F32) for half in range(2)]
+    return jnp.concatenate(total, axis=1), first, last, kept[0]
+
+
+def input_kernel(
+    place_ref,
+    mine_ref,
+    other_ref,
+    hidden_ref,
+    mid_ref,
+    gain_ref,
+    *refs,
+):
+    lower = place_ref[2] == 0
+    out_ref = refs[-1]
+    parts = []
+    for weights in (mine_ref, other_ref):
+        total, start = None, 0
+        for heads_ref in refs[:-1]:
+            stop = start + heads_ref.shape[2]
+            for at in range(heads_ref.shape[0]):
+                part = last_dims(heads_ref[at], weights[at, :, start:stop])
+                total = part if total is None else total + part
+            start = stop
+        parts.append(total)
+    grad = jnp.concatenate(
+        [jnp.where(lower, parts[0], parts[1]), jnp.where(lower, parts[1], parts[0])], axis=1
+    )
+    values = hidden_ref[...].astype(F32)
+    inverse = lax.rsqrt(jnp.mean(values * values, axis=1, keepdims=True) + epsilon)
+    scaled = grad * gain_ref[...]
+    inner = jnp.mean(scaled * values, axis=1, keepdims=True)
+    out_ref[...] = (
+        mid_ref[...].astype(F32) + inverse * scaled - values * (inverse**3 * inner)
+    )
+
+
+def input_gradient(place, heads, halves, hidden_in, grad_mid, gain, size):
+    length, width = hidden_in.shape
+    wide = halves[0].shape[2]
+    rows = length // size
+    half = pl.BlockSpec((size, width // 2, wide), lambda r, place: (0, 0, 0))
+    return pl.pallas_call(
+        input_kernel,
+        grid_spec=pltpu.PrefetchScalarGridSpec(
+            num_scalar_prefetch=1,
+            grid=(size,),
+            in_specs=[
+                half,
+                half,
+                pl.BlockSpec((rows, width), lambda r, place: (r, 0)),
+                pl.BlockSpec((rows, width), lambda r, place: (r ^ place[0], 0)),
+                pl.BlockSpec((1, width), lambda r, place: (0, 0)),
+            ]
+            + [
+                pl.BlockSpec((size, rows, part.shape[2]), lambda r, place: (0, r, 0))
+                for part in heads
+            ],
+            out_specs=pl.BlockSpec((rows, width), lambda r, place: (r, 0)),
+        ),
+        out_shape=jax.ShapeDtypeStruct((length, width), F32),
+        compiler_params=limits(),
+        cost_estimate=estimate(
+            flops=2 * length * width * wide * size,
+            bytes_accessed=2 * size * wide * (length + width) + 8 * length * width,
+            transcendentals=length,
+        ),
+    )(place, *halves, hidden_in, grad_mid, gain[None], *heads)
 
 
 def local(
@@ -501,7 +573,7 @@
     length, width = hidden_in.shape
     quarter = length // size
     wide, units = w_query.shape[1], w_gate.shape[1]
-    early = round_up(units // 2, 128)
+    early = units * 3 // 4 // 256 * 256
     late = round_up(units - early, 128)
 
     def columns(array, start, count):
@@ -519,7 +591,8 @@
     gains = gains.astype(F32)
     attn_scale, ffn_scale, kv_scale = gains[0], gains[1], gains[2]
 
-    place = jnp.stack([me, lengths[0]])
+    core = lax.axis_index("dp") % 2
+    place = jnp.stack([me, lengths[0], core])
     valid = jnp.arange(length, dtype=jnp.int32) < lengths[0]
     cosine, sine = rotary_tables(length)
     hidden = hidden_in.astype(F32)
@@ -541,10 +614,16 @@
     queries, keys, values, attended_low, attended_flip = attend_forward(
         place, normed, kv_normed, w_heads, cosine, sine, size
     )
-    mid_sum = product_scatter([(attended_low, w_heads, 3)], size, width)
+    mid_sum, _, _, _ = product_scatter([(attended_low, w_heads, 3)], size, width)
     mid = hidden_own + mid_sum
     m_inverse, m_normed = rms_scale(mid, ffn_scale)
-    ffn_in = gather_rows(m_normed.astype(BF), size).reshape(length, width)
+    ffn_in, _, ffn_last = gather_rows(m_normed.astype(BF), size)
+    ffn_in = ffn_in.reshape(length, width)
+
+    half_rows = lax.dynamic_slice_in_dim(w_heads[:, :wide], core * (width // 2), width // 2, 0)
+    query_half, query_first, query_last = gather_rows(after(half_rows, *ffn_last), size)
+    query_other = lax.ppermute(query_half, "dp", [(i, i ^ 1) for i in range(dp_size)])
+    query_halves = (query_half, query_other)
 
     act_early, gate_early, up_early, flip_early = feed_forward(ffn_in, grad_y_low, w_early)
 
@@ -552,11 +631,11 @@
         return products([(flip, 0, 0), (flip, 1, 0), (flip, 2, 1)], [ffn_in, grad_y_low])
 
     grads_early = unit_grads(flip_early)
-    sum_early = lax.psum_scatter(grads_early, "dp", scatter_dimension=1, tiled=True)
+    sum_early = lax.psum_scatter(after(grads_early, w_late, *query_last), "dp", scatter_dimension=1, tiled=True)
     act_late, gate_late, up_late, flip_late = feed_forward(
         after(ffn_in, grads_early), grad_y_low, w_late
     )
-    back_sum = product_scatter(
+    back_sum, _, _, _ = product_scatter(
         [
             (gate_early, w_early, 0),
             (up_early, w_early, 1),
@@ -566,64 +645,103 @@
         size,
         width,
     )
-    grads_late = unit_grads(flip_late)
-    sum_late = lax.psum_scatter(grads_late, "dp", scatter_dimension=1, tiled=True)
-
-    mid_part, grad_ffn_gain = norm_back(back_sum, mid, m_inverse, ffn_scale)
+    mid_part = norm_back(back_sum, mid, m_inverse, ffn_scale)
     grad_mid = grad_y + mid_part
-    grad_mid_low = gather_rows(grad_mid.astype(BF), size).reshape(length, width)
-
-    out_sum = product_scatter([(act_early, w_early, 2), (act_late, w_late, 2)], size, width)
-    layer_out = absolute(gather_rows((mid + out_sum).astype(BF), size), me)
-
-    rel_q, rel_k, rel_v, flip_heads = attend_backward(
-        place, grad_mid_low, w_heads, queries, keys, values, cosine, sine, size
-    )
-    grad_kv_normed = product_scatter([(rel_k, w_heads, 1), (rel_v, w_heads, 2)], size, width)
-    grad_normed = product_scatter([(rel_q, w_heads, 0)], size, width)
+    mid_low = grad_mid.astype(BF)
+    grad_mid_low, mid_first, mid_last = gather_rows(mid_low, size)
+    grad_mid_low = grad_mid_low.reshape(length, width)
+    act_early, act_late = after((act_early, act_late), *mid_first)
+    out_sum, out_first, out_last, out_done = product_scatter(
+        [(act_early, w_early, 2), (act_late, w_late, 2)], size, width, free=mid_last
+    )
+    grads_late = unit_grads(after(flip_late, mid_low))
+    sum_late = lax.psum_scatter(after(grads_late, *mid_first), "dp", scatter_dimension=1, tiled=True)
+    grad_mid_low = after(grad_mid_low, grads_late, out_done)
+
+    group = head_group(wide)
+    groups = wide // group
+    backs, heads_q, q_first, q_last = [], [], [], []
+    grad_in = grad_mid_low
+    for at in range(groups):
+        backs.append(
+            attend_backward(
+                place, grad_in, w_heads, queries, keys, values, cosine, sine, size, at
+            )
+        )
+        part, first, last = gather_part(backs[-1][0], size, at % 2)
+        heads_q.append(jnp.stack(part))
+        q_first.append(first)
+        q_last.append(last)
+        grad_in = after(grad_mid_low, backs[-1][0])
+    kv_terms = [(backs[at][1], w_heads, at + groups) for at in range(groups)]
+    kv_terms += [(backs[at][2], w_heads, at + 2 * groups) for at in range(groups)]
+    lefts = after([left for left, _, _ in kv_terms], *out_first, *q_first[:-1])
+    kv_terms = [(left, right, at) for left, (_, right, at) in zip(lefts, kv_terms)]
+    grad_kv_normed, kv_first, kv_last, kv_done = product_scatter(
+        kv_terms, size, width, earlier=(q_first[-1], *out_last)
+    )
+    layer_own = after((mid + out_sum).astype(BF), *kv_first)
+    layer_rows, layer_first, _ = gather_rows(layer_own, size)
+    layer_out = absolute(layer_rows, me)
     grads_heads = products(
-        [(flip_heads, 0, 0), (flip_heads, 1, 1), (flip_heads, 2, 1), (attended_flip[None], 0, 2)],
-        [normed, kv_normed, after(grad_mid_low, sum_early)],
-    )
+        [(backs[at][3], lead, min(lead, 1)) for lead in range(3) for at in range(groups)]
+        + [(attended_flip[None], 0, 2)],
+        [after(normed, kv_done), kv_normed, after(grad_mid_low, sum_early)],
+    )
+    grads_heads = after(grads_heads, *kv_first, *q_last[:-1])
     sum_heads = lax.psum_scatter(grads_heads, "dp", scatter_dimension=1, tiled=True).astype(F32)
-    x_part, grad_attn_gain = norm_back(grad_normed, hidden_own, own_rows(x_inverse), attn_scale)
-    s_part, grad_kv_gain = norm_back(grad_kv_normed, self_own, own_rows(s_inverse), kv_scale)
-    self_grad = absolute(gather_rows(s_part.astype(BF), size), me).astype(F32)
-    input_grad = absolute(gather_rows((grad_mid + x_part).astype(BF), size), me).astype(F32)
-
-    gain_grads = jnp.stack([grad_attn_gain, grad_ffn_gain, grad_kv_gain])
-    for bit in bit_orders(size)[0]:
-        gain_grads = gain_grads + swap(gain_grads, bit, size)
-    place = lax.axis_index("dp")
-    piece = width // dp_size
-
-    def gain_piece(step):
-        return lax.dynamic_slice_in_dim(gain_grads, ((place + step) % dp_size) * piece, piece, 1)
-
-    total = gain_piece(0)
-    for step in range(1, dp_size):
-        total = total + lax.ppermute(
-            gain_piece(step), "dp", [(i, (i + step) % dp_size) for i in range(dp_size)]
-        )
+    s_part = norm_back(grad_kv_normed, self_own, own_rows(s_inverse), kv_scale)
+    self_rows, self_first, _ = gather_rows(s_part.astype(BF), size)
+    self_grad = absolute(self_rows, me).astype(F32)
+    heads_q[0] = after(heads_q[0], *self_first, *layer_first)
+    input_grad = input_gradient(
+        place, heads_q, query_halves, hidden_in, grad_mid_low, attn_scale, size
+    )
+
     def unit_sums(at):
         early_rows = sum_early[at * early : (at + 1) * early]
         late_rows = sum_late[at * late : at * late + units - early]
         return jnp.concatenate([early_rows, late_rows], axis=0).astype(F32)
 
+    sum_query, sum_key, sum_value = [
+        sum_heads[at * wide : (at + 1) * wide].T for at in range(3)
+    ]
+    sum_gate, sum_up = unit_sums(0).T, unit_sums(1).T
+
+    def gain_part(gain, *pairs):
+        total = 0.0
+        for weights, grads in pairs:
+            total = total + jnp.sum(weights.astype(F32) * grads, axis=1)
+        return total / gain.astype(F32)
+
+    gain_sums = jnp.stack(
+        [
+            gain_part(attn_gain, (w_query, sum_query)),
+            gain_part(ffn_gain, (w_gate, sum_gate), (w_up, sum_up)),
+            gain_part(kv_gain, (w_key, sum_key), (w_value, sum_value)),
+        ]
+    )
+    others = [
+        lax.ppermute(gain_sums, "tensor", [(t, t ^ step) for t in range(size)])
+        for step in range(1, size)
+    ]
+    for other in others:
+        gain_sums = gain_sums + other
+
     return (
         layer_out,
         input_grad,
         self_grad,
-        sum_heads[:wide].T,
-        sum_heads[wide : 2 * wide].T,
-        sum_heads[2 * wide : 3 * wide].T,
+        sum_query,
+        sum_key,
+        sum_value,
         sum_heads[3 * wide :],
-        unit_sums(0).T,
-        unit_sums(1).T,
+        sum_gate,
+        sum_up,
         unit_sums(2),
-        total[0],
-        total[1],
-        total[2],
+        gain_sums[0],
+        gain_sums[1],
+        gain_sums[2],
     )
 
 

time: 699 us -> 621 us (0.89)
  waiting for transfers between devices: 258 us -> 186 us
  local copies, waits for them, and re-layouts: 28.8 us -> 50.8 us
  other arithmetic: 94.5 us -> 76.7 us
    ppermute x42 -> x40, waiting for transfers between devices: 197 us -> 131 us  [swap(): return lax.ppermute(array, 'tensor', [(t, t ^ bit) for t in range(size)])]
    convert_element_type x36 -> x5, other arithmetic: 44.4 us -> 7 us  [the longest x1 3.94 us: local(): self_grad = absolute(self_rows, me).astype(F32)]
    unnamed x71 -> x148, local copies, waits for them, and re-layouts: 11.1 us -> 24.5 us
    another operation x33 -> x37, other arithmetic: 15.1 us -> 27.4 us  [the longest x12 13.9 us: gather_part(): sent = jnp.stack([held[place] for place in places])]
    add x13 -> x17, other arithmetic: 5.33 us -> 14.7 us  [the longest x8 11.4 us: product_scatter(): kept[half].astype(F32) + first[half].astype(F32)]
    squeeze x10, local copies, waits for them, and re-layouts: 3.13 us -> 11.7 us  [gather_part(): held[place ^ bit] = came[-1][at]]
    ppermute x42 -> x40, starting transfers between devices: 44.5 us -> 42.4 us  [swap(): return lax.ppermute(array, 'tensor', [(t, t ^ bit) for t in range(size)])]
    pallas_call x21 -> x11, Pallas kernels: 110 us -> 110 us  [the longest x8 65.9 us: row_products(): pl.pallas_call(functools.partial(rows_kernel, len(terms), side, steps), g...]
  transfers between devices with their start and end apart: 55 -> 50, of which waited for: 27 -> 21; matrix products, arithmetic and copies ran while one was open for 15% -> 17% of each run, Pallas kernels for 33% -> 36%
where the time goes in v3:
time: 621 us; the launch traced here: 614 us
  Pallas kernels  223 us (36%)
  waiting for transfers between devices  186 us (30%)
  other arithmetic  76.7 us (12%)
  local copies, waits for them, and re-layouts  50.8 us (8%)
  starting transfers between devices  46.6 us (8%)
  between operations  16.2 us (3%)
  blocking collectives  14.6 us (2%)
    ppermute x40, waiting for transfers between devices, swap(): return lax.ppermute(array, 'tensor', [(t, t ^ bit) for t in range(size)])  131 us
    pallas_call x8, Pallas kernels, row_products(): pl.pallas_call(functools.partial(rows_kernel, len(terms), side, steps), g...  65.9 us
    all_gather x3, waiting for transfers between devices, local(): lax.all_gather(w, 'dp', axis=0, tiled=True)  54.9 us
    pallas_call x3, Pallas kernels, products(): pl.pallas_call(functools.partial(products_kernel, counts), grid=(total,),...  51.4 us
    ppermute x40, starting transfers between devices, swap(): return lax.ppermute(array, 'tensor', [(t, t ^ bit) for t in range(size)])  42.4 us
    pallas_call x2, Pallas kernels, feed_forward(): pl.pallas_call(feed_kernel, grid=(steps,), in_specs=[whole, whole, pl.Blo...  36.5 us
    pallas_call x2, Pallas kernels, attend_backward(): pl.pallas_call(functools.partial(backward_kernel, size), grid=(1,), in_sp...  25.5 us
    pallas_call x1, Pallas kernels, attend_forward(): pl.pallas_call(functools.partial(forward_kernel, size), grid=(groups,), i...  24.9 us
  transfers between devices with their start and end apart: 50, of which 21 were waited for; matrix products, arithmetic and copies ran while one was open for 17% of the time, Pallas kernels for 36%

profile of v3, /device:TPU:0, one launch (start us, length us, event | category | flops | bytes accessed | tf_op | source)
XLA Modules:
  0.0 614.0 jit_solution(8723468307312009416)
XLA Ops:
  14.4 14.6 %all_gather.12 = bf16[3,2048]{1,0:T(4,128)(2,1)S(1)} all-gather(bf16[3,256]{1,0:T(4,128)(2,1)S(1)} %pad_maximum_fusion.26), channel_id=1, replica_groups=mesh['dp'=8,'tensor'=4] {'dp'}, dimensions={1}, use_global_device_ids=true | all-gather | bytes 13824 | tf_op jit(solution)/shard_map/all_gather | solution.py:590
  40.7 54.9 %all-gather.4.cloned.1.call-done.wq_ref.wk_ref.wv_ref.refs_1_.wo_ref.refs_4_.refs_5_.refs_6_.refs_7_ = bf16[2048,2048]{1,0:T(8,128)(2,1)} async-done(((bf16[256,2048]{1,0:T(8,128)(2,1)}), bf16[2048,2048]{1,0:T(8,128)(2,1)}) %all-gather.4.cloned.1.call-update) | async-done | bytes 8388624 | tf_op jit(solution)/shard_map/all_gather | solution.py:589
  95.6 24.9 %shard_map.237 = (bf16[1024,512]{1,0:T(8,128)(2,1)}, bf16[1024,512]{1,0:T(8,128)(2,1)}, bf16[1024,512]{1,0:T(8,128)(2,1)}, bf16[1024,512]{1,0:T(8,128)(2,1)}, bf16[512,1024]{1,0:T(8,128)(2,1)}) custom-call(s32[3]{0:T(128)} %pad_add_fusion.place_ref, bf16[1024,2048]{1,0:T(8,128)(2,1)} %get-tuple-element.144.normed_ref.refs_7_, ...), custom_call_target="tpu_custom_call" | custom-call | flops 8053063680 | bytes 18874368 | tf_op jit(solution)/shard_map/pallas_call | solution.py:114
  135.3 16.2 %collective-permute-done.2 = bf16[2,256,1024]{2,1,0:T(8,128)(2,1)} collective-permute-done((bf16[2,256,1024]{2,1,0:T(8,128)(2,1)}, bf16[2,256,1024]{2,1,0:T(8,128)(2,1)}, u32[]{:S(2)}, u32[]{:S(2)}) %collective-permute-start.2) | collective-permute-done | bytes 1048608 | tf_op jit(solution)/shard_map/ppermute | solution.py:408
  160.6 7.2 %collective-permute-done.3 = bf16[256,1024]{1,0:T(8,128)(2,1)} collective-permute-done((bf16[256,1024]{1,0:T(8,128)(2,1)}, bf16[256,1024]{1,0:T(8,128)(2,1)}, u32[]{:S(2)}, u32[]{:S(2)}) %collective-permute-start.3) | collective-permute-done | bytes 524320 | tf_op jit(solution)/shard_map/ppermute | solution.py:408
  176.2 9.7 %collective-permute-done.6 = bf16[1,256,1024]{2,1,0:T(8,128)(2,1)S(1)} collective-permute-done((bf16[1,256,1024]{2,1,0:T(8,128)(2,1)S(1)}, bf16[1,256,1024]{2,1,0:T(8,128)(2,1)S(1)}, u32[]{:S(2)}, u32[]{:S(2)}) %collective-permute-start.6) | collective-permute-done | bytes 524320 | tf_op jit(solution)/shard_map/ppermute | solution.py:408
  198.3 11.6 %collective-permute-done.7 = bf16[2,256,1024]{2,1,0:T(8,128)(2,1)} collective-permute-done((bf16[2,256,1024]{2,1,0:T(8,128)(2,1)}, bf16[2,256,1024]{2,1,0:T(8,128)(2,1)}, u32[]{:S(2)}, u32[]{:S(2)}) %collective-permute-start.7) | collective-permute-done | bytes 1048608 | tf_op jit(solution)/shard_map/ppermute | solution.py:408
  228.7 21.6 %shard_map.240 = (bf16[1024,1024]{1,0:T(8,128)(2,1)}, bf16[1024,1024]{1,0:T(8,128)(2,1)}, bf16[1024,1024]{1,0:T(8,128)(2,1)}, bf16[3,1024,1024]{2,1,0:T(8,128)(2,1)}) custom-call(bf16[1024,2048]{1,0:T(8,128)(2,1)} %bitcast.249, bf16[1024,2048]{1,0:T(8,128)(2,1)} %bitcast.245, ...), custom_call_target="tpu_custom_call" | custom-call | flops 12884901888 | bytes 33554432 | tf_op jit(solution)/shard_map/pallas_call | solution.py:275
  250.4 21.1 %shard_map.241 = bf16[3072,2048]{1,0:T(8,128)(2,1)} custom-call(bf16[3,1024,1024]{2,1,0:T(8,128)(2,1)} %get-tuple-element.88.refs_0_.refs_1_.refs_2_, bf16[3,1024,1024]{2,1,0:T(8,128)(2,1)} %get-tuple-element.88.refs_0_.refs_1_.refs_2_, bf16[3,1024,1024]{2,1,0:T(8,128)(2,1)} %get-tuple-element.88.refs_0_.refs_1_.refs_2_, bf16[1024,2048]{1,0:T(8,128)(2,1)} %bitcast.250, ...), custom_call_target="tpu_custom_call" | custom-call | flops 12884901888 | bytes 27262976 | tf_op jit(solution)/shard_map/pallas_call | solution.py:324
  272.8 14.8 %shard_map.242 = (bf16[1024,384]{1,0:T(8,128)(2,1)}, bf16[1024,384]{1,0:T(8,128)(2,1)}, bf16[1024,384]{1,0:T(8,128)(2,1)}, bf16[3,384,1024]{2,1,0:T(8,128)(2,1)}) custom-call(bf16[1024,2048]{1,0:T(8,128)(2,1)} %bitcast.251, bf16[1024,2048]{1,0:T(8,128)(2,1)} %bitcast.247, ...), custom_call_target="tpu_custom_call" | custom-call | flops 4831838208 | bytes 17825792 | tf_op jit(solution)/shard_map/pallas_call | solution.py:275
  287.6 12.6 %shard_map.243 = (bf16[2,256,1024]{2,1,0:T(8,128)(2,1)}, bf16[2,256,1024]{2,1,0:T(8,128)(2,1)}) custom-call(bf16[4,256,1024]{2,1,0:T(8,128)(2,1)} %bitcast.259, bf16[4,256,1024]{2,1,0:T(8,128)(2,1)} %bitcast.261, bf16[4,256,384]{2,1,0:T(8,128)(2,1)} %bitcast.267, bf16[4,256,384]{2,1,0:T(8,128)(2,1)} %bitcast.269, ...), custom_call_target="tpu_custom_call" | custom-call | flops 5905580032 | bytes 19398656 | tf_op jit(solution)/shard_map/pallas_call | solution.py:368
  300.9 12.4 %shard_map.244 = (bf16[2,256,1024]{2,1,0:T(8,128)(2,1)}, bf16[2,256,1024]{2,1,0:T(8,128)(2,1)}) custom-call(bf16[4,256,1024]{2,1,0:T(8,128)(2,1)} %bitcast.260, bf16[4,256,1024]{2,1,0:T(8,128)(2,1)} %bitcast.262, bf16[4,256,384]{2,1,0:T(8,128)(2,1)} %bitcast.268, bf16[4,256,384]{2,1,0:T(8,128)(2,1)} %bitcast.270, ...), custom_call_target="tpu_custom_call" | custom-call | flops 5905580032 | bytes 19398656 | tf_op jit(solution)/shard_map/pallas_call | solution.py:368
  338.4 12.6 %shard_map.247 = bf16[1152,2048]{1,0:T(8,128)(2,1)} custom-call(bf16[3,384,1024]{2,1,0:T(8,128)(2,1)} %get-tuple-element.114.refs_0_.refs_1_.refs_2_, bf16[3,384,1024]{2,1,0:T(8,128)(2,1)} %get-tuple-element.114.refs_0_.refs_1_.refs_2_, bf16[3,384,1024]{2,1,0:T(8,128)(2,1)} %get-tuple-element.114.refs_0_.refs_1_.refs_2_, bf16[1024,2048]{1,0:T(8,128)(2,1)} %bitcast.252, ...), custom_call_target="tpu_custom_call" | custom-call | flops 4831838208 | bytes 15466496 | tf_op jit(solution)/shard_map/pallas_call | solution.py:324
  358.4 8.5 %shard_map.245 = (bf16[2,256,1024]{2,1,0:T(8,128)(2,1)}, bf16[2,256,1024]{2,1,0:T(8,128)(2,1)}) custom-call(bf16[4,256,1024]{2,1,0:T(8,128)(2,1)} %bitcast.257, bf16[4,256,384]{2,1,0:T(8,128)(2,1)} %bitcast.265, bf16[2048,3072]{1,0:T(8,128)(2,1)} %all-gather.6.cloned.1.call-done.wg_ref.wu_ref.wd_ref.refs_4_.refs_5_.refs_2_, ...), custom_call_target="tpu_custom_call" | custom-call | flops 2952790016 | bytes 10747904 | tf_op jit(solution)/shard_map/pallas_call | solution.py:368
  366.9 8.1 %shard_map.246 = (bf16[2,256,1024]{2,1,0:T(8,128)(2,1)}, bf16[2,256,1024]{2,1,0:T(8,128)(2,1)}) custom-call(bf16[4,256,1024]{2,1,0:T(8,128)(2,1)} %bitcast.258, bf16[4,256,384]{2,1,0:T(8,128)(2,1)} %bitcast.266, bf16[2048,3072]{1,0:T(8,128)(2,1)} %all-gather.6.cloned.1.call-done.wg_ref.wu_ref.wd_ref.refs_4_.refs_5_.refs_2_, ...), custom_call_target="tpu_custom_call" | custom-call | flops 2952790016 | bytes 10747904 | tf_op jit(solution)/shard_map/pallas_call | solution.py:368
  388.5 12.6 %shard_map.248 = (bf16[1024,256]{1,0:T(8,128)(2,1)}, bf16[1024,256]{1,0:T(8,128)(2,1)}, bf16[1024,256]{1,0:T(8,128)(2,1)}, bf16[3,256,1024]{2,1,0:T(8,128)(2,1)}) custom-call(s32[3]{0:T(128)} %pad_add_fusion.place_ref, bf16[1024,2048]{1,0:T(8,128)(2,1)} %bitcast.241, ...), custom_call_target="tpu_custom_call" | custom-call | flops 3758096384 | bytes 9961472 | tf_op jit(solution)/shard_map/pallas_call | solution.py:221
  401.1 12.9 %shard_map.249 = (bf16[1024,256]{1,0:T(8,128)(2,1)}, bf16[1024,256]{1,0:T(8,128)(2,1)}, bf16[1024,256]{1,0:T(8,128)(2,1)}, bf16[3,256,1024]{2,1,0:T(8,128)(2,1)}) custom-call(s32[3]{0:T(128)} %pad_add_fusion.place_ref, bf16[1024,2048]{1,0:T(8,128)(2,1)} %bitcast.242, ...), custom_call_target="tpu_custom_call" | custom-call | flops 3758096384 | bytes 9961472 | tf_op jit(solution)/shard_map/pallas_call | solution.py:221
  440.4 6.9 %shard_map.251 = (bf16[2,256,1024]{2,1,0:T(8,128)(2,1)}, bf16[2,256,1024]{2,1,0:T(8,128)(2,1)}) custom-call(bf16[4,256,256]{2,1,0:T(8,128)(2,1)} %bitcast.274, bf16[4,256,256]{2,1,0:T(8,128)(2,1)} %bitcast.278, bf16[4,256,256]{2,1,0:T(8,128)(2,1)} %bitcast.276, bf16[4,256,256]{2,1,0:T(8,128)(2,1)} %bitcast.280, ...), custom_call_target="tpu_custom_call" | custom-call | flops 2147483648 | bytes 8388608 | tf_op jit(solution)/shard_map/pallas_call | solution.py:368
  447.3 17.7 %shard_map.253 = bf16[2048,2048]{1,0:T(8,128)(2,1)} custom-call(bf16[3,256,1024]{2,1,0:T(8,128)(2,1)} %get-tuple-element.141.refs_0_.refs_2_.refs_4_, bf16[3,256,1024]{2,1,0:T(8,128)(2,1)} %get-tuple-element.142.refs_1_.refs_3_.refs_5_, bf16[3,256,1024]{2,1,0:T(8,128)(2,1)} %get-tuple-element.141.refs_0_.refs_2_.refs_4_, ...), custom_call_target="tpu_custom_call" | custom-call | flops 8589934592 | bytes 25165824 | tf_op jit(solution)/shard_map/pallas_call | solution.py:324
  492.0 10.2 %collective-permute-done.35 = bf16[256,1024]{1,0:T(8,128)(2,1)S(1)} collective-permute-done((bf16[256,1024]{1,0:T(8,128)(2,1)S(1)}, bf16[256,1024]{1,0:T(8,128)(2,1)S(1)}, u32[]{:S(2)}, u32[]{:S(2)}) %collective-permute-start.35) | collective-permute-done | bytes 524320 | tf_op jit(solution)/shard_map/ppermute | solution.py:408
  503.1 13.3 %collective-permute-done.34 = bf16[256,1024]{1,0:T(8,128)(2,1)S(1)} collective-permute-done((bf16[256,1024]{1,0:T(8,128)(2,1)S(1)}, bf16[256,1024]{1,0:T(8,128)(2,1)S(1)}, u32[]{:S(2)}, u32[]{:S(2)}) %collective-permute-start.34) | collective-permute-done | bytes 524320 | tf_op jit(solution)/shard_map/ppermute | solution.py:408
  529.9 9.0 %collective-permute-done.36 = bf16[1,256,1024]{2,1,0:T(8,128)(2,1)S(1)} collective-permute-done((bf16[1,256,1024]{2,1,0:T(8,128)(2,1)S(1)}, bf16[1,256,1024]{2,1,0:T(8,128)(2,1)S(1)}, u32[]{:S(2)}, u32[]{:S(2)}) %collective-permute-start.36) | collective-permute-done | bytes 524320 | tf_op jit(solution)/shard_map/ppermute | solution.py:408
  542.6 18.7 %shard_map.252 = f32[1024,2048]{1,0:T(8,128)} custom-call(s32[3]{0:T(128)} %pad_add_fusion.place_ref, bf16[4,1024,512]{2,1,0:T(8,128)(2,1)} %copy-done.16, bf16[4,1024,512]{2,1,0:T(8,128)(2,1)} %collective-permute-done.31.other_ref, bf16[1024,2048]{1,0:T(8,128)(2,1)} %hidden_ref.1, bf16[1024,2048]{1,0:T(8,128)(2,1)} %bitcast.244, f32[1,2048]{1,0:T(1,128)} %copy-done.60, ...), custom_call_target="tpu_custom_call" | custom-call | flops 8589934592 | bytes 29360128 | tf_op jit(solution)/shard_map/pallas_call | solution.py:526
  568.7 14.4 %collective-permute-done.40 = bf16[2,256,1024]{2,1,0:T(8,128)(2,1)} collective-permute-done((bf16[2,256,1024]{2,1,0:T(8,128)(2,1)}, bf16[2,256,1024]{2,1,0:T(8,128)(2,1)}, u32[]{:S(2)}, u32[]{:S(2)}) %collective-permute-start.40) | collective-permute-done | bytes 1048608 | tf_op jit(solution)/shard_map/ppermute | solution.py:408
  (388 shorter events, 231.2 us)
Async XLA Ops:
  7.2 88.4 %all-gather.4.cloned.1.call-start = ((), (), s32[]{:S(2)}) async-start(), calls=%async_computation.3 | async-start | bytes 9437184 | tf_op jit(solution)/shard_map/all_gather | solution.py:589
  10.6 218.1 %all-gather.6.cloned.1.call-start = ((), (), s32[]{:S(2)}) async-start(), calls=%async_computation.4 | async-start | bytes 14155776 | tf_op jit(solution)/shard_map/all_gather | solution.py:589
  13.6 257.8 %all-gather.8.cloned.1.call-start = ((), (), s32[]{:S(2)}) async-start(), calls=%async_computation.5 | async-start | bytes 5308416 | tf_op jit(solution)/shard_map/all_gather | solution.py:589
  125.9 25.6 %collective-permute-start.2 = (bf16[2,256,1024]{2,1,0:T(8,128)(2,1)}, bf16[2,256,1024]{2,1,0:T(8,128)(2,1)}, u32[]{:S(2)}, u32[]{:S(2)}) collective-permute-start(bf16[2,256,1024]{2,1,0:T(8,128)(2,1)} %get-tuple-element.83), channel_id=1, source_target_pairs={{0,2},{1,3},{2,0},{3,1},{4,6},{5,7},{6,4},{7,5},{8,10},{9,11},{10,... | collective-permute-start | bytes 3145736 | tf_op jit(solution)/shard_map/ppermute | solution.py:408
  127.4 28.5 %collective-permute-start = (bf16[2,256,1024]{2,1,0:T(8,128)(2,1)}, bf16[2,256,1024]{2,1,0:T(8,128)(2,1)S(1)}, u32[]{:S(2)}, u32[]{:S(2)}) collective-permute-start(bf16[2,256,1024]{2,1,0:T(8,128)(2,1)} %get-tuple-element.82), channel_id=1, source_target_pairs={{0,1},{1,0},{2,3},{3,2},{4,5},{5,4},{6,7},{7,6},{8,9},{9,8},{10,11... | collective-permute-start | bytes 3145736 | tf_op jit(solution)/shard_map/ppermute | solution.py:408
  160.1 287.2 %reduce-scatter.4.cloned.1.call-start = ((), (), s32[]{:S(2)}) async-start(), calls=%async_computation.6 | async-start | bytes 14155776 | tf_op jit(solution)/shard_map/reduce_scatter | solution.py:634
  223.5 47.9 %collective-permute-start.30 = (bf16[2,1024,256]{2,1,0:T(8,128)(2,1)S(1)}, bf16[2,1024,256]{2,1,0:T(8,128)(2,1)S(1)}, u32[]{:S(2)}, u32[]{:S(2)}) collective-permute-start(bf16[2,1024,256]{2,1,0:T(8,128)(2,1)S(1)} %pad_maximum_fusion.18), channel_id=1, source_target_pairs={{0,2},{1,3},{2,0},{3,1},{4,6},{5,7},{6,4},{7,5},{8,10},{9,11},{10,... | collective-permute-start | bytes 3145736 | tf_op jit(solution)/shard_map/ppermute | solution.py:408
  226.0 45.4 %collective-permute-start.28 = (bf16[2,1024,256]{2,1,0:T(8,128)(2,1)}, bf16[2,1024,256]{2,1,0:T(8,128)(2,1)S(1)}, u32[]{:S(2)}, u32[]{:S(2)}) collective-permute-start(bf16[2,1024,256]{2,1,0:T(8,128)(2,1)} %pad_maximum_fusion.17), channel_id=1, source_target_pairs={{0,1},{1,0},{2,3},{3,2},{4,5},{5,4},{6,7},{7,6},{8,9},{9,8},{10,11... | collective-permute-start | bytes 3145736 | tf_op jit(solution)/shard_map/ppermute | solution.py:408
  272.8 319.2 %reduce-scatter.8.cloned.1.call-start = ((), (), s32[]{:S(2)}) async-start(), calls=%async_computation.8 | async-start | bytes 5308416 | tf_op jit(solution)/shard_map/reduce_scatter | solution.py:658
  351.1 246.1 %reduce-scatter.6.cloned.1.call-start = ((), (), s32[]{:S(2)}) async-start(), calls=%async_computation.7 | async-start | bytes 9437184 | tf_op jit(solution)/shard_map/reduce_scatter | solution.py:692
  378.2 37.2 %collective-permute-start.18 = (bf16[2,256,1024]{2,1,0:T(8,128)(2,1)}, bf16[2,256,1024]{2,1,0:T(8,128)(2,1)}, u32[]{:S(2)}, u32[]{:S(2)}) collective-permute-start(bf16[2,256,1024]{2,1,0:T(8,128)(2,1)} %get-tuple-element.112), channel_id=1, source_target_pairs={{0,2},{1,3},{2,0},{3,1},{4,6},{5,7},{6,4},{7,5},{8,10},{9,11},{10,... | collective-permute-start | bytes 3145736 | tf_op jit(solution)/shard_map/ppermute | solution.py:408
  380.6 38.5 %collective-permute-start.16 = (bf16[2,256,1024]{2,1,0:T(8,128)(2,1)}, bf16[2,256,1024]{2,1,0:T(8,128)(2,1)}, u32[]{:S(2)}, u32[]{:S(2)}) collective-permute-start(bf16[2,256,1024]{2,1,0:T(8,128)(2,1)} %get-tuple-element.110), channel_id=1, source_target_pairs={{0,1},{1,0},{2,3},{3,2},{4,5},{5,4},{6,7},{7,6},{8,9},{9,8},{10,11... | collective-permute-start | bytes 3145736 | tf_op jit(solution)/shard_map/ppermute | solution.py:408
  425.6 39.5 %collective-permute-start.32 = (bf16[2,1024,256]{2,1,0:T(8,128)(2,1)}, bf16[2,1024,256]{2,1,0:T(8,128)(2,1)}, u32[]{:S(2)}, u32[]{:S(2)}) collective-permute-start(bf16[2,1024,256]{2,1,0:T(8,128)(2,1)} %pad_maximum_fusion.19), channel_id=1, source_target_pairs={{0,1},{1,0},{2,3},{3,2},{4,5},{5,4},{6,7},{7,6},{8,9},{9,8},{10,11... | collective-permute-start | bytes 3145736 | tf_op jit(solution)/shard_map/ppermute | solution.py:408
  433.5 36.8 %collective-permute-start.21 = (bf16[2,256,1024]{2,1,0:T(8,128)(2,1)}, bf16[2,256,1024]{2,1,0:T(8,128)(2,1)}, u32[]{:S(2)}, u32[]{:S(2)}) collective-permute-start(bf16[2,256,1024]{2,1,0:T(8,128)(2,1)} %get-tuple-element.129), channel_id=1, source_target_pairs={{0,1},{1,0},{2,3},{3,2},{4,5},{5,4},{6,7},{7,6},{8,9},{9,8},{10,11... | collective-permute-start | bytes 3145736 | tf_op jit(solution)/shard_map/ppermute | solution.py:408
  434.3 36.0 %collective-permute-start.22 = (bf16[2,256,1024]{2,1,0:T(8,128)(2,1)}, bf16[2,256,1024]{2,1,0:T(8,128)(2,1)}, u32[]{:S(2)}, u32[]{:S(2)}) collective-permute-start(bf16[2,256,1024]{2,1,0:T(8,128)(2,1)} %get-tuple-element.130), channel_id=1, source_target_pairs={{0,2},{1,3},{2,0},{3,1},{4,6},{5,7},{6,4},{7,5},{8,10},{9,11},{10,... | collective-permute-start | bytes 3145736 | tf_op jit(solution)/shard_map/ppermute | solution.py:408
  478.6 64.0 %collective-permute-start.31 = (bf16[4,1024,512]{2,1,0:T(8,128)(2,1)S(1)}, bf16[4,1024,512]{2,1,0:T(8,128)(2,1)}, u32[]{:S(2)}, u32[]{:S(2)}) collective-permute-start(bf16[4,1024,512]{2,1,0:T(8,128)(2,1)S(1)} %pad_maximum_fusion.5.mine_ref), channel_id=1, source_target_pairs={{0,4},{4,0},{8,12},{12,8},{16,20},{20,16},{24,28},{28,24},{1,5},{5... | collective-permute-start | bytes 12582920 | tf_op jit(solution)/shard_map/ppermute | solution.py:625
  479.1 39.3 %collective-permute-start.38 = (bf16[2,1024,256]{2,1,0:T(8,128)(2,1)S(1)}, bf16[2,1024,256]{2,1,0:T(8,128)(2,1)S(1)}, u32[]{:S(2)}, u32[]{:S(2)}) collective-permute-start(bf16[2,1024,256]{2,1,0:T(8,128)(2,1)S(1)} %pad_maximum_fusion.20), channel_id=1, source_target_pairs={{0,2},{1,3},{2,0},{3,1},{4,6},{5,7},{6,4},{7,5},{8,10},{9,11},{10,... | collective-permute-start | bytes 3145736 | tf_op jit(solution)/shard_map/ppermute | solution.py:408
  490.2 26.3 %collective-permute-start.34 = (bf16[256,1024]{1,0:T(8,128)(2,1)S(1)}, bf16[256,1024]{1,0:T(8,128)(2,1)S(1)}, u32[]{:S(2)}, u32[]{:S(2)}) collective-permute-start(bf16[256,1024]{1,0:T(8,128)(2,1)S(1)} %fusion.31), channel_id=1, source_target_pairs={{0,2},{1,3},{2,0},{3,1},{4,6},{5,7},{6,4},{7,5},{8,10},{9,11},{10,... | collective-permute-start | bytes 1572872 | tf_op jit(solution)/shard_map/ppermute | solution.py:408
  490.5 31.8 %collective-permute-start.25 = (bf16[1,256,1024]{2,1,0:T(8,128)(2,1)S(1)}, bf16[1,256,1024]{2,1,0:T(8,128)(2,1)S(1)}, u32[]{:S(2)}, u32[]{:S(2)}) collective-permute-start(bf16[1,256,1024]{2,1,0:T(8,128)(2,1)S(1)} %get-tuple-element.221), channel_id=1, source_target_pairs={{0,1},{1,0},{2,3},{3,2},{4,5},{5,4},{6,7},{7,6},{8,9},{9,8},{10,11... | collective-permute-start | bytes 1572872 | tf_op jit(solution)/shard_map/ppermute | solution.py:408
  502.2 25.5 %collective-permute-start.23 = (bf16[1,256,1024]{2,1,0:T(8,128)(2,1)S(1)}, bf16[1,256,1024]{2,1,0:T(8,128)(2,1)S(1)}, u32[]{:S(2)}, u32[]{:S(2)}) collective-permute-start(bf16[1,256,1024]{2,1,0:T(8,128)(2,1)S(1)} %get-tuple-element.220), channel_id=1, source_target_pairs={{0,2},{1,3},{2,0},{3,1},{4,6},{5,7},{6,4},{7,5},{8,10},{9,11},{10,... | collective-permute-start | bytes 1572872 | tf_op jit(solution)/shard_map/ppermute | solution.py:408
  523.4 38.0 %collective-permute-start.26 = (bf16[2,256,1024]{2,1,0:T(8,128)(2,1)}, bf16[2,256,1024]{2,1,0:T(8,128)(2,1)}, u32[]{:S(2)}, u32[]{:S(2)}) collective-permute-start(bf16[2,256,1024]{2,1,0:T(8,128)(2,1)} %pad_maximum_fusion.16), channel_id=1, source_target_pairs={{0,2},{1,3},{2,0},{3,1},{4,6},{5,7},{6,4},{7,5},{8,10},{9,11},{10,... | collective-permute-start | bytes 3145736 | tf_op jit(solution)/shard_map/ppermute | solution.py:408
  528.8 34.0 %collective-permute-start.24 = (bf16[2,256,1024]{2,1,0:T(8,128)(2,1)}, bf16[2,256,1024]{2,1,0:T(8,128)(2,1)}, u32[]{:S(2)}, u32[]{:S(2)}) collective-permute-start(bf16[2,256,1024]{2,1,0:T(8,128)(2,1)} %pad_maximum_fusion.15), channel_id=1, source_target_pairs={{0,1},{1,0},{2,3},{3,2},{4,5},{5,4},{6,7},{7,6},{8,9},{9,8},{10,11... | collective-permute-start | bytes 3145736 | tf_op jit(solution)/shard_map/ppermute | solution.py:408
  540.1 43.1 %collective-permute-start.40 = (bf16[2,256,1024]{2,1,0:T(8,128)(2,1)}, bf16[2,256,1024]{2,1,0:T(8,128)(2,1)}, u32[]{:S(2)}, u32[]{:S(2)}) collective-permute-start(bf16[2,256,1024]{2,1,0:T(8,128)(2,1)} %pad_maximum_fusion.22), channel_id=1, source_target_pairs={{0,2},{1,3},{2,0},{3,1},{4,6},{5,7},{6,4},{7,5},{8,10},{9,11},{10,... | collective-permute-start | bytes 3145736 | tf_op jit(solution)/shard_map/ppermute | solution.py:408
  541.9 42.5 %collective-permute-start.39 = (bf16[2,256,1024]{2,1,0:T(8,128)(2,1)}, bf16[2,256,1024]{2,1,0:T(8,128)(2,1)}, u32[]{:S(2)}, u32[]{:S(2)}) collective-permute-start(bf16[2,256,1024]{2,1,0:T(8,128)(2,1)} %pad_maximum_fusion.21), channel_id=1, source_target_pairs={{0,1},{1,0},{2,3},{3,2},{4,5},{5,4},{6,7},{7,6},{8,9},{9,8},{10,11... | collective-permute-start | bytes 3145736 | tf_op jit(solution)/shard_map/ppermute | solution.py:408
  (99 other events, 732.2 us)
Sparse Core Ops, SparseCore 0:
  10.7 84.7 all-gather.3
  97.2 115.2 all-gather.5
  214.2 49.9 all-gather.7
  271.6 126.1 reduce-scatter.3
  400.0 53.3 reduce-scatter.7
  470.5 89.3 reduce-scatter.5

commit v4 on v3

--- a/solution.py
+++ b/solution.py
@@ -336,17 +336,16 @@
     )(*[left for left, _, _ in terms], *rights)
 
 
-def rows_kernel(count, side, steps, *refs):
-    lefts, rights, outs = refs[:count], refs[count:-2], refs[-2:]
+def rows_kernel(count, steps, *refs):
+    lefts, rights, outs = refs[: 2 * count], refs[2 * count : -2], refs[-2:]
     for half in range(2):
 
         @pl.when(pl.program_id(0) // steps == half)
         def _(half=half):
             for piece in range(2):
-                row = 2 * piece + side if half == 0 else 2 * side + piece
                 total = None
-                for left, right in zip(lefts, rights):
-                    part = last_dims(left[row], right[...])
+                for at, right in enumerate(rights):
+                    part = last_dims(lefts[2 * at + piece][...], right[...])
                     total = part if total is None else total + part
                 outs[half][piece] = total.astype(BF)
 
@@ -359,14 +358,20 @@
     flops = nbytes = 0
     for left, right, at in terms:
         rows, depth = left.shape[0] // 4, left.shape[1]
-        lefts.append(left.reshape(4, rows, depth))
-        left_specs.append(pl.BlockSpec((4, rows, depth), lambda j: (0, 0, 0)))
+        for piece in range(2):
+
+            def block(j, piece=piece):
+                upper = j // steps
+                return ((1 - upper) * (2 * piece + side) + upper * (2 * side + piece), 0)
+
+            lefts.append(left)
+            left_specs.append(pl.BlockSpec((rows, depth), block))
         right_specs.append(pl.BlockSpec((step, depth), lambda j, at=at: (j, at)))
         rights.append(right)
         flops += 8 * rows * depth * columns
         nbytes += 4 * depth * (2 * rows + columns)
     return pl.pallas_call(
-        functools.partial(rows_kernel, len(terms), side, steps),
+        functools.partial(rows_kernel, len(terms), steps),
         grid=(2 * steps,),
         in_specs=left_specs + right_specs,
         out_specs=[
@@ -418,14 +423,6 @@
     return jnp.stack(
         [lax.dynamic_slice_in_dim(array, (me ^ step) * part, part, 0) for step in range(size)]
     )
-
-
-def absolute(blocks, me):
-    parts = [
-        lax.dynamic_index_in_dim(blocks, me ^ step, 0, keepdims=False)
-        for step in range(blocks.shape[0])
-    ]
-    return jnp.concatenate(parts, axis=0)
 
 
 def scatter_sum(blocks):
@@ -448,63 +445,127 @@
     return jnp.concatenate(sums, axis=1)
 
 
-def gather_part(own, size, group, earlier=()):
-    held, came = {0: own}, []
-    for bit in bit_orders(size)[group][::-1]:
-        places = list(held)
-        sent = jnp.stack([held[place] for place in places])
-        came.append(swap(after(sent, *earlier) if came else sent, bit, size))
-        for at, place in enumerate(places):
-            held[place ^ bit] = came[-1][at]
-    return [held[place] for place in range(size)], came[0], came[-1]
-
-
-def gather_rows(own, size, earlier=()):
+def gather_start(own, size, group):
+    return gather_step({0: (own[None], 0)}, bit_orders(size)[group][-1], size)
+
+
+def gather_step(held, bit, size, earlier=()):
+    places = list(held)
+    sent = jnp.stack([held[place][0][held[place][1]] for place in places])
+    got = swap(after(sent, *earlier), bit, size)
+    return {**held, **{place ^ bit: (got, at) for at, place in enumerate(places)}}, got
+
+
+def gather_end(held, size, group, earlier=()):
+    got = None
+    for bit in bit_orders(size)[group][-2::-1]:
+        held, got = gather_step(held, bit, size, earlier)
+    return [held[place] for place in range(size)], got
+
+
+def halves_start(own, size):
     half = own.shape[1] // 2
-    low, low_first, low_last = gather_part(own[:, :half], size, 0, earlier)
-    high, high_first, high_last = gather_part(own[:, half:], size, 1, earlier)
-    rows = jnp.stack([jnp.concatenate(pair, axis=1) for pair in zip(low, high)])
-    return rows, [low_first, high_first], [low_last, high_last]
-
-
-def product_scatter(terms, size, width, earlier=(), free=()):
+    parts = (own[:, :half], own[:, half:])
+    state = [gather_start(part, size, group) for group, part in enumerate(parts)]
+    return [held for held, _ in state], [got for _, got in state]
+
+
+def halves_end(state, size, earlier=()):
+    ends = [gather_end(held, size, group, earlier) for group, held in enumerate(state)]
+    return [parts for parts, _ in ends], [got for _, got in ends]
+
+
+def assemble_kernel(cases, shift_ref, *refs):
+    out_ref = refs[-1]
+    place = pl.program_id(0) ^ shift_ref[0]
+    for case, picks in enumerate(cases):
+
+        @pl.when(place == case)
+        def _(picks=picks):
+            columns = 0
+            for at, index in picks:
+                part = refs[at][index]
+                out_ref[:, columns : columns + part.shape[1]] = part.astype(out_ref.dtype)
+                columns += part.shape[1]
+
+
+def arrays_of(halves):
+    arrays, picks = [], []
+    for parts in halves:
+        picks.append([])
+        for array, index in parts:
+            known = [at for at, other in enumerate(arrays) if other is array]
+            if not known:
+                arrays.append(array)
+            picks[-1].append((known[0] if known else len(arrays) - 1, index))
+    return arrays, picks
+
+
+def assemble(halves, shift, dtype):
+    arrays, picks = arrays_of(halves)
+    size = len(picks[0])
+    rows = arrays[0].shape[1]
+    width = sum(parts[0][0].shape[2] for parts in halves)
+    return pl.pallas_call(
+        functools.partial(assemble_kernel, list(zip(*picks))),
+        grid=(size,),
+        in_specs=[pl.BlockSpec(memory_space=pltpu.SMEM)]
+        + [pl.BlockSpec(array.shape, lambda r: (0, 0, 0)) for array in arrays],
+        out_specs=pl.BlockSpec((rows, width), lambda r: (r, 0)),
+        out_shape=jax.ShapeDtypeStruct((size * rows, width), dtype),
+        compiler_params=limits(),
+        cost_estimate=estimate(
+            flops=size * rows * width, bytes_accessed=6 * size * rows * width, transcendentals=0
+        ),
+    )(shift, *arrays)
+
+
+def scatter_start(terms, size, width, earlier=(), free=()):
     if size != 4:
         total = 0.0
         for left, right, at in terms:
             depth = left.shape[1]
             total = total + last_dims(left, right[:, at * depth : (at + 1) * depth])
-        return scatter_sum(total.reshape(size, -1, width)), [total], [total], total
+        return total, [total], [total], [total]
     sent = row_products(terms, 1, width)
-    first = [swap(after(sent[half], *free), 1 + half, size) for half in range(2)]
     lefts = after([left for left, _, _ in terms], *sent, *earlier)
     terms = [(left, right, at) for left, (_, right, at) in zip(lefts, terms)]
     kept = row_products(terms, 0, width)
+    if free:
+        free = (*free, *kept)
+    first = [swap(after(sent[half], *free), 1 + half, size) for half in range(2)]
+    return (first, kept), sent, first, kept
+
+
+def scatter_end(state, size, width, earlier=()):
+    if size != 4:
+        total = scatter_sum(state.reshape(size, -1, width))
+        return total, [total], [total]
+    first, kept = state
+    first = after(first, *earlier)
     held = [kept[half].astype(F32) + first[half].astype(F32) for half in range(2)]
-    last = [swap(held[half][1].astype(BF), 2 - half, size) for half in range(2)]
+    sent = [held[half][1].astype(BF) for half in range(2)]
+    last = [swap(sent[half], 2 - half, size) for half in range(2)]
     total = [held[half][0] + last[half].astype(F32) for half in range(2)]
-    return jnp.concatenate(total, axis=1), first, last, kept[0]
-
-
-def input_kernel(
-    place_ref,
-    mine_ref,
-    other_ref,
-    hidden_ref,
-    mid_ref,
-    gain_ref,
-    *refs,
-):
+    return jnp.concatenate(total, axis=1), sent, last
+
+
+def input_kernel(picks, sizes, place_ref, hidden_ref, mid_ref, gain_ref, *refs):
     lower = place_ref[2] == 0
     out_ref = refs[-1]
+    heads_picks, mine_picks, other_picks = picks
+    heads_size, weights_size = sizes
     parts = []
-    for weights in (mine_ref, other_ref):
-        total, start = None, 0
-        for heads_ref in refs[:-1]:
-            stop = start + heads_ref.shape[2]
-            for at in range(heads_ref.shape[0]):
-                part = last_dims(heads_ref[at], weights[at, :, start:stop])
+    for weights_picks in (mine_picks, other_picks):
+        total = None
+        for half, parts_of in enumerate(weights_picks):
+            start = half * weights_size
+            heads_of = heads_picks[start // heads_size]
+            start = start % heads_size
+            for (head, row), (weight, place) in zip(heads_of, parts_of):
+                left = refs[head][row, :, start : start + weights_size]
+                part = last_dims(left, refs[weight][place])
                 total = part if total is None else total + part
-            start = stop
         parts.append(total)
     grad = jnp.concatenate(
         [jnp.where(lower, parts[0], parts[1]), jnp.where(lower, parts[1], parts[0])], axis=1
@@ -518,27 +579,33 @@
     )
 
 
-def input_gradient(place, heads, halves, hidden_in, grad_mid, gain, size):
+def input_gradient(place, heads, mine, other, hidden_in, grad_mid, gain, size):
     length, width = hidden_in.shape
-    wide = halves[0].shape[2]
     rows = length // size
-    half = pl.BlockSpec((size, width // 2, wide), lambda r, place: (0, 0, 0))
+    arrays, picks = [], []
+    for group in (heads, mine, other):
+        more, at = arrays_of(group)
+        picks.append([[(len(arrays) + array, index) for array, index in part] for part in at])
+        arrays += more
+        if group is heads:
+            count = len(arrays)
+    sizes = (heads[0][0][0].shape[2], mine[0][0][0].shape[2])
+    wide = sum(part[0][0].shape[2] for part in heads)
     return pl.pallas_call(
-        input_kernel,
+        functools.partial(input_kernel, picks, sizes),
         grid_spec=pltpu.PrefetchScalarGridSpec(
             num_scalar_prefetch=1,
             grid=(size,),
             in_specs=[
-                half,
-                half,
                 pl.BlockSpec((rows, width), lambda r, place: (r, 0)),
                 pl.BlockSpec((rows, width), lambda r, place: (r ^ place[0], 0)),
                 pl.BlockSpec((1, width), lambda r, place: (0, 0)),
             ]
             + [
-                pl.BlockSpec((size, rows, part.shape[2]), lambda r, place: (0, r, 0))
-                for part in heads
-            ],
+                pl.BlockSpec((array.shape[0], rows, array.shape[2]), lambda r, place: (0, r, 0))
+                for array in arrays[:count]
+            ]
+            + [pl.BlockSpec(array.shape, lambda r, place: (0, 0, 0)) for array in arrays[count:]],
             out_specs=pl.BlockSpec((rows, width), lambda r, place: (r, 0)),
         ),
         out_shape=jax.ShapeDtypeStruct((length, width), F32),
@@ -548,7 +615,7 @@
             bytes_accessed=2 * size * wide * (length + width) + 8 * length * width,
             transcendentals=length,
         ),
-    )(place, *halves, hidden_in, grad_mid, gain[None], *heads)
+    )(place, hidden_in, grad_mid, gain[None], *arrays)
 
 
 def local(
@@ -614,16 +681,18 @@
     queries, keys, values, attended_low, attended_flip = attend_forward(
         place, normed, kv_normed, w_heads, cosine, sine, size
     )
-    mid_sum, _, _, _ = product_scatter([(attended_low, w_heads, 3)], size, width)
+    state, _, _, _ = scatter_start([(attended_low, w_heads, 3)], size, width)
+    mid_sum, _, _ = scatter_end(state, size, width)
     mid = hidden_own + mid_sum
     m_inverse, m_normed = rms_scale(mid, ffn_scale)
-    ffn_in, _, ffn_last = gather_rows(m_normed.astype(BF), size)
-    ffn_in = ffn_in.reshape(length, width)
+    held, _ = halves_start(m_normed.astype(BF), size)
+    parts, ffn_last = halves_end(held, size)
+    still = jnp.zeros((1,), jnp.int32)
+    ffn_in = assemble(parts, still, BF)
 
     half_rows = lax.dynamic_slice_in_dim(w_heads[:, :wide], core * (width // 2), width // 2, 0)
-    query_half, query_first, query_last = gather_rows(after(half_rows, *ffn_last), size)
-    query_other = lax.ppermute(query_half, "dp", [(i, i ^ 1) for i in range(dp_size)])
-    query_halves = (query_half, query_other)
+    held, _ = halves_start(after(half_rows, *ffn_last), size)
+    query_mine, query_last = halves_end(held, size)
 
     act_early, gate_early, up_early, flip_early = feed_forward(ffn_in, grad_y_low, w_early)
 
@@ -635,7 +704,7 @@
     act_late, gate_late, up_late, flip_late = feed_forward(
         after(ffn_in, grads_early), grad_y_low, w_late
     )
-    back_sum, _, _, _ = product_scatter(
+    state, _, _, _ = scatter_start(
         [
             (gate_early, w_early, 0),
             (up_early, w_early, 1),
@@ -645,22 +714,26 @@
         size,
         width,
     )
+    back_sum, _, _ = scatter_end(state, size, width)
     mid_part = norm_back(back_sum, mid, m_inverse, ffn_scale)
     grad_mid = grad_y + mid_part
     mid_low = grad_mid.astype(BF)
-    grad_mid_low, mid_first, mid_last = gather_rows(mid_low, size)
-    grad_mid_low = grad_mid_low.reshape(length, width)
+    held, mid_first = halves_start(mid_low, size)
+    parts, mid_last = halves_end(held, size)
+    grad_mid_low = assemble(parts, still, BF)
     act_early, act_late = after((act_early, act_late), *mid_first)
-    out_sum, out_first, out_last, out_done = product_scatter(
+    out_state, _, out_first, out_kept = scatter_start(
         [(act_early, w_early, 2), (act_late, w_late, 2)], size, width, free=mid_last
     )
     grads_late = unit_grads(after(flip_late, mid_low))
-    sum_late = lax.psum_scatter(after(grads_late, *mid_first), "dp", scatter_dimension=1, tiled=True)
-    grad_mid_low = after(grad_mid_low, grads_late, out_done)
+    sum_late = lax.psum_scatter(
+        after(grads_late, *mid_first), "dp", scatter_dimension=1, tiled=True
+    )
+    grad_mid_low = after(grad_mid_low, grads_late, *out_kept)
 
     group = head_group(wide)
     groups = wide // group
-    backs, heads_q, q_first, q_last = [], [], [], []
+    backs, heads_held, q_first = [], [], []
     grad_in = grad_mid_low
     for at in range(groups):
         backs.append(
@@ -668,45 +741,39 @@
                 place, grad_in, w_heads, queries, keys, values, cosine, sine, size, at
             )
         )
-        part, first, last = gather_part(backs[-1][0], size, at % 2)
-        heads_q.append(jnp.stack(part))
+        held, first = gather_start(backs[-1][0], size, at % 2)
+        heads_held.append(held)
         q_first.append(first)
-        q_last.append(last)
         grad_in = after(grad_mid_low, backs[-1][0])
     kv_terms = [(backs[at][1], w_heads, at + groups) for at in range(groups)]
     kv_terms += [(backs[at][2], w_heads, at + 2 * groups) for at in range(groups)]
     lefts = after([left for left, _, _ in kv_terms], *out_first, *q_first[:-1])
     kv_terms = [(left, right, at) for left, (_, right, at) in zip(lefts, kv_terms)]
-    grad_kv_normed, kv_first, kv_last, kv_done = product_scatter(
-        kv_terms, size, width, earlier=(q_first[-1], *out_last)
-    )
-    layer_own = after((mid + out_sum).astype(BF), *kv_first)
-    layer_rows, layer_first, _ = gather_rows(layer_own, size)
-    layer_out = absolute(layer_rows, me)
+    kv_state, kv_sent, kv_first, kv_kept = scatter_start(
+        kv_terms, size, width, earlier=q_first[-1:]
+    )
+    grad_kv_normed, kv_more, kv_last = scatter_end(kv_state, size, width)
+    heads_q, q_last = [], []
+    for at in range(groups):
+        parts, last = gather_end(heads_held[at], size, at % 2, kv_more)
+        heads_q.append(parts)
+        q_last.append(last)
+    out_sum, out_more, out_last = scatter_end(out_state, size, width, kv_more)
+    layer_own = (mid + out_sum).astype(BF)
+    layer_held, layer_first = halves_start(layer_own, size)
+    layer_parts, _ = halves_end(layer_held, size)
+    layer_out = assemble(layer_parts, place, BF)
     grads_heads = products(
         [(backs[at][3], lead, min(lead, 1)) for lead in range(3) for at in range(groups)]
         + [(attended_flip[None], 0, 2)],
-        [after(normed, kv_done), kv_normed, after(grad_mid_low, sum_early)],
-    )
-    grads_heads = after(grads_heads, *kv_first, *q_last[:-1])
+        [after(normed, kv_kept[0]), kv_normed, after(grad_mid_low, sum_early)],
+    )
+    grads_heads = after(grads_heads, *kv_first)
     sum_heads = lax.psum_scatter(grads_heads, "dp", scatter_dimension=1, tiled=True).astype(F32)
-    s_part = norm_back(grad_kv_normed, self_own, own_rows(s_inverse), kv_scale)
-    self_rows, self_first, _ = gather_rows(s_part.astype(BF), size)
-    self_grad = absolute(self_rows, me).astype(F32)
-    heads_q[0] = after(heads_q[0], *self_first, *layer_first)
-    input_grad = input_gradient(
-        place, heads_q, query_halves, hidden_in, grad_mid_low, attn_scale, size
-    )
-
     def unit_sums(at):
         early_rows = sum_early[at * early : (at + 1) * early]
         late_rows = sum_late[at * late : at * late + units - early]
         return jnp.concatenate([early_rows, late_rows], axis=0).astype(F32)
-
-    sum_query, sum_key, sum_value = [
-        sum_heads[at * wide : (at + 1) * wide].T for at in range(3)
-    ]
-    sum_gate, sum_up = unit_sums(0).T, unit_sums(1).T
 
     def gain_part(gain, *pairs):
         total = 0.0
@@ -714,13 +781,43 @@
             total = total + jnp.sum(weights.astype(F32) * grads, axis=1)
         return total / gain.astype(F32)
 
+    s_part = norm_back(grad_kv_normed, self_own, own_rows(s_inverse), kv_scale)
+    self_own_grad = s_part.astype(BF)
+    self_held, self_first = halves_start(self_own_grad, size)
+
+    weights_in = after((w_gate, w_up), *self_first)
+    sum_gate, sum_up, sum_down = unit_sums(0).T, unit_sums(1).T, unit_sums(2)
+    ffn_gain_sum = gain_part(ffn_gain, (weights_in[0], sum_gate), (weights_in[1], sum_up))
+
+    query_arrays, query_picks = arrays_of(query_mine)
+    other_arrays = [
+        lax.ppermute(array, "dp", [(i, i ^ 1) for i in range(dp_size)])
+        for array in after(query_arrays, *kv_more)
+    ]
+    query_other = [[(other_arrays[at], index) for at, index in part] for part in query_picks]
+    input_grad = input_gradient(
+        place,
+        heads_q,
+        query_mine,
+        query_other,
+        after(hidden_in, self_own_grad),
+        grad_mid_low,
+        attn_scale,
+        size,
+    )
+    self_parts, _ = halves_end(self_held, size, [input_grad])
+    weights_in = after((w_query, w_key, w_value), *self_first)
+    sum_query, sum_key, sum_value = [
+        sum_heads[at * wide : (at + 1) * wide].T for at in range(3)
+    ]
     gain_sums = jnp.stack(
         [
-            gain_part(attn_gain, (w_query, sum_query)),
-            gain_part(ffn_gain, (w_gate, sum_gate), (w_up, sum_up)),
-            gain_part(kv_gain, (w_key, sum_key), (w_value, sum_value)),
+            gain_part(attn_gain, (weights_in[0], sum_query)),
+            ffn_gain_sum,
+            gain_part(kv_gain, (weights_in[1], sum_key), (weights_in[2], sum_value)),
         ]
     )
+    self_grad = assemble(self_parts, after(place, gain_sums), F32)
     others = [
         lax.ppermute(gain_sums, "tensor", [(t, t ^ step) for t in range(size)])
         for step in range(1, size)
@@ -738,7 +835,7 @@
         sum_heads[3 * wide :],
         sum_gate,
         sum_up,
-        unit_sums(2),
+        sum_down,
         gain_sums[0],
         gain_sums[1],
         gain_sums[2],

time: 621 us -> 592 us (0.953)
  local copies, waits for them, and re-layouts: 50.8 us -> 27.3 us
  Pallas kernels: 223 us -> 241 us
  other arithmetic: 76.7 us -> 59.2 us
  waiting for transfers between devices: 186 us -> 179 us
    pallas_call x9 -> x13, Pallas kernels: 84.7 us -> 103 us  [the longest x8 64.3 us: row_products(): pl.pallas_call(functools.partial(rows_kernel, len(terms), steps), grid=(2...]
    squeeze x12 -> x0, local copies, waits for them, and re-layouts: 12.9 us -> none  [the longest x10 11.7 us: gather_part(): held[place ^ bit] = came[-1][at]]
    unnamed x148 -> x125, local copies, waits for them, and re-layouts: 24.5 us -> 12.9 us
    another operation x36 -> x13, other arithmetic: 26.8 us -> 16.5 us  [the longest x12 16.5 us: gather_step(): sent = jnp.stack([held[place][0][held[place][1]] for place in places])]
    ppermute x40, waiting for transfers between devices: 131 us -> 125 us  [swap(): return lax.ppermute(array, 'tensor', [(t, t ^ bit) for t in range(size)])]
  transfers between devices with their start and end apart: 50 -> 55, of which waited for: 21 -> 26; matrix products, arithmetic and copies ran while one was open for 17% -> 12% of each run, Pallas kernels for 36% -> 41%
where the time goes in v4:
time: 592 us; the launch traced here: 585 us
  Pallas kernels  241 us (41%)
  waiting for transfers between devices  179 us (30%)
  other arithmetic  59.2 us (10%)
  starting transfers between devices  48.4 us (8%)
  local copies, waits for them, and re-layouts  27.3 us (5%)
  between operations  16.1 us (3%)
  blocking collectives  14.5 us (2%)
    ppermute x40, waiting for transfers between devices, swap(): return lax.ppermute(array, 'tensor', [(t, t ^ bit) for t in range(size)])  125 us
    pallas_call x8, Pallas kernels, row_products(): pl.pallas_call(functools.partial(rows_kernel, len(terms), steps), grid=(2...  64.3 us
    all_gather x3, waiting for transfers between devices, local(): lax.all_gather(w, 'dp', axis=0, tiled=True)  54.5 us
    pallas_call x3, Pallas kernels, products(): pl.pallas_call(functools.partial(products_kernel, counts), grid=(total,),...  51.7 us
    ppermute x40, starting transfers between devices, swap(): return lax.ppermute(array, 'tensor', [(t, t ^ bit) for t in range(size)])  44.6 us
    pallas_call x2, Pallas kernels, feed_forward(): pl.pallas_call(feed_kernel, grid=(steps,), in_specs=[whole, whole, pl.Blo...  35.3 us
    pallas_call x2, Pallas kernels, attend_backward(): pl.pallas_call(functools.partial(backward_kernel, size), grid=(1,), in_sp...  25.4 us
    pallas_call x1, Pallas kernels, attend_forward(): pl.pallas_call(functools.partial(forward_kernel, size), grid=(groups,), i...  24.8 us
  transfers between devices with their start and end apart: 55, of which 26 were waited for; matrix products, arithmetic and copies ran while one was open for 12% of the time, Pallas kernels for 41%

profile of v4, /device:TPU:0, one launch (start us, length us, event | category | flops | bytes accessed | tf_op | source)
XLA Modules:
  0.0 585.5 jit_solution(4500838246228752558)
XLA Ops:
  14.4 14.5 %all_gather.12 = bf16[3,2048]{1,0:T(4,128)(2,1)S(1)} all-gather(bf16[3,256]{1,0:T(4,128)(2,1)S(1)} %pad_maximum_fusion.18), channel_id=1, replica_groups=mesh['dp'=8,'tensor'=4] {'dp'}, dimensions={1}, use_global_device_ids=true | all-gather | bytes 13824 | tf_op jit(solution)/shard_map/all_gather | solution.py:657
  41.1 54.5 %all-gather.4.cloned.1.call-done.wq_ref.wk_ref.wv_ref.refs_2_.wo_ref.refs_8_.refs_9_.refs_10_.refs_11_ = bf16[2048,2048]{1,0:T(8,128)(2,1)} async-done(((bf16[256,2048]{1,0:T(8,128)(2,1)}), bf16[2048,2048]{1,0:T(8,128)(2,1)}) %all-gather.4.cloned.1.call-update) | async-done | bytes 8388624 | tf_op jit(solution)/shard_map/all_gather | solution.py:656
  95.6 24.8 %shard_map.237 = (bf16[1024,512]{1,0:T(8,128)(2,1)}, bf16[1024,512]{1,0:T(8,128)(2,1)}, bf16[1024,512]{1,0:T(8,128)(2,1)}, bf16[1024,512]{1,0:T(8,128)(2,1)}, bf16[512,1024]{1,0:T(8,128)(2,1)}) custom-call(s32[3]{0:T(128)} %pad_add_fusion.place_ref.shift_ref, bf16[1024,2048]{1,0:T(8,128)(2,1)} %get-tuple-element.183.normed_ref.refs_7_, ...), custom_call_target="tpu_custom_call" | custom-call | flops 8053063680 | bytes 18874368 | tf_op jit(solution)/shard_map/pallas_call | solution.py:114
  135.6 15.7 %collective-permute-done.1 = bf16[2,256,1024]{2,1,0:T(8,128)(2,1)S(1)} collective-permute-done((bf16[2,256,1024]{2,1,0:T(8,128)(2,1)}, bf16[2,256,1024]{2,1,0:T(8,128)(2,1)S(1)}, u32[]{:S(2)}, u32[]{:S(2)}) %collective-permute-start.1) | collective-permute-done | bytes 1048608 | tf_op jit(solution)/shard_map/ppermute | solution.py:413
  159.5 9.3 %collective-permute-done.2 = bf16[256,1024]{1,0:T(8,128)(2,1)} collective-permute-done((bf16[256,1024]{1,0:T(8,128)(2,1)}, bf16[256,1024]{1,0:T(8,128)(2,1)}, u32[]{:S(2)}, u32[]{:S(2)}) %collective-permute-start.2) | collective-permute-done | bytes 524320 | tf_op jit(solution)/shard_map/ppermute | solution.py:413
  176.7 8.8 %collective-permute-done.6.refs_4_ = bf16[1,256,1024]{2,1,0:T(8,128)(2,1)S(1)} collective-permute-done((bf16[1,256,1024]{2,1,0:T(8,128)(2,1)S(1)}, bf16[1,256,1024]{2,1,0:T(8,128)(2,1)S(1)}, u32[]{:S(2)}, u32[]{:S(2)}) %collective-permute-start.6) | collective-permute-done | bytes 524320 | tf_op jit(solution)/shard_map/ppermute | solution.py:413
  196.7 13.8 %collective-permute-done.5.refs_1_ = bf16[2,256,1024]{2,1,0:T(8,128)(2,1)} collective-permute-done((bf16[2,256,1024]{2,1,0:T(8,128)(2,1)}, bf16[2,256,1024]{2,1,0:T(8,128)(2,1)}, u32[]{:S(2)}, u32[]{:S(2)}) %collective-permute-start.5) | collective-permute-done | bytes 1048608 | tf_op jit(solution)/shard_map/ppermute | solution.py:413
  227.5 21.6 %shard_map.241 = (bf16[1024,1024]{1,0:T(8,128)(2,1)}, bf16[1024,1024]{1,0:T(8,128)(2,1)}, bf16[1024,1024]{1,0:T(8,128)(2,1)}, bf16[3,1024,1024]{2,1,0:T(8,128)(2,1)}) custom-call(bf16[1024,2048]{1,0:T(8,128)(2,1)} %shard_map.240.x_ref.refs_3_, bf16[1024,2048]{1,0:T(8,128)(2,1)} %bitcast.115, ...), custom_call_target="tpu_custom_call" | custom-call | flops 12884901888 | bytes 33554432 | tf_op jit(solution)/shard_map/pallas_call | solution.py:275
  249.1 21.1 %shard_map.242 = bf16[3072,2048]{1,0:T(8,128)(2,1)} custom-call(bf16[3,1024,1024]{2,1,0:T(8,128)(2,1)} %get-tuple-element.113.refs_0_.refs_1_.refs_2_, bf16[3,1024,1024]{2,1,0:T(8,128)(2,1)} %get-tuple-element.113.refs_0_.refs_1_.refs_2_, bf16[3,1024,1024]{2,1,0:T(8,128)(2,1)} %get-tuple-element.113.refs_0_.refs_1_.refs_2_, ...), custom_call_target="tpu_custom_call" | custom-call | flops 12884901888 | bytes 27262976 | tf_op jit(solution)/shard_map/pallas_call | solution.py:324
  270.2 13.7 %shard_map.243 = (bf16[1024,384]{1,0:T(8,128)(2,1)}, bf16[1024,384]{1,0:T(8,128)(2,1)}, bf16[1024,384]{1,0:T(8,128)(2,1)}, bf16[3,384,1024]{2,1,0:T(8,128)(2,1)}) custom-call(bf16[1024,2048]{1,0:T(8,128)(2,1)} %shard_map.240.x_ref.refs_3_, bf16[1024,2048]{1,0:T(8,128)(2,1)} %bitcast.117, ...), custom_call_target="tpu_custom_call" | custom-call | flops 4831838208 | bytes 17825792 | tf_op jit(solution)/shard_map/pallas_call | solution.py:275
  283.9 12.0 %shard_map.244 = (bf16[2,256,1024]{2,1,0:T(8,128)(2,1)}, bf16[2,256,1024]{2,1,0:T(8,128)(2,1)}) custom-call(bf16[1024,1024]{1,0:T(8,128)(2,1)} %get-tuple-element.122.refs_0_.refs_1_, bf16[1024,1024]{1,0:T(8,128)(2,1)} %get-tuple-element.122.refs_0_.refs_1_, bf16[1024,1024]{1,0:T(8,128)(2,1)} %get-tuple-element.123.refs_2_.refs_3_, ...), custom_call_target="tpu_custom_call" | custom-call | flops 5905580032 | bytes 19398656 | tf_op jit(solution)/shard_map/pallas_call | solution.py:373
  299.5 12.2 %shard_map.245 = (bf16[2,256,1024]{2,1,0:T(8,128)(2,1)}, bf16[2,256,1024]{2,1,0:T(8,128)(2,1)}) custom-call(bf16[1024,1024]{1,0:T(8,128)(2,1)} %get-tuple-element.122.refs_0_.refs_1_, bf16[1024,1024]{1,0:T(8,128)(2,1)} %get-tuple-element.122.refs_0_.refs_1_, bf16[1024,1024]{1,0:T(8,128)(2,1)} %get-tuple-element.123.refs_2_.refs_3_, ...), custom_call_target="tpu_custom_call" | custom-call | flops 5905580032 | bytes 19398656 | tf_op jit(solution)/shard_map/pallas_call | solution.py:373
  323.1 8.1 %collective-permute-done.10 = bf16[256,1024]{1,0:T(8,128)(2,1)S(1)} collective-permute-done((bf16[256,1024]{1,0:T(8,128)(2,1)S(1)}, bf16[256,1024]{1,0:T(8,128)(2,1)S(1)}, u32[]{:S(2)}, u32[]{:S(2)}) %collective-permute-start.10) | collective-permute-done | bytes 524320 | tf_op jit(solution)/shard_map/ppermute | solution.py:413
  338.7 12.7 %shard_map.249 = bf16[1152,2048]{1,0:T(8,128)(2,1)} custom-call(bf16[3,384,1024]{2,1,0:T(8,128)(2,1)} %get-tuple-element.141.refs_0_.refs_1_.refs_2_, bf16[3,384,1024]{2,1,0:T(8,128)(2,1)} %get-tuple-element.141.refs_0_.refs_1_.refs_2_, bf16[3,384,1024]{2,1,0:T(8,128)(2,1)} %get-tuple-element.141.refs_0_.refs_1_.refs_2_, ...), custom_call_target="tpu_custom_call" | custom-call | flops 4831838208 | bytes 15466496 | tf_op jit(solution)/shard_map/pallas_call | solution.py:324
  357.4 7.7 %shard_map.246 = (bf16[2,256,1024]{2,1,0:T(8,128)(2,1)}, bf16[2,256,1024]{2,1,0:T(8,128)(2,1)}) custom-call(bf16[1024,1024]{1,0:T(8,128)(2,1)} %get-tuple-element.134.refs_0_.refs_1_, bf16[1024,1024]{1,0:T(8,128)(2,1)} %get-tuple-element.134.refs_0_.refs_1_, bf16[1024,384]{1,0:T(8,128)(2,1)} %get-tuple-element.135.refs_2_.refs_3_, ...), custom_call_target="tpu_custom_call" | custom-call | flops 2952790016 | bytes 10747904 | tf_op jit(solution)/shard_map/pallas_call | solution.py:373
  365.1 7.9 %shard_map.247 = (bf16[2,256,1024]{2,1,0:T(8,128)(2,1)}, bf16[2,256,1024]{2,1,0:T(8,128)(2,1)}) custom-call(bf16[1024,1024]{1,0:T(8,128)(2,1)} %get-tuple-element.134.refs_0_.refs_1_, bf16[1024,1024]{1,0:T(8,128)(2,1)} %get-tuple-element.134.refs_0_.refs_1_, bf16[1024,384]{1,0:T(8,128)(2,1)} %get-tuple-element.135.refs_2_.refs_3_, ...), custom_call_target="tpu_custom_call" | custom-call | flops 2952790016 | bytes 10747904 | tf_op jit(solution)/shard_map/pallas_call | solution.py:373
  387.1 12.6 %shard_map.250 = (bf16[1024,256]{1,0:T(8,128)(2,1)}, bf16[1024,256]{1,0:T(8,128)(2,1)}, bf16[1024,256]{1,0:T(8,128)(2,1)}, bf16[3,256,1024]{2,1,0:T(8,128)(2,1)}) custom-call(s32[3]{0:T(128)} %pad_add_fusion.place_ref.shift_ref, bf16[1024,2048]{1,0:T(8,128)(2,1)} %shard_map.248.grad_ref.mid_ref.refs_9_, ...), custom_call_target="tpu_custom_call" | custom-call | flops 3758096384 | bytes 9961472 | tf_op jit(solution)/shard_map/pallas_call | solution.py:221
  400.3 12.8 %shard_map.251 = (bf16[1024,256]{1,0:T(8,128)(2,1)}, bf16[1024,256]{1,0:T(8,128)(2,1)}, bf16[1024,256]{1,0:T(8,128)(2,1)}, bf16[3,256,1024]{2,1,0:T(8,128)(2,1)}) custom-call(s32[3]{0:T(128)} %pad_add_fusion.place_ref.shift_ref, bf16[1024,2048]{1,0:T(8,128)(2,1)} %shard_map.248.grad_ref.mid_ref.refs_9_, ...), custom_call_target="tpu_custom_call" | custom-call | flops 3758096384 | bytes 9961472 | tf_op jit(solution)/shard_map/pallas_call | solution.py:221
  414.5 6.8 %shard_map.252 = (bf16[2,256,1024]{2,1,0:T(8,128)(2,1)}, bf16[2,256,1024]{2,1,0:T(8,128)(2,1)}) custom-call(bf16[1024,256]{1,0:T(8,128)(2,1)} %get-tuple-element.159.refs_0_.refs_1_, bf16[1024,256]{1,0:T(8,128)(2,1)} %get-tuple-element.159.refs_0_.refs_1_, bf16[1024,256]{1,0:T(8,128)(2,1)} %get-tuple-element.160.refs_2_.refs_3_, ...), custom_call_target="tpu_custom_call" | custom-call | flops 2147483648 | bytes 8388608 | tf_op jit(solution)/shard_map/pallas_call | solution.py:373
  423.4 6.7 %shard_map.253 = (bf16[2,256,1024]{2,1,0:T(8,128)(2,1)}, bf16[2,256,1024]{2,1,0:T(8,128)(2,1)}) custom-call(bf16[1024,256]{1,0:T(8,128)(2,1)} %get-tuple-element.159.refs_0_.refs_1_, bf16[1024,256]{1,0:T(8,128)(2,1)} %get-tuple-element.159.refs_0_.refs_1_, bf16[1024,256]{1,0:T(8,128)(2,1)} %get-tuple-element.160.refs_2_.refs_3_, ...), custom_call_target="tpu_custom_call" | custom-call | flops 2147483648 | bytes 8388608 | tf_op jit(solution)/shard_map/pallas_call | solution.py:373
  430.2 17.9 %shard_map.256 = bf16[2048,2048]{1,0:T(8,128)(2,1)} custom-call(bf16[3,256,1024]{2,1,0:T(8,128)(2,1)} %get-tuple-element.180.refs_0_.refs_2_.refs_4_, bf16[3,256,1024]{2,1,0:T(8,128)(2,1)} %get-tuple-element.181.refs_1_.refs_3_.refs_5_, bf16[3,256,1024]{2,1,0:T(8,128)(2,1)} %get-tuple-element.180.refs_0_.refs_2_.refs_4_, ...), custom_call_target="tpu_custom_call" | custom-call | flops 8589934592 | bytes 25165824 | tf_op jit(solution)/shard_map/pallas_call | solution.py:324
  486.2 8.2 %collective-permute-done.42.refs_2_ = bf16[1,256,1024]{2,1,0:T(8,128)(2,1)S(1)} collective-permute-done((bf16[1,256,1024]{2,1,0:T(8,128)(2,1)S(1)}, bf16[1,256,1024]{2,1,0:T(8,128)(2,1)S(1)}, u32[]{:S(2)}, u32[]{:S(2)}) %collective-permute-start.42) | collective-permute-done | bytes 524320 | tf_op jit(solution)/shard_map/ppermute | solution.py:413
  494.3 21.2 %collective-permute-done.43.refs_4_ = bf16[1,256,1024]{2,1,0:T(8,128)(2,1)S(1)} collective-permute-done((bf16[1,256,1024]{2,1,0:T(8,128)(2,1)S(1)}, bf16[1,256,1024]{2,1,0:T(8,128)(2,1)S(1)}, u32[]{:S(2)}, u32[]{:S(2)}) %collective-permute-start.43) | collective-permute-done | bytes 524320 | tf_op jit(solution)/shard_map/ppermute | solution.py:413
  525.3 18.6 %shard_map.255 = f32[1024,2048]{1,0:T(8,128)} custom-call(s32[3]{0:T(128)} %pad_add_fusion.place_ref.shift_ref, bf16[1024,2048]{1,0:T(8,128)(2,1)} %hidden_ref, bf16[1024,2048]{1,0:T(8,128)(2,1)} %shard_map.248.grad_ref.mid_ref.refs_9_, f32[1,2048]{1,0:T(1,128)} %copy-done.47, bf16[1,1024,256]{2,1,0:T(8,128)(2,1)} %bitcast.123, ...), custom_call_target="tpu_custom_call" | custom-call | flops 8589934592 | bytes 29360128 | tf_op jit(solution)/shard_map/pallas_call | solution.py:594
  (344 shorter events, 206.4 us)
Async XLA Ops:
  7.2 88.4 %all-gather.4.cloned.1.call-start = ((), (), s32[]{:S(2)}) async-start(), calls=%async_computation.3 | async-start | bytes 9437184 | tf_op jit(solution)/shard_map/all_gather | solution.py:656
  10.6 216.9 %all-gather.6.cloned.1.call-start = ((), (), s32[]{:S(2)}) async-start(), calls=%async_computation.4 | async-start | bytes 14155776 | tf_op jit(solution)/shard_map/all_gather | solution.py:656
  13.6 256.5 %all-gather.8.cloned.1.call-start = ((), (), s32[]{:S(2)}) async-start(), calls=%async_computation.5 | async-start | bytes 5308416 | tf_op jit(solution)/shard_map/all_gather | solution.py:656
  125.8 25.5 %collective-permute-start.1 = (bf16[2,256,1024]{2,1,0:T(8,128)(2,1)}, bf16[2,256,1024]{2,1,0:T(8,128)(2,1)S(1)}, u32[]{:S(2)}, u32[]{:S(2)}) collective-permute-start(bf16[2,256,1024]{2,1,0:T(8,128)(2,1)} %get-tuple-element.106), channel_id=1, source_target_pairs={{0,2},{1,3},{2,0},{3,1},{4,6},{5,7},{6,4},{7,5},{8,10},{9,11},{10,... | collective-permute-start | bytes 3145736 | tf_op jit(solution)/shard_map/ppermute | solution.py:413
  127.3 25.3 %collective-permute-start = (bf16[2,256,1024]{2,1,0:T(8,128)(2,1)}, bf16[2,256,1024]{2,1,0:T(8,128)(2,1)}, u32[]{:S(2)}, u32[]{:S(2)}) collective-permute-start(bf16[2,256,1024]{2,1,0:T(8,128)(2,1)} %get-tuple-element.105), channel_id=1, source_target_pairs={{0,1},{1,0},{2,3},{3,2},{4,5},{5,4},{6,7},{7,6},{8,9},{9,8},{10,11... | collective-permute-start | bytes 3145736 | tf_op jit(solution)/shard_map/ppermute | solution.py:413
  130.1 300.1 %reduce-scatter.4.cloned.1.call-start = ((), (), s32[]{:S(2)}) async-start(), calls=%async_computation.6 | async-start | bytes 14155776 | tf_op jit(solution)/shard_map/reduce_scatter | solution.py:703
  189.4 23.2 %collective-permute-start.7 = (bf16[2,256,1024]{2,1,0:T(8,128)(2,1)}, bf16[2,256,1024]{2,1,0:T(8,128)(2,1)S(1)}, u32[]{:S(2)}, u32[]{:S(2)}) collective-permute-start(bf16[2,256,1024]{2,1,0:T(8,128)(2,1)} %pad_maximum_fusion.4), channel_id=1, source_target_pairs={{0,2},{1,3},{2,0},{3,1},{4,6},{5,7},{6,4},{7,5},{8,10},{9,11},{10,... | collective-permute-start | bytes 3145736 | tf_op jit(solution)/shard_map/ppermute | solution.py:413
  227.0 43.2 %collective-permute-start.33 = (bf16[2,1024,256]{2,1,0:T(8,128)(2,1)S(1)}, bf16[2,1024,256]{2,1,0:T(8,128)(2,1)}, u32[]{:S(2)}, u32[]{:S(2)}) collective-permute-start(bf16[2,1024,256]{2,1,0:T(8,128)(2,1)S(1)} %pad_maximum_fusion.11), channel_id=1, source_target_pairs={{0,1},{1,0},{2,3},{3,2},{4,5},{5,4},{6,7},{7,6},{8,9},{9,8},{10,11... | collective-permute-start | bytes 3145736 | tf_op jit(solution)/shard_map/ppermute | solution.py:413
  227.3 42.8 %collective-permute-start.35 = (bf16[2,1024,256]{2,1,0:T(8,128)(2,1)S(1)}, bf16[2,1024,256]{2,1,0:T(8,128)(2,1)}, u32[]{:S(2)}, u32[]{:S(2)}) collective-permute-start(bf16[2,1024,256]{2,1,0:T(8,128)(2,1)S(1)} %pad_maximum_fusion.12), channel_id=1, source_target_pairs={{0,2},{1,3},{2,0},{3,1},{4,6},{5,7},{6,4},{7,5},{8,10},{9,11},{10,... | collective-permute-start | bytes 3145736 | tf_op jit(solution)/shard_map/ppermute | solution.py:413
  270.2 284.0 %reduce-scatter.8.cloned.1.call-start = ((), (), s32[]{:S(2)}) async-start(), calls=%async_computation.8 | async-start | bytes 5308416 | tf_op jit(solution)/shard_map/reduce_scatter | solution.py:729
  351.5 207.8 %reduce-scatter.6.cloned.1.call-start = ((), (), s32[]{:S(2)}) async-start(), calls=%async_computation.7 | async-start | bytes 9437184 | tf_op jit(solution)/shard_map/reduce_scatter | solution.py:772
  378.2 36.3 %collective-permute-start.16 = (bf16[2,256,1024]{2,1,0:T(8,128)(2,1)}, bf16[2,256,1024]{2,1,0:T(8,128)(2,1)}, u32[]{:S(2)}, u32[]{:S(2)}) collective-permute-start(bf16[2,256,1024]{2,1,0:T(8,128)(2,1)} %get-tuple-element.138), channel_id=1, source_target_pairs={{0,1},{1,0},{2,3},{3,2},{4,5},{5,4},{6,7},{7,6},{8,9},{9,8},{10,11... | collective-permute-start | bytes 3145736 | tf_op jit(solution)/shard_map/ppermute | solution.py:413
  380.6 33.9 %collective-permute-start.17 = (bf16[2,256,1024]{2,1,0:T(8,128)(2,1)}, bf16[2,256,1024]{2,1,0:T(8,128)(2,1)}, u32[]{:S(2)}, u32[]{:S(2)}) collective-permute-start(bf16[2,256,1024]{2,1,0:T(8,128)(2,1)} %get-tuple-element.139), channel_id=1, source_target_pairs={{0,2},{1,3},{2,0},{3,1},{4,6},{5,7},{6,4},{7,5},{8,10},{9,11},{10,... | collective-permute-start | bytes 3145736 | tf_op jit(solution)/shard_map/ppermute | solution.py:413
  421.3 26.8 %collective-permute-start.21 = (bf16[2,256,1024]{2,1,0:T(8,128)(2,1)}, bf16[2,256,1024]{2,1,0:T(8,128)(2,1)S(1)}, u32[]{:S(2)}, u32[]{:S(2)}) collective-permute-start(bf16[2,256,1024]{2,1,0:T(8,128)(2,1)} %get-tuple-element.157), channel_id=1, source_target_pairs={{0,2},{1,3},{2,0},{3,1},{4,6},{5,7},{6,4},{7,5},{8,10},{9,11},{10,... | collective-permute-start | bytes 3145736 | tf_op jit(solution)/shard_map/ppermute | solution.py:413
  421.7 26.5 %collective-permute-start.20 = (bf16[2,256,1024]{2,1,0:T(8,128)(2,1)}, bf16[2,256,1024]{2,1,0:T(8,128)(2,1)}, u32[]{:S(2)}, u32[]{:S(2)}) collective-permute-start(bf16[2,256,1024]{2,1,0:T(8,128)(2,1)} %get-tuple-element.156), channel_id=1, source_target_pairs={{0,1},{1,0},{2,3},{3,2},{4,5},{5,4},{6,7},{7,6},{8,9},{9,8},{10,11... | collective-permute-start | bytes 3145736 | tf_op jit(solution)/shard_map/ppermute | solution.py:413
  477.2 46.6 %collective-permute-start.30 = (bf16[2,1024,256]{2,1,0:T(8,128)(2,1)}, bf16[2,1024,256]{2,1,0:T(8,128)(2,1)}, u32[]{:S(2)}, u32[]{:S(2)}) collective-permute-start(bf16[2,1024,256]{2,1,0:T(8,128)(2,1)} %pad_maximum_fusion.9), channel_id=1, source_target_pairs={{0,1},{1,0},{2,3},{3,2},{4,5},{5,4},{6,7},{7,6},{8,9},{9,8},{10,11... | collective-permute-start | bytes 3145736 | tf_op jit(solution)/shard_map/ppermute | solution.py:413
  477.6 37.9 %collective-permute-start.43 = (bf16[1,256,1024]{2,1,0:T(8,128)(2,1)S(1)}, bf16[1,256,1024]{2,1,0:T(8,128)(2,1)S(1)}, u32[]{:S(2)}, u32[]{:S(2)}) collective-permute-start(bf16[1,256,1024]{2,1,0:T(8,128)(2,1)S(1)} %get-tuple-element.240.refs_3_), channel_id=1, source_target_pairs={{0,1},{1,0},{2,3},{3,2},{4,5},{5,4},{6,7},{7,6},{8,9},{9,8},{10,11... | collective-permute-start | bytes 1572872 | tf_op jit(solution)/shard_map/ppermute | solution.py:413
  483.1 42.2 %collective-permute-start.31 = (bf16[2,1024,256]{2,1,0:T(8,128)(2,1)}, bf16[2,1024,256]{2,1,0:T(8,128)(2,1)}, u32[]{:S(2)}, u32[]{:S(2)}) collective-permute-start(bf16[2,1024,256]{2,1,0:T(8,128)(2,1)} %pad_maximum_fusion.10), channel_id=1, source_target_pairs={{0,2},{1,3},{2,0},{3,1},{4,6},{5,7},{6,4},{7,5},{8,10},{9,11},{10,... | collective-permute-start | bytes 3145736 | tf_op jit(solution)/shard_map/ppermute | solution.py:413
  486.2 39.1 %collective-permute-start.37 = (bf16[2,1024,256]{2,1,0:T(8,128)(2,1)}, bf16[2,1024,256]{2,1,0:T(8,128)(2,1)}, u32[]{:S(2)}, u32[]{:S(2)}) collective-permute-start(bf16[2,1024,256]{2,1,0:T(8,128)(2,1)} %collective-permute-done.33.refs_7_), channel_id=1, source_target_pairs={{0,4},{4,0},{8,12},{12,8},{16,20},{20,16},{24,28},{28,24},{1,5},{5... | collective-permute-start | bytes 3145736 | tf_op jit(solution)/shard_map/ppermute | solution.py:794
  494.3 31.0 %collective-permute-start.41 = (bf16[2,1024,256]{2,1,0:T(8,128)(2,1)}, bf16[2,1024,256]{2,1,0:T(8,128)(2,1)}, u32[]{:S(2)}, u32[]{:S(2)}) collective-permute-start(bf16[2,1024,256]{2,1,0:T(8,128)(2,1)} %collective-permute-done.35.refs_11_), channel_id=1, source_target_pairs={{0,4},{4,0},{8,12},{12,8},{16,20},{20,16},{24,28},{28,24},{1,5},{5... | collective-permute-start | bytes 3145736 | tf_op jit(solution)/shard_map/ppermute | solution.py:794
  522.4 26.0 %collective-permute-start.25 = (bf16[2,256,1024]{2,1,0:T(8,128)(2,1)}, bf16[2,256,1024]{2,1,0:T(8,128)(2,1)S(1)}, u32[]{:S(2)}, u32[]{:S(2)}) collective-permute-start(bf16[2,256,1024]{2,1,0:T(8,128)(2,1)} %pad_maximum_fusion.7), channel_id=1, source_target_pairs={{0,1},{1,0},{2,3},{3,2},{4,5},{5,4},{6,7},{7,6},{8,9},{9,8},{10,11... | collective-permute-start | bytes 3145736 | tf_op jit(solution)/shard_map/ppermute | solution.py:413
  523.8 25.5 %collective-permute-start.27 = (bf16[2,256,1024]{2,1,0:T(8,128)(2,1)}, bf16[2,256,1024]{2,1,0:T(8,128)(2,1)}, u32[]{:S(2)}, u32[]{:S(2)}) collective-permute-start(bf16[2,256,1024]{2,1,0:T(8,128)(2,1)} %pad_maximum_fusion.8), channel_id=1, source_target_pairs={{0,2},{1,3},{2,0},{3,1},{4,6},{5,7},{6,4},{7,5},{8,10},{9,11},{10,... | collective-permute-start | bytes 3145736 | tf_op jit(solution)/shard_map/ppermute | solution.py:413
  545.0 25.8 %collective-permute-start.44 = (bf16[2,256,1024]{2,1,0:T(8,128)(2,1)}, bf16[2,256,1024]{2,1,0:T(8,128)(2,1)}, u32[]{:S(2)}, u32[]{:S(2)}) collective-permute-start(bf16[2,256,1024]{2,1,0:T(8,128)(2,1)} %pad_maximum_fusion.13), channel_id=1, source_target_pairs={{0,1},{1,0},{2,3},{3,2},{4,5},{5,4},{6,7},{7,6},{8,9},{9,8},{10,11... | collective-permute-start | bytes 3145736 | tf_op jit(solution)/shard_map/ppermute | solution.py:413
  546.7 25.2 %collective-permute-start.45 = (bf16[2,256,1024]{2,1,0:T(8,128)(2,1)}, bf16[2,256,1024]{2,1,0:T(8,128)(2,1)}, u32[]{:S(2)}, u32[]{:S(2)}) collective-permute-start(bf16[2,256,1024]{2,1,0:T(8,128)(2,1)} %pad_maximum_fusion.14), channel_id=1, source_target_pairs={{0,2},{1,3},{2,0},{3,1},{4,6},{5,7},{6,4},{7,5},{8,10},{9,11},{10,... | collective-permute-start | bytes 3145736 | tf_op jit(solution)/shard_map/ppermute | solution.py:413
  (94 other events, 1145.7 us)
Sparse Core Ops, SparseCore 0:
  10.7 84.7 all-gather.3
  97.2 115.2 all-gather.5
  214.2 49.9 all-gather.7
  270.3 128.3 reduce-scatter.3
  400.9 53.3 reduce-scatter.7
  457.0 87.9 reduce-scatter.5

commit v5 on v4

--- a/solution.py
+++ b/solution.py
@@ -136,26 +136,20 @@
 
 
 def backward_kernel(
-    size,
+    picks,
     place_ref,
-    grad_ref,
     wo_ref,
     q_ref,
     k_ref,
     v_ref,
     cos_ref,
     sin_ref,
-    gq_ref,
-    rk_ref,
-    rv_ref,
-    flip_ref,
-    ga_ref,
-    kt_ref,
-    sum_k,
-    sum_v,
+    *refs,
 ):
+    gq_ref, rk_ref, rv_ref, flip_ref, ga_ref, kt_ref, sum_k, sum_v = refs[-8:]
     me, live = place_ref[0], place_ref[1]
-    length = grad_ref.shape[0]
+    length = q_ref.shape[0]
+    size = len(picks[0])
     group = wo_ref.shape[1]
     part = length // size
     scale = HD ** (-0.5)
@@ -166,9 +160,14 @@
         return pl.multiple_of(pl.multiple_of((block ^ me) * part, part) + row % part, 128)
 
     for block in range(size):
-        ga_ref[pl.ds(home(block * part), part), :] = plain_dot(
-            grad_ref[block * part : (block + 1) * part, :], wo_ref[...]
-        ).astype(BF)
+        total, start = None, 0
+        for half in picks:
+            array, index = half[block]
+            stop = start + refs[array].shape[2]
+            term = plain_dot(refs[array][index], wo_ref[start:stop, :])
+            total = term if total is None else total + term
+            start = stop
+        ga_ref[pl.ds(home(block * part), part), :] = total.astype(BF)
     for at in range(0, group, HD):
         kt_ref[...] = k_ref[:, at : at + HD].T
         for start in reversed(range(0, length, QROWS)):
@@ -209,9 +208,10 @@
             rv_ref[pl.ds(home(block * part), part), at : at + HD] = grad_v[rows]
 
 
-def attend_backward(place, grad_mid_low, weights, queries, keys, values, cosine, sine, size, at):
-    length, width = grad_mid_low.shape
-    wide = queries.shape[1]
+def attend_backward(place, grads, weights, queries, keys, values, cosine, sine, at):
+    arrays, picks = grads
+    length, wide = queries.shape
+    width = weights.shape[0]
     group = head_group(wide)
     groups = wide // group
     table = pl.BlockSpec((length, HD), lambda g: (0, 0))
@@ -219,18 +219,18 @@
     outs = pl.BlockSpec((length, group), lambda g: (0, 0))
     out = jax.ShapeDtypeStruct((length, group), BF)
     return pl.pallas_call(
-        functools.partial(backward_kernel, size),
+        functools.partial(backward_kernel, picks),
         grid=(1,),
         in_specs=[
             pl.BlockSpec(memory_space=pltpu.SMEM),
-            pl.BlockSpec((length, width), lambda g: (0, 0)),
             pl.BlockSpec((width, group), lambda g: (0, at + 3 * groups)),
             heads,
             heads,
             heads,
             table,
             table,
-        ],
+        ]
+        + [pl.BlockSpec(array.shape, lambda g: (0, 0, 0)) for array in arrays],
         out_specs=[outs] * 3 + [pl.BlockSpec((3, group, length), lambda g: (0, 0, 0))],
         out_shape=[out] * 3 + [jax.ShapeDtypeStruct((3, group, length), BF)],
         scratch_shapes=[
@@ -245,7 +245,7 @@
             bytes_accessed=2 * length * width + 2 * width * group + 18 * length * group,
             transcendentals=length * length * group // HD,
         ),
-    )(place, grad_mid_low, weights, queries, keys, values, cosine, sine)
+    )(place, weights, queries, keys, values, cosine, sine, *arrays)
 
 
 def feed_kernel(x_ref, g_ref, wg_ref, wu_ref, wd_ref, act_ref, gate_ref, up_ref, flip_ref):
@@ -294,24 +294,47 @@
     )(ffn_in, grad_low, weights, weights, weights)
 
 
-def products_kernel(counts, *refs):
+def products_kernel(counts, forms, *refs):
     step = pl.program_id(0)
     lefts, rights, out_ref = refs[: len(counts)], refs[len(counts) : -1], refs[-1]
     first = 0
     for (steps, right), left in zip(counts, lefts):
 
         @pl.when((step >= first) & (step < first + steps))
-        def _(left=left, right=right):
-            out_ref[...] = plain_dot(left[...], rights[right][...]).astype(BF)
+        def _(left=left, form=forms[right]):
+            if isinstance(form, int):
+                out_ref[...] = plain_dot(left[...], rights[form][...]).astype(BF)
+                return
+            start = 0
+            for half in form:
+                total = None
+                for place, (array, index) in enumerate(half):
+                    rows, columns = rights[array].shape[1:]
+                    part = plain_dot(
+                        left[:, place * rows : (place + 1) * rows], rights[array][index]
+                    )
+                    total = part if total is None else total + part
+                out_ref[:, start : start + columns] = total.astype(BF)
+                start += columns
 
         first += steps
 
 
 def products(terms, rights):
-    length, width = rights[0].shape
+    length = terms[0][0].shape[2]
+    width = rights[0].shape[1]
     step = 256 if all(left.shape[1] % 256 == 0 for left, _, _ in terms) else 128
     counts = tuple((left.shape[1] // step, at) for left, _, at in terms)
     total = sum(steps for steps, _ in counts)
+    arrays, forms = [], []
+    for right in rights:
+        if isinstance(right, tuple):
+            more, picks = right
+            forms.append([[(len(arrays) + at, index) for at, index in half] for half in picks])
+            arrays += more
+        else:
+            forms.append(len(arrays))
+            arrays.append(right)
     left_specs = []
     first = 0
     for (steps, _), (_, lead, _) in zip(counts, terms):
@@ -321,10 +344,13 @@
 
         left_specs.append(pl.BlockSpec((None, step, length), block))
         first += steps
+    right_specs = [
+        pl.BlockSpec(array.shape, lambda i, ndim=array.ndim: (0,) * ndim) for array in arrays
+    ]
     return pl.pallas_call(
-        functools.partial(products_kernel, counts),
+        functools.partial(products_kernel, counts, forms),
         grid=(total,),
-        in_specs=left_specs + [pl.BlockSpec((length, width), lambda i: (0, 0))] * len(rights),
+        in_specs=left_specs + right_specs,
         out_specs=pl.BlockSpec((step, width), lambda i: (i, 0)),
         out_shape=jax.ShapeDtypeStruct((total * step, width), BF),
         compiler_params=limits(),
@@ -333,24 +359,30 @@
             bytes_accessed=2 * (total * step * (length + width) + len(rights) * length * width),
             transcendentals=0,
         ),
-    )(*[left for left, _, _ in terms], *rights)
-
-
-def rows_kernel(count, steps, *refs):
-    lefts, rights, outs = refs[: 2 * count], refs[2 * count : -2], refs[-2:]
+    )(*[left for left, _, _ in terms], *arrays)
+
+
+def rows_kernel(count, sides, steps, *refs):
+    outs = refs[-2 * len(sides) :]
+    lefts, rights = refs[: -2 * len(sides) - count], refs[-2 * len(sides) - count : -2 * len(sides)]
     for half in range(2):
 
         @pl.when(pl.program_id(0) // steps == half)
         def _(half=half):
-            for piece in range(2):
-                total = None
-                for at, right in enumerate(rights):
-                    part = last_dims(lefts[2 * at + piece][...], right[...])
-                    total = part if total is None else total + part
-                outs[half][piece] = total.astype(BF)
-
-
-def row_products(terms, side, width):
+            for number, side in enumerate(sides):
+                for piece in range(2):
+                    if len(sides) == 1:
+                        row, parts = piece, 2
+                    else:
+                        row, parts = (2 * side + piece if half else 2 * piece + side), 4
+                    total = None
+                    for at, right in enumerate(rights):
+                        part = last_dims(lefts[parts * at + row][...], right[...])
+                        total = part if total is None else total + part
+                    outs[2 * number + half][piece] = total.astype(BF)
+
+
+def row_products(terms, sides, width):
     columns = width // 2
     step = 512 if columns % 512 == 0 else columns
     steps = columns // step
@@ -358,32 +390,38 @@
     flops = nbytes = 0
     for left, right, at in terms:
         rows, depth = left.shape[0] // 4, left.shape[1]
-        for piece in range(2):
+        for piece in range(2 * len(sides)):
 
             def block(j, piece=piece):
-                upper = j // steps
+                if len(sides) == 2:
+                    return (piece, 0)
+                upper, side = j // steps, sides[0]
                 return ((1 - upper) * (2 * piece + side) + upper * (2 * side + piece), 0)
 
             lefts.append(left)
             left_specs.append(pl.BlockSpec((rows, depth), block))
         right_specs.append(pl.BlockSpec((step, depth), lambda j, at=at: (j, at)))
         rights.append(right)
-        flops += 8 * rows * depth * columns
+        flops += 8 * rows * depth * columns * len(sides)
         nbytes += 4 * depth * (2 * rows + columns)
-    return pl.pallas_call(
-        functools.partial(rows_kernel, len(terms), steps),
+    outs = pl.pallas_call(
+        functools.partial(rows_kernel, len(terms), sides, steps),
         grid=(2 * steps,),
         in_specs=left_specs + right_specs,
         out_specs=[
             pl.BlockSpec((2, rows, step), lambda j: (0, 0, lax.min(j, steps - 1))),
             pl.BlockSpec((2, rows, step), lambda j: (0, 0, lax.max(j - steps, 0))),
-        ],
-        out_shape=[jax.ShapeDtypeStruct((2, rows, columns), BF)] * 2,
+        ]
+        * len(sides),
+        out_shape=[jax.ShapeDtypeStruct((2, rows, columns), BF)] * (2 * len(sides)),
         compiler_params=limits(),
         cost_estimate=estimate(
-            flops=flops, bytes_accessed=nbytes + 8 * rows * columns, transcendentals=0
+            flops=flops,
+            bytes_accessed=nbytes + 8 * rows * columns * len(sides),
+            transcendentals=0,
         ),
     )(*lefts, *rights)
+    return [outs[2 * number : 2 * number + 2] for number in range(len(sides))]
 
 
 def rms_scale(values, gain):
@@ -451,8 +489,8 @@
 
 def gather_step(held, bit, size, earlier=()):
     places = list(held)
-    sent = jnp.stack([held[place][0][held[place][1]] for place in places])
-    got = swap(after(sent, *earlier), bit, size)
+    sent = after([held[place][0][held[place][1]] for place in places], *earlier)
+    got = swap(jnp.stack(sent), bit, size)
     return {**held, **{place ^ bit: (got, at) for at, place in enumerate(places)}}, got
 
 
@@ -473,6 +511,22 @@
 def halves_end(state, size, earlier=()):
     ends = [gather_end(held, size, group, earlier) for group, held in enumerate(state)]
     return [parts for parts, _ in ends], [got for _, got in ends]
+
+
+def gather_split(own, size, earlier=()):
+    half = own.shape[1] // 2
+    state, first, last = [], [], []
+    for part, order in zip((own[:, :half], own[:, half:]), bit_orders(size)):
+        held, came = {0: part}, []
+        for bit in order[::-1]:
+            for place in list(held):
+                sent = after(held[place], *earlier) if place else held[place]
+                held[place ^ bit] = swap(sent, bit, size)
+                came.append(held[place ^ bit])
+        state.append([(held[place][None], 0) for place in range(size)])
+        first.append(came[0])
+        last.append(came[-1])
+    return state, first, last
 
 
 def assemble_kernel(cases, shift_ref, *refs):
@@ -520,17 +574,20 @@
     )(shift, *arrays)
 
 
-def scatter_start(terms, size, width, earlier=(), free=()):
+def scatter_start(terms, size, width, free=(), together=False):
     if size != 4:
         total = 0.0
         for left, right, at in terms:
             depth = left.shape[1]
             total = total + last_dims(left, right[:, at * depth : (at + 1) * depth])
         return total, [total], [total], [total]
-    sent = row_products(terms, 1, width)
-    lefts = after([left for left, _, _ in terms], *sent, *earlier)
-    terms = [(left, right, at) for left, (_, right, at) in zip(lefts, terms)]
-    kept = row_products(terms, 0, width)
+    if together:
+        sent, kept = row_products(terms, (1, 0), width)
+    else:
+        (sent,) = row_products(terms, (1,), width)
+        lefts = after([left for left, _, _ in terms], *sent)
+        terms = [(left, right, at) for left, (_, right, at) in zip(lefts, terms)]
+        (kept,) = row_products(terms, (0,), width)
     if free:
         free = (*free, *kept)
     first = [swap(after(sent[half], *free), 1 + half, size) for half in range(2)]
@@ -718,9 +775,8 @@
     mid_part = norm_back(back_sum, mid, m_inverse, ffn_scale)
     grad_mid = grad_y + mid_part
     mid_low = grad_mid.astype(BF)
-    held, mid_first = halves_start(mid_low, size)
-    parts, mid_last = halves_end(held, size)
-    grad_mid_low = assemble(parts, still, BF)
+    parts, mid_first, mid_last = gather_split(mid_low, size)
+    mid_arrays, mid_picks = arrays_of(parts)
     act_early, act_late = after((act_early, act_late), *mid_first)
     out_state, _, out_first, out_kept = scatter_start(
         [(act_early, w_early, 2), (act_late, w_late, 2)], size, width, free=mid_last
@@ -729,33 +785,33 @@
     sum_late = lax.psum_scatter(
         after(grads_late, *mid_first), "dp", scatter_dimension=1, tiled=True
     )
-    grad_mid_low = after(grad_mid_low, grads_late, *out_kept)
+    mid_arrays = after(mid_arrays, grads_late, *out_kept)
 
     group = head_group(wide)
     groups = wide // group
     backs, heads_held, q_first = [], [], []
-    grad_in = grad_mid_low
+    grad_in = mid_arrays
     for at in range(groups):
         backs.append(
             attend_backward(
-                place, grad_in, w_heads, queries, keys, values, cosine, sine, size, at
+                place, (grad_in, mid_picks), w_heads, queries, keys, values, cosine, sine, at
             )
         )
         held, first = gather_start(backs[-1][0], size, at % 2)
         heads_held.append(held)
         q_first.append(first)
-        grad_in = after(grad_mid_low, backs[-1][0])
+        grad_in = after(mid_arrays, backs[-1][0])
     kv_terms = [(backs[at][1], w_heads, at + groups) for at in range(groups)]
     kv_terms += [(backs[at][2], w_heads, at + 2 * groups) for at in range(groups)]
     lefts = after([left for left, _, _ in kv_terms], *out_first, *q_first[:-1])
     kv_terms = [(left, right, at) for left, (_, right, at) in zip(lefts, kv_terms)]
     kv_state, kv_sent, kv_first, kv_kept = scatter_start(
-        kv_terms, size, width, earlier=q_first[-1:]
+        kv_terms, size, width, together=True
     )
     grad_kv_normed, kv_more, kv_last = scatter_end(kv_state, size, width)
     heads_q, q_last = [], []
     for at in range(groups):
-        parts, last = gather_end(heads_held[at], size, at % 2, kv_more)
+        parts, last = gather_end(heads_held[at], size, at % 2, kv_kept)
         heads_q.append(parts)
         q_last.append(last)
     out_sum, out_more, out_last = scatter_end(out_state, size, width, kv_more)
@@ -766,9 +822,9 @@
     grads_heads = products(
         [(backs[at][3], lead, min(lead, 1)) for lead in range(3) for at in range(groups)]
         + [(attended_flip[None], 0, 2)],
-        [after(normed, kv_kept[0]), kv_normed, after(grad_mid_low, sum_early)],
-    )
-    grads_heads = after(grads_heads, *kv_first)
+        [after(normed, sum_early, *kv_kept), kv_normed, (mid_arrays, mid_picks)],
+    )
+    grads_heads = after(grads_heads, *kv_first, *q_last)
     sum_heads = lax.psum_scatter(grads_heads, "dp", scatter_dimension=1, tiled=True).astype(F32)
     def unit_sums(at):
         early_rows = sum_early[at * early : (at + 1) * early]
@@ -788,6 +844,9 @@
     weights_in = after((w_gate, w_up), *self_first)
     sum_gate, sum_up, sum_down = unit_sums(0).T, unit_sums(1).T, unit_sums(2)
     ffn_gain_sum = gain_part(ffn_gain, (weights_in[0], sum_gate), (weights_in[1], sum_up))
+
+    mid_parts = [[(mid_arrays[at], index) for at, index in part] for part in mid_picks]
+    grad_mid_low = assemble(mid_parts, after(still, self_own_grad), BF)
 
     query_arrays, query_picks = arrays_of(query_mine)
     other_arrays = [

time: 592 us -> 582 us (0.983)
    another operation x12 -> x10, other arithmetic: 16.5 us -> 11.2 us  [gather_step(): got = swap(jnp.stack(sent), bit, size)]
    ppermute x40 -> x42, starting transfers between devices: 44.6 us -> 40.4 us  [swap(): return lax.ppermute(array, 'tensor', [(t, t ^ bit) for t in range(size)])]
    pallas_call x13 -> x12, Pallas kernels: 141 us -> 138 us  [the longest x7 60.5 us: row_products(): pl.pallas_call(functools.partial(rows_kernel, len(terms), sides, steps),...]
    unnamed x125 -> x105, local copies, waits for them, and re-layouts: 12.9 us -> 11 us
    ppermute x40 -> x42, waiting for transfers between devices: 125 us -> 123 us  [swap(): return lax.ppermute(array, 'tensor', [(t, t ^ bit) for t in range(size)])]
  transfers between devices with their start and end apart: 55 -> 57, of which waited for: 26 -> 30; matrix products, arithmetic and copies ran while one was open for 12% -> 13% of each run, Pallas kernels for 41% -> 41%
where the time goes in v5:
time: 582 us; the launch traced here: 576 us
  Pallas kernels  238 us (41%)
  waiting for transfers between devices  178 us (31%)
  other arithmetic  54 us (9%)
  starting transfers between devices  44.4 us (8%)
  local copies, waits for them, and re-layouts  31.7 us (5%)
  between operations  16.1 us (3%)
  blocking collectives  14.5 us (2%)
    ppermute x42, waiting for transfers between devices, swap(): return lax.ppermute(array, 'tensor', [(t, t ^ bit) for t in range(size)])  123 us
    pallas_call x7, Pallas kernels, row_products(): pl.pallas_call(functools.partial(rows_kernel, len(terms), sides, steps),...  60.5 us
    all_gather x3, waiting for transfers between devices, local(): lax.all_gather(w, 'dp', axis=0, tiled=True)  54.4 us
    pallas_call x3, Pallas kernels, products(): pl.pallas_call(functools.partial(products_kernel, counts, forms), grid=(t...  51.6 us
    ppermute x42, starting transfers between devices, swap(): return lax.ppermute(array, 'tensor', [(t, t ^ bit) for t in range(size)])  40.4 us
    pallas_call x2, Pallas kernels, feed_forward(): pl.pallas_call(feed_kernel, grid=(steps,), in_specs=[whole, whole, pl.Blo...  36.4 us
    pallas_call x2, Pallas kernels, attend_backward(): pl.pallas_call(functools.partial(backward_kernel, picks), grid=(1,), in_s...  25.4 us
    pallas_call x1, Pallas kernels, attend_forward(): pl.pallas_call(functools.partial(forward_kernel, size), grid=(groups,), i...  24.8 us
  transfers between devices with their start and end apart: 57, of which 30 were waited for; matrix products, arithmetic and copies ran while one was open for 13% of the time, Pallas kernels for 41%

profile of v5, /device:TPU:0, one launch (start us, length us, event | category | flops | bytes accessed | tf_op | source)
XLA Modules:
  0.0 575.7 jit_solution(12190751848675467227)
XLA Ops:
  14.4 14.5 %all_gather.12 = bf16[3,2048]{1,0:T(4,128)(2,1)S(1)} all-gather(bf16[3,256]{1,0:T(4,128)(2,1)S(1)} %pad_maximum_fusion.16), channel_id=1, replica_groups=mesh['dp'=8,'tensor'=4] {'dp'}, dimensions={1}, use_global_device_ids=true | all-gather | bytes 13824 | tf_op jit(solution)/shard_map/all_gather | solution.py:714
  41.2 54.4 %all-gather.4.cloned.1.call-done.wq_ref.wk_ref.wv_ref.refs_2_.wo_ref.refs_16_.refs_17_.refs_18_.refs_19_ = bf16[2048,2048]{1,0:T(8,128)(2,1)} async-done(((bf16[256,2048]{1,0:T(8,128)(2,1)}), bf16[2048,2048]{1,0:T(8,128)(2,1)}) %all-gather.4.cloned.1.call-update) | async-done | bytes 8388624 | tf_op jit(solution)/shard_map/all_gather | solution.py:713
  95.6 24.8 %shard_map.237 = (bf16[1024,512]{1,0:T(8,128)(2,1)}, bf16[1024,512]{1,0:T(8,128)(2,1)}, bf16[1024,512]{1,0:T(8,128)(2,1)}, bf16[1024,512]{1,0:T(8,128)(2,1)}, bf16[512,1024]{1,0:T(8,128)(2,1)}) custom-call(s32[3]{0:T(128)} %pad_add_fusion.place_ref.shift_ref, bf16[1024,2048]{1,0:T(8,128)(2,1)} %get-tuple-element.235.normed_ref.refs_7_, ...), custom_call_target="tpu_custom_call" | custom-call | flops 8053063680 | bytes 18874368 | tf_op jit(solution)/shard_map/pallas_call | solution.py:114
  135.6 15.6 %collective-permute-done.1 = bf16[2,256,1024]{2,1,0:T(8,128)(2,1)S(1)} collective-permute-done((bf16[2,256,1024]{2,1,0:T(8,128)(2,1)}, bf16[2,256,1024]{2,1,0:T(8,128)(2,1)S(1)}, u32[]{:S(2)}, u32[]{:S(2)}) %collective-permute-start.1) | collective-permute-done | bytes 1048608 | tf_op jit(solution)/shard_map/ppermute | solution.py:451
  159.4 9.3 %collective-permute-done.2 = bf16[256,1024]{1,0:T(8,128)(2,1)} collective-permute-done((bf16[256,1024]{1,0:T(8,128)(2,1)}, bf16[256,1024]{1,0:T(8,128)(2,1)}, u32[]{:S(2)}, u32[]{:S(2)}) %collective-permute-start.2) | collective-permute-done | bytes 524320 | tf_op jit(solution)/shard_map/ppermute | solution.py:451
  176.9 8.8 %collective-permute-done.4.refs_2_ = bf16[1,256,1024]{2,1,0:T(8,128)(2,1)S(1)} collective-permute-done((bf16[1,256,1024]{2,1,0:T(8,128)(2,1)S(1)}, bf16[1,256,1024]{2,1,0:T(8,128)(2,1)S(1)}, u32[]{:S(2)}, u32[]{:S(2)}) %collective-permute-start.4) | collective-permute-done | bytes 524320 | tf_op jit(solution)/shard_map/ppermute | solution.py:451
  196.9 13.5 %collective-permute-done.7.refs_5_ = bf16[2,256,1024]{2,1,0:T(8,128)(2,1)} collective-permute-done((bf16[2,256,1024]{2,1,0:T(8,128)(2,1)}, bf16[2,256,1024]{2,1,0:T(8,128)(2,1)}, u32[]{:S(2)}, u32[]{:S(2)}) %collective-permute-start.7) | collective-permute-done | bytes 1048608 | tf_op jit(solution)/shard_map/ppermute | solution.py:451
  228.7 21.6 %shard_map.241 = (bf16[1024,1024]{1,0:T(8,128)(2,1)}, bf16[1024,1024]{1,0:T(8,128)(2,1)}, bf16[1024,1024]{1,0:T(8,128)(2,1)}, bf16[3,1024,1024]{2,1,0:T(8,128)(2,1)}) custom-call(bf16[1024,2048]{1,0:T(8,128)(2,1)} %shard_map.240.x_ref.refs_3_, bf16[1024,2048]{1,0:T(8,128)(2,1)} %bitcast.161, ...), custom_call_target="tpu_custom_call" | custom-call | flops 12884901888 | bytes 33554432 | tf_op jit(solution)/shard_map/pallas_call | solution.py:275
  250.3 21.1 %shard_map.242 = bf16[3072,2048]{1,0:T(8,128)(2,1)} custom-call(bf16[3,1024,1024]{2,1,0:T(8,128)(2,1)} %get-tuple-element.143.refs_0_.refs_1_.refs_2_, bf16[3,1024,1024]{2,1,0:T(8,128)(2,1)} %get-tuple-element.143.refs_0_.refs_1_.refs_2_, bf16[3,1024,1024]{2,1,0:T(8,128)(2,1)} %get-tuple-element.143.refs_0_.refs_1_.refs_2_, ...), custom_call_target="tpu_custom_call" | custom-call | flops 12884901888 | bytes 27262976 | tf_op jit(solution)/shard_map/pallas_call | solution.py:350
  271.4 14.8 %shard_map.243 = (bf16[1024,384]{1,0:T(8,128)(2,1)}, bf16[1024,384]{1,0:T(8,128)(2,1)}, bf16[1024,384]{1,0:T(8,128)(2,1)}, bf16[3,384,1024]{2,1,0:T(8,128)(2,1)}) custom-call(bf16[1024,2048]{1,0:T(8,128)(2,1)} %shard_map.240.x_ref.refs_3_, bf16[1024,2048]{1,0:T(8,128)(2,1)} %bitcast.163, ...), custom_call_target="tpu_custom_call" | custom-call | flops 4831838208 | bytes 17825792 | tf_op jit(solution)/shard_map/pallas_call | solution.py:275
  286.3 12.1 %shard_map.244 = (bf16[2,256,1024]{2,1,0:T(8,128)(2,1)}, bf16[2,256,1024]{2,1,0:T(8,128)(2,1)}) custom-call(bf16[1024,1024]{1,0:T(8,128)(2,1)} %get-tuple-element.152.refs_0_.refs_1_, bf16[1024,1024]{1,0:T(8,128)(2,1)} %get-tuple-element.152.refs_0_.refs_1_, bf16[1024,1024]{1,0:T(8,128)(2,1)} %get-tuple-element.153.refs_2_.refs_3_, ...), custom_call_target="tpu_custom_call" | custom-call | flops 5905580032 | bytes 19398656 | tf_op jit(solution)/shard_map/pallas_call | solution.py:407
  298.7 12.2 %shard_map.245 = (bf16[2,256,1024]{2,1,0:T(8,128)(2,1)}, bf16[2,256,1024]{2,1,0:T(8,128)(2,1)}) custom-call(bf16[1024,1024]{1,0:T(8,128)(2,1)} %get-tuple-element.152.refs_0_.refs_1_, bf16[1024,1024]{1,0:T(8,128)(2,1)} %get-tuple-element.152.refs_0_.refs_1_, bf16[1024,1024]{1,0:T(8,128)(2,1)} %get-tuple-element.153.refs_2_.refs_3_, ...), custom_call_target="tpu_custom_call" | custom-call | flops 5905580032 | bytes 19398656 | tf_op jit(solution)/shard_map/pallas_call | solution.py:407
  310.9 7.6 %collective-permute-done.9 = bf16[2,256,1024]{2,1,0:T(8,128)(2,1)S(1)} collective-permute-done((bf16[2,256,1024]{2,1,0:T(8,128)(2,1)}, bf16[2,256,1024]{2,1,0:T(8,128)(2,1)S(1)}, u32[]{:S(2)}, u32[]{:S(2)}) %collective-permute-start.9) | collective-permute-done | bytes 1048608 | tf_op jit(solution)/shard_map/ppermute | solution.py:451
  322.7 7.2 %collective-permute-done.10 = bf16[256,1024]{1,0:T(8,128)(2,1)S(1)} collective-permute-done((bf16[256,1024]{1,0:T(8,128)(2,1)S(1)}, bf16[256,1024]{1,0:T(8,128)(2,1)S(1)}, u32[]{:S(2)}, u32[]{:S(2)}) %collective-permute-start.10) | collective-permute-done | bytes 524320 | tf_op jit(solution)/shard_map/ppermute | solution.py:451
  338.8 12.6 %shard_map.248 = bf16[1152,2048]{1,0:T(8,128)(2,1)} custom-call(bf16[3,384,1024]{2,1,0:T(8,128)(2,1)} %get-tuple-element.174.refs_0_.refs_1_.refs_2_, bf16[3,384,1024]{2,1,0:T(8,128)(2,1)} %get-tuple-element.174.refs_0_.refs_1_.refs_2_, bf16[3,384,1024]{2,1,0:T(8,128)(2,1)} %get-tuple-element.174.refs_0_.refs_1_.refs_2_, ...), custom_call_target="tpu_custom_call" | custom-call | flops 4831838208 | bytes 15466496 | tf_op jit(solution)/shard_map/pallas_call | solution.py:350
  355.6 7.7 %shard_map.246 = (bf16[2,256,1024]{2,1,0:T(8,128)(2,1)}, bf16[2,256,1024]{2,1,0:T(8,128)(2,1)}) custom-call(bf16[1024,1024]{1,0:T(8,128)(2,1)} %get-tuple-element.164.refs_0_.refs_1_, bf16[1024,1024]{1,0:T(8,128)(2,1)} %get-tuple-element.164.refs_0_.refs_1_, bf16[1024,384]{1,0:T(8,128)(2,1)} %get-tuple-element.165.refs_2_.refs_3_, ...), custom_call_target="tpu_custom_call" | custom-call | flops 2952790016 | bytes 10747904 | tf_op jit(solution)/shard_map/pallas_call | solution.py:407
  363.4 8.2 %shard_map.247 = (bf16[2,256,1024]{2,1,0:T(8,128)(2,1)}, bf16[2,256,1024]{2,1,0:T(8,128)(2,1)}) custom-call(bf16[1024,1024]{1,0:T(8,128)(2,1)} %get-tuple-element.164.refs_0_.refs_1_, bf16[1024,1024]{1,0:T(8,128)(2,1)} %get-tuple-element.164.refs_0_.refs_1_, bf16[1024,384]{1,0:T(8,128)(2,1)} %get-tuple-element.165.refs_2_.refs_3_, ...), custom_call_target="tpu_custom_call" | custom-call | flops 2952790016 | bytes 10747904 | tf_op jit(solution)/shard_map/pallas_call | solution.py:407
  378.0 12.5 %shard_map.249 = (bf16[1024,256]{1,0:T(8,128)(2,1)}, bf16[1024,256]{1,0:T(8,128)(2,1)}, bf16[1024,256]{1,0:T(8,128)(2,1)}, bf16[3,256,1024]{2,1,0:T(8,128)(2,1)}) custom-call(s32[3]{0:T(128)} %pad_add_fusion.place_ref.shift_ref, bf16[2048,2048]{1,0:T(8,128)(2,1)} %all-gather.4.cloned.1.call-done.wq_ref.wk_ref.wv_ref.refs_2_.wo_ref.refs_16_.refs_17_.refs_18_.refs_19_, ...), custom_call_target="tpu_custom_call" | custom-call | flops 3758096384 | bytes 9961472 | tf_op jit(solution)/shard_map/pallas_call | solution.py:221
  392.0 12.9 %shard_map.250 = (bf16[1024,256]{1,0:T(8,128)(2,1)}, bf16[1024,256]{1,0:T(8,128)(2,1)}, bf16[1024,256]{1,0:T(8,128)(2,1)}, bf16[3,256,1024]{2,1,0:T(8,128)(2,1)}) custom-call(s32[3]{0:T(128)} %pad_add_fusion.place_ref.shift_ref, bf16[2048,2048]{1,0:T(8,128)(2,1)} %all-gather.4.cloned.1.call-done.wq_ref.wk_ref.wv_ref.refs_2_.wo_ref.refs_16_.refs_17_.refs_18_.refs_19_, ...), custom_call_target="tpu_custom_call" | custom-call | flops 3758096384 | bytes 9961472 | tf_op jit(solution)/shard_map/pallas_call | solution.py:221
  404.9 9.4 %shard_map.251 = (bf16[2,256,1024]{2,1,0:T(8,128)(2,1)}, bf16[2,256,1024]{2,1,0:T(8,128)(2,1)}, bf16[2,256,1024]{2,1,0:T(8,128)(2,1)}, bf16[2,256,1024]{2,1,0:T(8,128)(2,1)}) custom-call(bf16[1024,256]{1,0:T(8,128)(2,1)} %get-tuple-element.196.refs_0_.refs_1_.refs_2_.refs_3_, bf16[1024,256]{1,0:T(8,128)(2,1)} %get-tuple-element.196.refs_0_.refs_1_.refs_2_.refs_3_, ...), custom_call_target="tpu_custom_call" | custom-call | flops 4294967296 | bytes 10485760 | tf_op jit(solution)/shard_map/pallas_call | solution.py:407
  424.9 17.9 %shard_map.255 = bf16[2048,2048]{1,0:T(8,128)(2,1)} custom-call(bf16[3,256,1024]{2,1,0:T(8,128)(2,1)} %get-tuple-element.231.refs_0_.refs_2_.refs_4_, bf16[3,256,1024]{2,1,0:T(8,128)(2,1)} %get-tuple-element.232.refs_1_.refs_3_.refs_5_, bf16[3,256,1024]{2,1,0:T(8,128)(2,1)} %get-tuple-element.231.refs_0_.refs_2_.refs_4_, ...), custom_call_target="tpu_custom_call" | custom-call | flops 8589934592 | bytes 25165824 | tf_op jit(solution)/shard_map/pallas_call | solution.py:350
  451.0 9.7 %collective-permute-done.21 = bf16[2,256,1024]{2,1,0:T(8,128)(2,1)} collective-permute-done((bf16[2,256,1024]{2,1,0:T(8,128)(2,1)}, bf16[2,256,1024]{2,1,0:T(8,128)(2,1)}, u32[]{:S(2)}, u32[]{:S(2)}) %collective-permute-start.21) | collective-permute-done | bytes 1048608 | tf_op jit(solution)/shard_map/ppermute | solution.py:451
  484.4 8.2 %collective-permute-done.25.refs_2_ = bf16[1,256,1024]{2,1,0:T(8,128)(2,1)S(1)} collective-permute-done((bf16[1,256,1024]{2,1,0:T(8,128)(2,1)S(1)}, bf16[1,256,1024]{2,1,0:T(8,128)(2,1)S(1)}, u32[]{:S(2)}, u32[]{:S(2)}) %collective-permute-start.25) | collective-permute-done | bytes 524320 | tf_op jit(solution)/shard_map/ppermute | solution.py:451
  506.3 18.6 %shard_map.254 = f32[1024,2048]{1,0:T(8,128)} custom-call(s32[3]{0:T(128)} %pad_add_fusion.place_ref.shift_ref, bf16[1024,2048]{1,0:T(8,128)(2,1)} %hidden_ref, bf16[1024,2048]{1,0:T(8,128)(2,1)} %shard_map.253.mid_ref, f32[1,2048]{1,0:T(1,128)} %copy-done.39, bf16[1,1024,256]{2,1,0:T(8,128)(2,1)} %bitcast.197, ...), custom_call_target="tpu_custom_call" | custom-call | flops 8589934592 | bytes 29360128 | tf_op jit(solution)/shard_map/pallas_call | solution.py:651
  (325 shorter events, 204.3 us)
Async XLA Ops:
  7.2 88.4 %all-gather.4.cloned.1.call-start = ((), (), s32[]{:S(2)}) async-start(), calls=%async_computation.3 | async-start | bytes 9437184 | tf_op jit(solution)/shard_map/all_gather | solution.py:713
  10.6 218.0 %all-gather.6.cloned.1.call-start = ((), (), s32[]{:S(2)}) async-start(), calls=%async_computation.4 | async-start | bytes 14155776 | tf_op jit(solution)/shard_map/all_gather | solution.py:713
  13.6 257.8 %all-gather.8.cloned.1.call-start = ((), (), s32[]{:S(2)}) async-start(), calls=%async_computation.5 | async-start | bytes 5308416 | tf_op jit(solution)/shard_map/all_gather | solution.py:713
  125.8 25.5 %collective-permute-start.1 = (bf16[2,256,1024]{2,1,0:T(8,128)(2,1)}, bf16[2,256,1024]{2,1,0:T(8,128)(2,1)S(1)}, u32[]{:S(2)}, u32[]{:S(2)}) collective-permute-start(bf16[2,256,1024]{2,1,0:T(8,128)(2,1)} %get-tuple-element.132), channel_id=1, source_target_pairs={{0,2},{1,3},{2,0},{3,1},{4,6},{5,7},{6,4},{7,5},{8,10},{9,11},{10,... | collective-permute-start | bytes 3145736 | tf_op jit(solution)/shard_map/ppermute | solution.py:451
  127.3 25.3 %collective-permute-start = (bf16[2,256,1024]{2,1,0:T(8,128)(2,1)}, bf16[2,256,1024]{2,1,0:T(8,128)(2,1)}, u32[]{:S(2)}, u32[]{:S(2)}) collective-permute-start(bf16[2,256,1024]{2,1,0:T(8,128)(2,1)} %get-tuple-element.131), channel_id=1, source_target_pairs={{0,1},{1,0},{2,3},{3,2},{4,5},{5,4},{6,7},{7,6},{8,9},{9,8},{10,11... | collective-permute-start | bytes 3145736 | tf_op jit(solution)/shard_map/ppermute | solution.py:451
  130.0 294.9 %reduce-scatter.4.cloned.1.call-start = ((), (), s32[]{:S(2)}) async-start(), calls=%async_computation.6 | async-start | bytes 14155776 | tf_op jit(solution)/shard_map/reduce_scatter | solution.py:760
  224.9 46.5 %collective-permute-start.37 = (bf16[2,1024,256]{2,1,0:T(8,128)(2,1)S(1)}, bf16[2,1024,256]{2,1,0:T(8,128)(2,1)}, u32[]{:S(2)}, u32[]{:S(2)}) collective-permute-start(bf16[2,1024,256]{2,1,0:T(8,128)(2,1)S(1)} %pad_maximum_fusion.10), channel_id=1, source_target_pairs={{0,2},{1,3},{2,0},{3,1},{4,6},{5,7},{6,4},{7,5},{8,10},{9,11},{10,... | collective-permute-start | bytes 3145736 | tf_op jit(solution)/shard_map/ppermute | solution.py:451
  227.1 44.2 %collective-permute-start.35 = (bf16[2,1024,256]{2,1,0:T(8,128)(2,1)S(1)}, bf16[2,1024,256]{2,1,0:T(8,128)(2,1)}, u32[]{:S(2)}, u32[]{:S(2)}) collective-permute-start(bf16[2,1024,256]{2,1,0:T(8,128)(2,1)S(1)} %pad_maximum_fusion.9), channel_id=1, source_target_pairs={{0,1},{1,0},{2,3},{3,2},{4,5},{5,4},{6,7},{7,6},{8,9},{9,8},{10,11... | collective-permute-start | bytes 3145736 | tf_op jit(solution)/shard_map/ppermute | solution.py:451
  271.4 273.9 %reduce-scatter.8.cloned.1.call-start = ((), (), s32[]{:S(2)}) async-start(), calls=%async_computation.8 | async-start | bytes 5308416 | tf_op jit(solution)/shard_map/reduce_scatter | solution.py:785
  351.5 198.9 %reduce-scatter.6.cloned.1.call-start = ((), (), s32[]{:S(2)}) async-start(), calls=%async_computation.7 | async-start | bytes 9437184 | tf_op jit(solution)/shard_map/reduce_scatter | solution.py:828
  351.5 25.7 %collective-permute-start.19 = (bf16[256,1024]{1,0:T(8,128)(2,1)}, bf16[256,1024]{1,0:T(8,128)(2,1)S(1)}, u32[]{:S(2)}, u32[]{:S(2)}) collective-permute-start(bf16[256,1024]{1,0:T(8,128)(2,1)} %get-tuple-element.306), channel_id=1, source_target_pairs={{0,2},{1,3},{2,0},{3,1},{4,6},{5,7},{6,4},{7,5},{8,10},{9,11},{10,... | collective-permute-start | bytes 1572872 | tf_op jit(solution)/shard_map/ppermute | solution.py:451
  352.4 24.8 %collective-permute-start.18 = (bf16[256,1024]{1,0:T(8,128)(2,1)}, bf16[256,1024]{1,0:T(8,128)(2,1)}, u32[]{:S(2)}, u32[]{:S(2)}) collective-permute-start(bf16[256,1024]{1,0:T(8,128)(2,1)} %get-tuple-element.307), channel_id=1, source_target_pairs={{0,1},{1,0},{2,3},{3,2},{4,5},{5,4},{6,7},{7,6},{8,9},{9,8},{10,11... | collective-permute-start | bytes 1572872 | tf_op jit(solution)/shard_map/ppermute | solution.py:451
  374.4 30.5 %collective-permute-start.16 = (bf16[2,256,1024]{2,1,0:T(8,128)(2,1)}, bf16[2,256,1024]{2,1,0:T(8,128)(2,1)}, u32[]{:S(2)}, u32[]{:S(2)}) collective-permute-start(bf16[2,256,1024]{2,1,0:T(8,128)(2,1)} %get-tuple-element.168), channel_id=1, source_target_pairs={{0,1},{1,0},{2,3},{3,2},{4,5},{5,4},{6,7},{7,6},{8,9},{9,8},{10,11... | collective-permute-start | bytes 3145736 | tf_op jit(solution)/shard_map/ppermute | solution.py:451
  376.7 28.2 %collective-permute-start.17 = (bf16[2,256,1024]{2,1,0:T(8,128)(2,1)}, bf16[2,256,1024]{2,1,0:T(8,128)(2,1)S(1)}, u32[]{:S(2)}, u32[]{:S(2)}) collective-permute-start(bf16[2,256,1024]{2,1,0:T(8,128)(2,1)} %get-tuple-element.169), channel_id=1, source_target_pairs={{0,2},{1,3},{2,0},{3,1},{4,6},{5,7},{6,4},{7,5},{8,10},{9,11},{10,... | collective-permute-start | bytes 3145736 | tf_op jit(solution)/shard_map/ppermute | solution.py:451
  419.7 23.1 %collective-permute-start.33 = (bf16[2,1024,256]{2,1,0:T(8,128)(2,1)S(1)}, bf16[2,1024,256]{2,1,0:T(8,128)(2,1)}, u32[]{:S(2)}, u32[]{:S(2)}) collective-permute-start(bf16[2,1024,256]{2,1,0:T(8,128)(2,1)S(1)} %pad_maximum_fusion.8), channel_id=1, source_target_pairs={{0,2},{1,3},{2,0},{3,1},{4,6},{5,7},{6,4},{7,5},{8,10},{9,11},{10,... | collective-permute-start | bytes 3145736 | tf_op jit(solution)/shard_map/ppermute | solution.py:451
  420.9 26.4 %collective-permute-start.31 = (bf16[2,1024,256]{2,1,0:T(8,128)(2,1)}, bf16[2,1024,256]{2,1,0:T(8,128)(2,1)}, u32[]{:S(2)}, u32[]{:S(2)}) collective-permute-start(bf16[2,1024,256]{2,1,0:T(8,128)(2,1)} %pad_maximum_fusion.7), channel_id=1, source_target_pairs={{0,1},{1,0},{2,3},{3,2},{4,5},{5,4},{6,7},{7,6},{8,9},{9,8},{10,11... | collective-permute-start | bytes 3145736 | tf_op jit(solution)/shard_map/ppermute | solution.py:451
  420.9 30.1 %collective-permute-start.22 = (bf16[2,256,1024]{2,1,0:T(8,128)(2,1)}, bf16[2,256,1024]{2,1,0:T(8,128)(2,1)}, u32[]{:S(2)}, u32[]{:S(2)}) collective-permute-start(bf16[2,256,1024]{2,1,0:T(8,128)(2,1)} %get-tuple-element.202), channel_id=1, source_target_pairs={{0,2},{1,3},{2,0},{3,1},{4,6},{5,7},{6,4},{7,5},{8,10},{9,11},{10,... | collective-permute-start | bytes 3145736 | tf_op jit(solution)/shard_map/ppermute | solution.py:451
  422.9 37.8 %collective-permute-start.21 = (bf16[2,256,1024]{2,1,0:T(8,128)(2,1)}, bf16[2,256,1024]{2,1,0:T(8,128)(2,1)}, u32[]{:S(2)}, u32[]{:S(2)}) collective-permute-start(bf16[2,256,1024]{2,1,0:T(8,128)(2,1)} %get-tuple-element.201), channel_id=1, source_target_pairs={{0,1},{1,0},{2,3},{3,2},{4,5},{5,4},{6,7},{7,6},{8,9},{9,8},{10,11... | collective-permute-start | bytes 3145736 | tf_op jit(solution)/shard_map/ppermute | solution.py:451
  475.5 29.0 %collective-permute-start.39 = (bf16[2,1024,256]{2,1,0:T(8,128)(2,1)}, bf16[2,1024,256]{2,1,0:T(8,128)(2,1)}, u32[]{:S(2)}, u32[]{:S(2)}) collective-permute-start(bf16[2,1024,256]{2,1,0:T(8,128)(2,1)} %collective-permute-done.35.refs_7_), channel_id=1, source_target_pairs={{0,4},{4,0},{8,12},{12,8},{16,20},{20,16},{24,28},{28,24},{1,5},{5... | collective-permute-start | bytes 3145736 | tf_op jit(solution)/shard_map/ppermute | solution.py:853
  476.1 30.2 %collective-permute-start.43 = (bf16[2,1024,256]{2,1,0:T(8,128)(2,1)}, bf16[2,1024,256]{2,1,0:T(8,128)(2,1)}, u32[]{:S(2)}, u32[]{:S(2)}) collective-permute-start(bf16[2,1024,256]{2,1,0:T(8,128)(2,1)} %collective-permute-done.37.refs_11_), channel_id=1, source_target_pairs={{0,4},{4,0},{8,12},{12,8},{16,20},{20,16},{24,28},{28,24},{1,5},{5... | collective-permute-start | bytes 3145736 | tf_op jit(solution)/shard_map/ppermute | solution.py:853
  503.0 36.4 %collective-permute-start.28 = (bf16[2,256,1024]{2,1,0:T(8,128)(2,1)}, bf16[2,256,1024]{2,1,0:T(8,128)(2,1)S(1)}, u32[]{:S(2)}, u32[]{:S(2)}) collective-permute-start(bf16[2,256,1024]{2,1,0:T(8,128)(2,1)} %pad_maximum_fusion.6), channel_id=1, source_target_pairs={{0,2},{1,3},{2,0},{3,1},{4,6},{5,7},{6,4},{7,5},{8,10},{9,11},{10,... | collective-permute-start | bytes 3145736 | tf_op jit(solution)/shard_map/ppermute | solution.py:451
  504.6 35.7 %collective-permute-start.26 = (bf16[2,256,1024]{2,1,0:T(8,128)(2,1)}, bf16[2,256,1024]{2,1,0:T(8,128)(2,1)}, u32[]{:S(2)}, u32[]{:S(2)}) collective-permute-start(bf16[2,256,1024]{2,1,0:T(8,128)(2,1)} %pad_maximum_fusion.5), channel_id=1, source_target_pairs={{0,1},{1,0},{2,3},{3,2},{4,5},{5,4},{6,7},{7,6},{8,9},{9,8},{10,11... | collective-permute-start | bytes 3145736 | tf_op jit(solution)/shard_map/ppermute | solution.py:451
  530.9 30.7 %collective-permute-start.47 = (bf16[2,256,1024]{2,1,0:T(8,128)(2,1)}, bf16[2,256,1024]{2,1,0:T(8,128)(2,1)}, u32[]{:S(2)}, u32[]{:S(2)}) collective-permute-start(bf16[2,256,1024]{2,1,0:T(8,128)(2,1)} %pad_maximum_fusion.12), channel_id=1, source_target_pairs={{0,2},{1,3},{2,0},{3,1},{4,6},{5,7},{6,4},{7,5},{8,10},{9,11},{10,... | collective-permute-start | bytes 3145736 | tf_op jit(solution)/shard_map/ppermute | solution.py:451
  532.7 29.5 %collective-permute-start.46 = (bf16[2,256,1024]{2,1,0:T(8,128)(2,1)}, bf16[2,256,1024]{2,1,0:T(8,128)(2,1)}, u32[]{:S(2)}, u32[]{:S(2)}) collective-permute-start(bf16[2,256,1024]{2,1,0:T(8,128)(2,1)} %pad_maximum_fusion.11), channel_id=1, source_target_pairs={{0,1},{1,0},{2,3},{3,2},{4,5},{5,4},{6,7},{7,6},{8,9},{9,8},{10,11... | collective-permute-start | bytes 3145736 | tf_op jit(solution)/shard_map/ppermute | solution.py:451
  (86 other events, 727.8 us)
Sparse Core Ops, SparseCore 0:
  10.7 84.7 all-gather.3
  97.2 115.2 all-gather.5
  214.2 49.9 all-gather.7
  271.5 126.7 reduce-scatter.3
  400.5 53.3 reduce-scatter.7
  460.8 86.9 reduce-scatter.5

commit v6 on v5

--- a/solution.py
+++ b/solution.py
@@ -824,7 +824,9 @@
         + [(attended_flip[None], 0, 2)],
         [after(normed, sum_early, *kv_kept), kv_normed, (mid_arrays, mid_picks)],
     )
-    grads_heads = after(grads_heads, *kv_first, *q_last)
+    mid_parts = [[(mid_arrays[at], index) for at, index in part] for part in mid_picks]
+    grad_mid_low = assemble(mid_parts, after(still, *kv_kept), BF)
+    grads_heads = after(grads_heads, *kv_first, *q_last, grad_mid_low)
     sum_heads = lax.psum_scatter(grads_heads, "dp", scatter_dimension=1, tiled=True).astype(F32)
     def unit_sums(at):
         early_rows = sum_early[at * early : (at + 1) * early]
@@ -845,8 +847,6 @@
     sum_gate, sum_up, sum_down = unit_sums(0).T, unit_sums(1).T, unit_sums(2)
     ffn_gain_sum = gain_part(ffn_gain, (weights_in[0], sum_gate), (weights_in[1], sum_up))
 
-    mid_parts = [[(mid_arrays[at], index) for at, index in part] for part in mid_picks]
-    grad_mid_low = assemble(mid_parts, after(still, self_own_grad), BF)
 
     query_arrays, query_picks = arrays_of(query_mine)
     other_arrays = [

time: 582 us -> 579 us (level)
    unnamed x105 -> x119, local copies, waits for them, and re-layouts: 11 us -> 12.3 us
  transfers between devices with their start and end apart: 57 -> 57, of which waited for: 30 -> 31; matrix products, arithmetic and copies ran while one was open for 13% -> 12% of each run, Pallas kernels for 41% -> 42%
where the time goes in v6:
time: 579 us; the launch traced here: 572 us
  Pallas kernels  238 us (41%)
  waiting for transfers between devices  174 us (30%)
  other arithmetic  51.9 us (9%)
  starting transfers between devices  45.4 us (8%)
  local copies, waits for them, and re-layouts  33 us (6%)
  between operations  16.1 us (3%)
  blocking collectives  14.6 us (3%)
    ppermute x42, waiting for transfers between devices, swap(): return lax.ppermute(array, 'tensor', [(t, t ^ bit) for t in range(size)])  119 us
    pallas_call x7, Pallas kernels, row_products(): pl.pallas_call(functools.partial(rows_kernel, len(terms), sides, steps),...  60.4 us
    all_gather x3, waiting for transfers between devices, local(): lax.all_gather(w, 'dp', axis=0, tiled=True)  54.3 us
    pallas_call x3, Pallas kernels, products(): pl.pallas_call(functools.partial(products_kernel, counts, forms), grid=(t...  51.7 us
    ppermute x42, starting transfers between devices, swap(): return lax.ppermute(array, 'tensor', [(t, t ^ bit) for t in range(size)])  41.5 us
    pallas_call x2, Pallas kernels, feed_forward(): pl.pallas_call(feed_kernel, grid=(steps,), in_specs=[whole, whole, pl.Blo...  36.2 us
    pallas_call x2, Pallas kernels, attend_backward(): pl.pallas_call(functools.partial(backward_kernel, picks), grid=(1,), in_s...  25.7 us
    pallas_call x1, Pallas kernels, attend_forward(): pl.pallas_call(functools.partial(forward_kernel, size), grid=(groups,), i...  24.8 us
  transfers between devices with their start and end apart: 57, of which 31 were waited for; matrix products, arithmetic and copies ran while one was open for 12% of the time, Pallas kernels for 42%

profile of v6, /device:TPU:0, one launch (start us, length us, event | category | flops | bytes accessed | tf_op | source)
XLA Modules:
  0.0 572.4 jit_solution(5366615528795686092)
XLA Ops:
  14.4 14.6 %all_gather.12 = bf16[3,2048]{1,0:T(4,128)(2,1)S(1)} all-gather(bf16[3,256]{1,0:T(4,128)(2,1)S(1)} %pad_maximum_fusion.16), channel_id=1, replica_groups=mesh['dp'=8,'tensor'=4] {'dp'}, dimensions={1}, use_global_device_ids=true | all-gather | bytes 13824 | tf_op jit(solution)/shard_map/all_gather | solution.py:714
  41.3 54.3 %all-gather.4.cloned.1.call-done.wq_ref.wk_ref.wv_ref.refs_2_.wo_ref.refs_16_.refs_17_.refs_18_.refs_19_ = bf16[2048,2048]{1,0:T(8,128)(2,1)} async-done(((bf16[256,2048]{1,0:T(8,128)(2,1)}), bf16[2048,2048]{1,0:T(8,128)(2,1)}) %all-gather.4.cloned.1.call-update) | async-done | bytes 8388624 | tf_op jit(solution)/shard_map/all_gather | solution.py:713
  95.6 24.8 %shard_map.237 = (bf16[1024,512]{1,0:T(8,128)(2,1)}, bf16[1024,512]{1,0:T(8,128)(2,1)}, bf16[1024,512]{1,0:T(8,128)(2,1)}, bf16[1024,512]{1,0:T(8,128)(2,1)}, bf16[512,1024]{1,0:T(8,128)(2,1)}) custom-call(s32[3]{0:T(128)} %pad_add_fusion.place_ref.shift_ref, bf16[1024,2048]{1,0:T(8,128)(2,1)} %get-tuple-element.235.normed_ref.refs_7_, ...), custom_call_target="tpu_custom_call" | custom-call | flops 8053063680 | bytes 18874368 | tf_op jit(solution)/shard_map/pallas_call | solution.py:114
  135.7 15.6 %collective-permute-done.1 = bf16[2,256,1024]{2,1,0:T(8,128)(2,1)S(1)} collective-permute-done((bf16[2,256,1024]{2,1,0:T(8,128)(2,1)}, bf16[2,256,1024]{2,1,0:T(8,128)(2,1)S(1)}, u32[]{:S(2)}, u32[]{:S(2)}) %collective-permute-start.1) | collective-permute-done | bytes 1048608 | tf_op jit(solution)/shard_map/ppermute | solution.py:451
  159.5 9.3 %collective-permute-done.2 = bf16[256,1024]{1,0:T(8,128)(2,1)} collective-permute-done((bf16[256,1024]{1,0:T(8,128)(2,1)}, bf16[256,1024]{1,0:T(8,128)(2,1)}, u32[]{:S(2)}, u32[]{:S(2)}) %collective-permute-start.2) | collective-permute-done | bytes 524320 | tf_op jit(solution)/shard_map/ppermute | solution.py:451
  177.0 8.8 %collective-permute-done.4.refs_2_ = bf16[1,256,1024]{2,1,0:T(8,128)(2,1)S(1)} collective-permute-done((bf16[1,256,1024]{2,1,0:T(8,128)(2,1)S(1)}, bf16[1,256,1024]{2,1,0:T(8,128)(2,1)S(1)}, u32[]{:S(2)}, u32[]{:S(2)}) %collective-permute-start.4) | collective-permute-done | bytes 524320 | tf_op jit(solution)/shard_map/ppermute | solution.py:451
  197.0 13.6 %collective-permute-done.7.refs_5_ = bf16[2,256,1024]{2,1,0:T(8,128)(2,1)} collective-permute-done((bf16[2,256,1024]{2,1,0:T(8,128)(2,1)}, bf16[2,256,1024]{2,1,0:T(8,128)(2,1)}, u32[]{:S(2)}, u32[]{:S(2)}) %collective-permute-start.7) | collective-permute-done | bytes 1048608 | tf_op jit(solution)/shard_map/ppermute | solution.py:451
  227.9 21.6 %shard_map.241 = (bf16[1024,1024]{1,0:T(8,128)(2,1)}, bf16[1024,1024]{1,0:T(8,128)(2,1)}, bf16[1024,1024]{1,0:T(8,128)(2,1)}, bf16[3,1024,1024]{2,1,0:T(8,128)(2,1)}) custom-call(bf16[1024,2048]{1,0:T(8,128)(2,1)} %shard_map.240.x_ref.refs_3_, bf16[1024,2048]{1,0:T(8,128)(2,1)} %bitcast.161, ...), custom_call_target="tpu_custom_call" | custom-call | flops 12884901888 | bytes 33554432 | tf_op jit(solution)/shard_map/pallas_call | solution.py:275
  249.5 21.1 %shard_map.242 = bf16[3072,2048]{1,0:T(8,128)(2,1)} custom-call(bf16[3,1024,1024]{2,1,0:T(8,128)(2,1)} %get-tuple-element.143.refs_0_.refs_1_.refs_2_, bf16[3,1024,1024]{2,1,0:T(8,128)(2,1)} %get-tuple-element.143.refs_0_.refs_1_.refs_2_, bf16[3,1024,1024]{2,1,0:T(8,128)(2,1)} %get-tuple-element.143.refs_0_.refs_1_.refs_2_, ...), custom_call_target="tpu_custom_call" | custom-call | flops 12884901888 | bytes 27262976 | tf_op jit(solution)/shard_map/pallas_call | solution.py:350
  270.7 14.6 %shard_map.243 = (bf16[1024,384]{1,0:T(8,128)(2,1)}, bf16[1024,384]{1,0:T(8,128)(2,1)}, bf16[1024,384]{1,0:T(8,128)(2,1)}, bf16[3,384,1024]{2,1,0:T(8,128)(2,1)}) custom-call(bf16[1024,2048]{1,0:T(8,128)(2,1)} %shard_map.240.x_ref.refs_3_, bf16[1024,2048]{1,0:T(8,128)(2,1)} %bitcast.163, ...), custom_call_target="tpu_custom_call" | custom-call | flops 4831838208 | bytes 17825792 | tf_op jit(solution)/shard_map/pallas_call | solution.py:275
  285.3 11.9 %shard_map.244 = (bf16[2,256,1024]{2,1,0:T(8,128)(2,1)}, bf16[2,256,1024]{2,1,0:T(8,128)(2,1)}) custom-call(bf16[1024,1024]{1,0:T(8,128)(2,1)} %get-tuple-element.152.refs_0_.refs_1_, bf16[1024,1024]{1,0:T(8,128)(2,1)} %get-tuple-element.152.refs_0_.refs_1_, bf16[1024,1024]{1,0:T(8,128)(2,1)} %get-tuple-element.153.refs_2_.refs_3_, ...), custom_call_target="tpu_custom_call" | custom-call | flops 5905580032 | bytes 19398656 | tf_op jit(solution)/shard_map/pallas_call | solution.py:407
  298.2 12.1 %shard_map.245 = (bf16[2,256,1024]{2,1,0:T(8,128)(2,1)}, bf16[2,256,1024]{2,1,0:T(8,128)(2,1)}) custom-call(bf16[1024,1024]{1,0:T(8,128)(2,1)} %get-tuple-element.152.refs_0_.refs_1_, bf16[1024,1024]{1,0:T(8,128)(2,1)} %get-tuple-element.152.refs_0_.refs_1_, bf16[1024,1024]{1,0:T(8,128)(2,1)} %get-tuple-element.153.refs_2_.refs_3_, ...), custom_call_target="tpu_custom_call" | custom-call | flops 5905580032 | bytes 19398656 | tf_op jit(solution)/shard_map/pallas_call | solution.py:407
  310.4 6.9 %collective-permute-done.9 = bf16[2,256,1024]{2,1,0:T(8,128)(2,1)S(1)} collective-permute-done((bf16[2,256,1024]{2,1,0:T(8,128)(2,1)}, bf16[2,256,1024]{2,1,0:T(8,128)(2,1)S(1)}, u32[]{:S(2)}, u32[]{:S(2)}) %collective-permute-start.9) | collective-permute-done | bytes 1048608 | tf_op jit(solution)/shard_map/ppermute | solution.py:451
  322.2 6.6 %collective-permute-done.10 = bf16[256,1024]{1,0:T(8,128)(2,1)S(1)} collective-permute-done((bf16[256,1024]{1,0:T(8,128)(2,1)S(1)}, bf16[256,1024]{1,0:T(8,128)(2,1)S(1)}, u32[]{:S(2)}, u32[]{:S(2)}) %collective-permute-start.10) | collective-permute-done | bytes 524320 | tf_op jit(solution)/shard_map/ppermute | solution.py:451
  337.9 12.7 %shard_map.248 = bf16[1152,2048]{1,0:T(8,128)(2,1)} custom-call(bf16[3,384,1024]{2,1,0:T(8,128)(2,1)} %get-tuple-element.174.refs_0_.refs_1_.refs_2_, bf16[3,384,1024]{2,1,0:T(8,128)(2,1)} %get-tuple-element.174.refs_0_.refs_1_.refs_2_, bf16[3,384,1024]{2,1,0:T(8,128)(2,1)} %get-tuple-element.174.refs_0_.refs_1_.refs_2_, ...), custom_call_target="tpu_custom_call" | custom-call | flops 4831838208 | bytes 15466496 | tf_op jit(solution)/shard_map/pallas_call | solution.py:350
  355.6 7.8 %shard_map.246 = (bf16[2,256,1024]{2,1,0:T(8,128)(2,1)}, bf16[2,256,1024]{2,1,0:T(8,128)(2,1)}) custom-call(bf16[1024,1024]{1,0:T(8,128)(2,1)} %get-tuple-element.164.refs_0_.refs_1_, bf16[1024,1024]{1,0:T(8,128)(2,1)} %get-tuple-element.164.refs_0_.refs_1_, bf16[1024,384]{1,0:T(8,128)(2,1)} %get-tuple-element.165.refs_2_.refs_3_, ...), custom_call_target="tpu_custom_call" | custom-call | flops 2952790016 | bytes 10747904 | tf_op jit(solution)/shard_map/pallas_call | solution.py:407
  363.4 8.3 %shard_map.247 = (bf16[2,256,1024]{2,1,0:T(8,128)(2,1)}, bf16[2,256,1024]{2,1,0:T(8,128)(2,1)}) custom-call(bf16[1024,1024]{1,0:T(8,128)(2,1)} %get-tuple-element.164.refs_0_.refs_1_, bf16[1024,1024]{1,0:T(8,128)(2,1)} %get-tuple-element.164.refs_0_.refs_1_, bf16[1024,384]{1,0:T(8,128)(2,1)} %get-tuple-element.165.refs_2_.refs_3_, ...), custom_call_target="tpu_custom_call" | custom-call | flops 2952790016 | bytes 10747904 | tf_op jit(solution)/shard_map/pallas_call | solution.py:407
  377.3 12.7 %shard_map.249 = (bf16[1024,256]{1,0:T(8,128)(2,1)}, bf16[1024,256]{1,0:T(8,128)(2,1)}, bf16[1024,256]{1,0:T(8,128)(2,1)}, bf16[3,256,1024]{2,1,0:T(8,128)(2,1)}) custom-call(s32[3]{0:T(128)} %pad_add_fusion.place_ref.shift_ref, bf16[2048,2048]{1,0:T(8,128)(2,1)} %all-gather.4.cloned.1.call-done.wq_ref.wk_ref.wv_ref.refs_2_.wo_ref.refs_16_.refs_17_.refs_18_.refs_19_, ...), custom_call_target="tpu_custom_call" | custom-call | flops 3758096384 | bytes 9961472 | tf_op jit(solution)/shard_map/pallas_call | solution.py:221
  391.9 13.0 %shard_map.250 = (bf16[1024,256]{1,0:T(8,128)(2,1)}, bf16[1024,256]{1,0:T(8,128)(2,1)}, bf16[1024,256]{1,0:T(8,128)(2,1)}, bf16[3,256,1024]{2,1,0:T(8,128)(2,1)}) custom-call(s32[3]{0:T(128)} %pad_add_fusion.place_ref.shift_ref, bf16[2048,2048]{1,0:T(8,128)(2,1)} %all-gather.4.cloned.1.call-done.wq_ref.wk_ref.wv_ref.refs_2_.wo_ref.refs_16_.refs_17_.refs_18_.refs_19_, ...), custom_call_target="tpu_custom_call" | custom-call | flops 3758096384 | bytes 9961472 | tf_op jit(solution)/shard_map/pallas_call | solution.py:221
  405.0 9.4 %shard_map.251 = (bf16[2,256,1024]{2,1,0:T(8,128)(2,1)}, bf16[2,256,1024]{2,1,0:T(8,128)(2,1)}, bf16[2,256,1024]{2,1,0:T(8,128)(2,1)}, bf16[2,256,1024]{2,1,0:T(8,128)(2,1)}) custom-call(bf16[1024,256]{1,0:T(8,128)(2,1)} %get-tuple-element.196.refs_0_.refs_1_.refs_2_.refs_3_, bf16[1024,256]{1,0:T(8,128)(2,1)} %get-tuple-element.196.refs_0_.refs_1_.refs_2_.refs_3_, ...), custom_call_target="tpu_custom_call" | custom-call | flops 4294967296 | bytes 10485760 | tf_op jit(solution)/shard_map/pallas_call | solution.py:407
  430.8 17.9 %shard_map.255 = bf16[2048,2048]{1,0:T(8,128)(2,1)} custom-call(bf16[3,256,1024]{2,1,0:T(8,128)(2,1)} %get-tuple-element.231.refs_0_.refs_2_.refs_4_, bf16[3,256,1024]{2,1,0:T(8,128)(2,1)} %get-tuple-element.232.refs_1_.refs_3_.refs_5_, bf16[3,256,1024]{2,1,0:T(8,128)(2,1)} %get-tuple-element.231.refs_0_.refs_2_.refs_4_, ...), custom_call_target="tpu_custom_call" | custom-call | flops 8589934592 | bytes 25165824 | tf_op jit(solution)/shard_map/pallas_call | solution.py:350
  450.4 11.6 %collective-permute-done.21 = bf16[2,256,1024]{2,1,0:T(8,128)(2,1)} collective-permute-done((bf16[2,256,1024]{2,1,0:T(8,128)(2,1)}, bf16[2,256,1024]{2,1,0:T(8,128)(2,1)}, u32[]{:S(2)}, u32[]{:S(2)}) %collective-permute-start.21) | collective-permute-done | bytes 1048608 | tf_op jit(solution)/shard_map/ppermute | solution.py:451
  486.1 7.7 %collective-permute-done.25.refs_2_ = bf16[1,256,1024]{2,1,0:T(8,128)(2,1)S(1)} collective-permute-done((bf16[1,256,1024]{2,1,0:T(8,128)(2,1)S(1)}, bf16[1,256,1024]{2,1,0:T(8,128)(2,1)S(1)}, u32[]{:S(2)}, u32[]{:S(2)}) %collective-permute-start.25) | collective-permute-done | bytes 524320 | tf_op jit(solution)/shard_map/ppermute | solution.py:451
  503.1 18.6 %shard_map.254 = f32[1024,2048]{1,0:T(8,128)} custom-call(s32[3]{0:T(128)} %pad_add_fusion.place_ref.shift_ref, bf16[1024,2048]{1,0:T(8,128)(2,1)} %hidden_ref, bf16[1024,2048]{1,0:T(8,128)(2,1)} %shard_map.253.mid_ref, f32[1,2048]{1,0:T(1,128)} %copy-done.43, bf16[1,1024,256]{2,1,0:T(8,128)(2,1)} %bitcast.197, ...), custom_call_target="tpu_custom_call" | custom-call | flops 8589934592 | bytes 29360128 | tf_op jit(solution)/shard_map/pallas_call | solution.py:651
  (339 shorter events, 200.8 us)
Async XLA Ops:
  7.2 88.4 %all-gather.4.cloned.1.call-start = ((), (), s32[]{:S(2)}) async-start(), calls=%async_computation.3 | async-start | bytes 9437184 | tf_op jit(solution)/shard_map/all_gather | solution.py:713
  10.6 217.3 %all-gather.6.cloned.1.call-start = ((), (), s32[]{:S(2)}) async-start(), calls=%async_computation.4 | async-start | bytes 14155776 | tf_op jit(solution)/shard_map/all_gather | solution.py:713
  13.6 257.0 %all-gather.8.cloned.1.call-start = ((), (), s32[]{:S(2)}) async-start(), calls=%async_computation.5 | async-start | bytes 5308416 | tf_op jit(solution)/shard_map/all_gather | solution.py:713
  125.8 25.5 %collective-permute-start.1 = (bf16[2,256,1024]{2,1,0:T(8,128)(2,1)}, bf16[2,256,1024]{2,1,0:T(8,128)(2,1)S(1)}, u32[]{:S(2)}, u32[]{:S(2)}) collective-permute-start(bf16[2,256,1024]{2,1,0:T(8,128)(2,1)} %get-tuple-element.132), channel_id=1, source_target_pairs={{0,2},{1,3},{2,0},{3,1},{4,6},{5,7},{6,4},{7,5},{8,10},{9,11},{10,... | collective-permute-start | bytes 3145736 | tf_op jit(solution)/shard_map/ppermute | solution.py:451
  127.3 25.3 %collective-permute-start = (bf16[2,256,1024]{2,1,0:T(8,128)(2,1)}, bf16[2,256,1024]{2,1,0:T(8,128)(2,1)}, u32[]{:S(2)}, u32[]{:S(2)}) collective-permute-start(bf16[2,256,1024]{2,1,0:T(8,128)(2,1)} %get-tuple-element.131), channel_id=1, source_target_pairs={{0,1},{1,0},{2,3},{3,2},{4,5},{5,4},{6,7},{7,6},{8,9},{9,8},{10,11... | collective-permute-start | bytes 3145736 | tf_op jit(solution)/shard_map/ppermute | solution.py:451
  130.1 300.7 %reduce-scatter.4.cloned.1.call-start = ((), (), s32[]{:S(2)}) async-start(), calls=%async_computation.6 | async-start | bytes 14155776 | tf_op jit(solution)/shard_map/reduce_scatter | solution.py:760
  225.3 45.3 %collective-permute-start.37 = (bf16[2,1024,256]{2,1,0:T(8,128)(2,1)S(1)}, bf16[2,1024,256]{2,1,0:T(8,128)(2,1)}, u32[]{:S(2)}, u32[]{:S(2)}) collective-permute-start(bf16[2,1024,256]{2,1,0:T(8,128)(2,1)S(1)} %pad_maximum_fusion.10), channel_id=1, source_target_pairs={{0,2},{1,3},{2,0},{3,1},{4,6},{5,7},{6,4},{7,5},{8,10},{9,11},{10,... | collective-permute-start | bytes 3145736 | tf_op jit(solution)/shard_map/ppermute | solution.py:451
  226.2 44.5 %collective-permute-start.35 = (bf16[2,1024,256]{2,1,0:T(8,128)(2,1)S(1)}, bf16[2,1024,256]{2,1,0:T(8,128)(2,1)}, u32[]{:S(2)}, u32[]{:S(2)}) collective-permute-start(bf16[2,1024,256]{2,1,0:T(8,128)(2,1)S(1)} %pad_maximum_fusion.9), channel_id=1, source_target_pairs={{0,1},{1,0},{2,3},{3,2},{4,5},{5,4},{6,7},{7,6},{8,9},{9,8},{10,11... | collective-permute-start | bytes 3145736 | tf_op jit(solution)/shard_map/ppermute | solution.py:451
  270.7 271.3 %reduce-scatter.8.cloned.1.call-start = ((), (), s32[]{:S(2)}) async-start(), calls=%async_computation.8 | async-start | bytes 5308416 | tf_op jit(solution)/shard_map/reduce_scatter | solution.py:785
  350.7 196.9 %reduce-scatter.6.cloned.1.call-start = ((), (), s32[]{:S(2)}) async-start(), calls=%async_computation.7 | async-start | bytes 9437184 | tf_op jit(solution)/shard_map/reduce_scatter | solution.py:830
  350.7 25.8 %collective-permute-start.19 = (bf16[256,1024]{1,0:T(8,128)(2,1)}, bf16[256,1024]{1,0:T(8,128)(2,1)S(1)}, u32[]{:S(2)}, u32[]{:S(2)}) collective-permute-start(bf16[256,1024]{1,0:T(8,128)(2,1)} %get-tuple-element.306), channel_id=1, source_target_pairs={{0,2},{1,3},{2,0},{3,1},{4,6},{5,7},{6,4},{7,5},{8,10},{9,11},{10,... | collective-permute-start | bytes 1572872 | tf_op jit(solution)/shard_map/ppermute | solution.py:451
  352.1 24.4 %collective-permute-start.18 = (bf16[256,1024]{1,0:T(8,128)(2,1)}, bf16[256,1024]{1,0:T(8,128)(2,1)}, u32[]{:S(2)}, u32[]{:S(2)}) collective-permute-start(bf16[256,1024]{1,0:T(8,128)(2,1)} %get-tuple-element.307), channel_id=1, source_target_pairs={{0,1},{1,0},{2,3},{3,2},{4,5},{5,4},{6,7},{7,6},{8,9},{9,8},{10,11... | collective-permute-start | bytes 1572872 | tf_op jit(solution)/shard_map/ppermute | solution.py:451
  374.1 30.9 %collective-permute-start.16 = (bf16[2,256,1024]{2,1,0:T(8,128)(2,1)}, bf16[2,256,1024]{2,1,0:T(8,128)(2,1)}, u32[]{:S(2)}, u32[]{:S(2)}) collective-permute-start(bf16[2,256,1024]{2,1,0:T(8,128)(2,1)} %get-tuple-element.168), channel_id=1, source_target_pairs={{0,1},{1,0},{2,3},{3,2},{4,5},{5,4},{6,7},{7,6},{8,9},{9,8},{10,11... | collective-permute-start | bytes 3145736 | tf_op jit(solution)/shard_map/ppermute | solution.py:451
  376.4 28.6 %collective-permute-start.17 = (bf16[2,256,1024]{2,1,0:T(8,128)(2,1)}, bf16[2,256,1024]{2,1,0:T(8,128)(2,1)S(1)}, u32[]{:S(2)}, u32[]{:S(2)}) collective-permute-start(bf16[2,256,1024]{2,1,0:T(8,128)(2,1)} %get-tuple-element.169), channel_id=1, source_target_pairs={{0,2},{1,3},{2,0},{3,1},{4,6},{5,7},{6,4},{7,5},{8,10},{9,11},{10,... | collective-permute-start | bytes 3145736 | tf_op jit(solution)/shard_map/ppermute | solution.py:451
  420.9 27.8 %collective-permute-start.33 = (bf16[2,1024,256]{2,1,0:T(8,128)(2,1)S(1)}, bf16[2,1024,256]{2,1,0:T(8,128)(2,1)}, u32[]{:S(2)}, u32[]{:S(2)}) collective-permute-start(bf16[2,1024,256]{2,1,0:T(8,128)(2,1)S(1)} %pad_maximum_fusion.8), channel_id=1, source_target_pairs={{0,2},{1,3},{2,0},{3,1},{4,6},{5,7},{6,4},{7,5},{8,10},{9,11},{10,... | collective-permute-start | bytes 3145736 | tf_op jit(solution)/shard_map/ppermute | solution.py:451
  422.1 26.6 %collective-permute-start.31 = (bf16[2,1024,256]{2,1,0:T(8,128)(2,1)}, bf16[2,1024,256]{2,1,0:T(8,128)(2,1)}, u32[]{:S(2)}, u32[]{:S(2)}) collective-permute-start(bf16[2,1024,256]{2,1,0:T(8,128)(2,1)} %pad_maximum_fusion.7), channel_id=1, source_target_pairs={{0,1},{1,0},{2,3},{3,2},{4,5},{5,4},{6,7},{7,6},{8,9},{9,8},{10,11... | collective-permute-start | bytes 3145736 | tf_op jit(solution)/shard_map/ppermute | solution.py:451
  422.1 28.3 %collective-permute-start.22 = (bf16[2,256,1024]{2,1,0:T(8,128)(2,1)}, bf16[2,256,1024]{2,1,0:T(8,128)(2,1)}, u32[]{:S(2)}, u32[]{:S(2)}) collective-permute-start(bf16[2,256,1024]{2,1,0:T(8,128)(2,1)} %get-tuple-element.202), channel_id=1, source_target_pairs={{0,2},{1,3},{2,0},{3,1},{4,6},{5,7},{6,4},{7,5},{8,10},{9,11},{10,... | collective-permute-start | bytes 3145736 | tf_op jit(solution)/shard_map/ppermute | solution.py:451
  424.1 37.9 %collective-permute-start.21 = (bf16[2,256,1024]{2,1,0:T(8,128)(2,1)}, bf16[2,256,1024]{2,1,0:T(8,128)(2,1)}, u32[]{:S(2)}, u32[]{:S(2)}) collective-permute-start(bf16[2,256,1024]{2,1,0:T(8,128)(2,1)} %get-tuple-element.201), channel_id=1, source_target_pairs={{0,1},{1,0},{2,3},{3,2},{4,5},{5,4},{6,7},{7,6},{8,9},{9,8},{10,11... | collective-permute-start | bytes 3145736 | tf_op jit(solution)/shard_map/ppermute | solution.py:451
  476.8 25.0 %collective-permute-start.39 = (bf16[2,1024,256]{2,1,0:T(8,128)(2,1)}, bf16[2,1024,256]{2,1,0:T(8,128)(2,1)}, u32[]{:S(2)}, u32[]{:S(2)}) collective-permute-start(bf16[2,1024,256]{2,1,0:T(8,128)(2,1)} %collective-permute-done.35.refs_7_), channel_id=1, source_target_pairs={{0,4},{4,0},{8,12},{12,8},{16,20},{20,16},{24,28},{28,24},{1,5},{5... | collective-permute-start | bytes 3145736 | tf_op jit(solution)/shard_map/ppermute | solution.py:853
  477.4 25.7 %collective-permute-start.43 = (bf16[2,1024,256]{2,1,0:T(8,128)(2,1)}, bf16[2,1024,256]{2,1,0:T(8,128)(2,1)}, u32[]{:S(2)}, u32[]{:S(2)}) collective-permute-start(bf16[2,1024,256]{2,1,0:T(8,128)(2,1)} %collective-permute-done.37.refs_11_), channel_id=1, source_target_pairs={{0,4},{4,0},{8,12},{12,8},{16,20},{20,16},{24,28},{28,24},{1,5},{5... | collective-permute-start | bytes 3145736 | tf_op jit(solution)/shard_map/ppermute | solution.py:853
  500.5 35.7 %collective-permute-start.28 = (bf16[2,256,1024]{2,1,0:T(8,128)(2,1)}, bf16[2,256,1024]{2,1,0:T(8,128)(2,1)S(1)}, u32[]{:S(2)}, u32[]{:S(2)}) collective-permute-start(bf16[2,256,1024]{2,1,0:T(8,128)(2,1)} %pad_maximum_fusion.6), channel_id=1, source_target_pairs={{0,2},{1,3},{2,0},{3,1},{4,6},{5,7},{6,4},{7,5},{8,10},{9,11},{10,... | collective-permute-start | bytes 3145736 | tf_op jit(solution)/shard_map/ppermute | solution.py:451
  501.8 35.2 %collective-permute-start.26 = (bf16[2,256,1024]{2,1,0:T(8,128)(2,1)}, bf16[2,256,1024]{2,1,0:T(8,128)(2,1)}, u32[]{:S(2)}, u32[]{:S(2)}) collective-permute-start(bf16[2,256,1024]{2,1,0:T(8,128)(2,1)} %pad_maximum_fusion.5), channel_id=1, source_target_pairs={{0,1},{1,0},{2,3},{3,2},{4,5},{5,4},{6,7},{7,6},{8,9},{9,8},{10,11... | collective-permute-start | bytes 3145736 | tf_op jit(solution)/shard_map/ppermute | solution.py:451
  527.7 30.7 %collective-permute-start.47 = (bf16[2,256,1024]{2,1,0:T(8,128)(2,1)}, bf16[2,256,1024]{2,1,0:T(8,128)(2,1)}, u32[]{:S(2)}, u32[]{:S(2)}) collective-permute-start(bf16[2,256,1024]{2,1,0:T(8,128)(2,1)} %pad_maximum_fusion.12), channel_id=1, source_target_pairs={{0,2},{1,3},{2,0},{3,1},{4,6},{5,7},{6,4},{7,5},{8,10},{9,11},{10,... | collective-permute-start | bytes 3145736 | tf_op jit(solution)/shard_map/ppermute | solution.py:451
  529.6 29.3 %collective-permute-start.46 = (bf16[2,256,1024]{2,1,0:T(8,128)(2,1)}, bf16[2,256,1024]{2,1,0:T(8,128)(2,1)}, u32[]{:S(2)}, u32[]{:S(2)}) collective-permute-start(bf16[2,256,1024]{2,1,0:T(8,128)(2,1)} %pad_maximum_fusion.11), channel_id=1, source_target_pairs={{0,1},{1,0},{2,3},{3,2},{4,5},{5,4},{6,7},{7,6},{8,9},{9,8},{10,11... | collective-permute-start | bytes 3145736 | tf_op jit(solution)/shard_map/ppermute | solution.py:451
  (93 other events, 727.7 us)
Sparse Core Ops, SparseCore 0:
  10.7 84.7 all-gather.3
  97.2 115.2 all-gather.5
  214.2 49.9 all-gather.7
  270.8 127.1 reduce-scatter.3
  400.1 53.3 reduce-scatter.7
  462.1 85.4 reduce-scatter.5

commit v7 on v6

--- a/solution.py
+++ b/solution.py
@@ -817,7 +817,7 @@
     out_sum, out_more, out_last = scatter_end(out_state, size, width, kv_more)
     layer_own = (mid + out_sum).astype(BF)
     layer_held, layer_first = halves_start(layer_own, size)
-    layer_parts, _ = halves_end(layer_held, size)
+    layer_parts, layer_last = halves_end(layer_held, size)
     layer_out = assemble(layer_parts, place, BF)
     grads_heads = products(
         [(backs[at][3], lead, min(lead, 1)) for lead in range(3) for at in range(groups)]
@@ -843,7 +843,7 @@
     self_own_grad = s_part.astype(BF)
     self_held, self_first = halves_start(self_own_grad, size)
 
-    weights_in = after((w_gate, w_up), *self_first)
+    weights_in = after((w_gate, w_up), *layer_last)
     sum_gate, sum_up, sum_down = unit_sums(0).T, unit_sums(1).T, unit_sums(2)
     ffn_gain_sum = gain_part(ffn_gain, (weights_in[0], sum_gate), (weights_in[1], sum_up))
 
@@ -865,7 +865,7 @@
         size,
     )
     self_parts, _ = halves_end(self_held, size, [input_grad])
-    weights_in = after((w_query, w_key, w_value), *self_first)
+    weights_in = after((w_query, w_key, w_value), *layer_last)
     sum_query, sum_key, sum_value = [
         sum_heads[at * wide : (at + 1) * wide].T for at in range(3)
     ]

time: 579 us -> 579 us (level)
  transfers between devices with their start and end apart: 57 -> 57, of which waited for: 31 -> 31; matrix products, arithmetic and copies ran while one was open for 12% -> 11% of each run, Pallas kernels for 42% -> 42%
where the time goes in v7:
time: 579 us; the launch traced here: 572 us
  Pallas kernels  238 us (41%)
  waiting for transfers between devices  178 us (31%)
  other arithmetic  51.8 us (9%)
  starting transfers between devices  45.5 us (8%)
  local copies, waits for them, and re-layouts  28.4 us (5%)
  between operations  16.1 us (3%)
  blocking collectives  14.6 us (3%)
    ppermute x42, waiting for transfers between devices, swap(): return lax.ppermute(array, 'tensor', [(t, t ^ bit) for t in range(size)])  124 us
    pallas_call x7, Pallas kernels, row_products(): pl.pallas_call(functools.partial(rows_kernel, len(terms), sides, steps),...  60.4 us
    all_gather x3, waiting for transfers between devices, local(): lax.all_gather(w, 'dp', axis=0, tiled=True)  54.3 us
    pallas_call x3, Pallas kernels, products(): pl.pallas_call(functools.partial(products_kernel, counts, forms), grid=(t...  51.7 us
    ppermute x42, starting transfers between devices, swap(): return lax.ppermute(array, 'tensor', [(t, t ^ bit) for t in range(size)])  41.5 us
    pallas_call x2, Pallas kernels, feed_forward(): pl.pallas_call(feed_kernel, grid=(steps,), in_specs=[whole, whole, pl.Blo...  36.2 us
    pallas_call x2, Pallas kernels, attend_backward(): pl.pallas_call(functools.partial(backward_kernel, picks), grid=(1,), in_s...  25.7 us
    pallas_call x1, Pallas kernels, attend_forward(): pl.pallas_call(functools.partial(forward_kernel, size), grid=(groups,), i...  24.8 us
  transfers between devices with their start and end apart: 57, of which 31 were waited for; matrix products, arithmetic and copies ran while one was open for 11% of the time, Pallas kernels for 42%

profile of v7, /device:TPU:0, one launch (start us, length us, event | category | flops | bytes accessed | tf_op | source)
XLA Modules:
  0.0 572.4 jit_solution(14550486130091947513)
XLA Ops:
  14.4 14.6 %all_gather.12 = bf16[3,2048]{1,0:T(4,128)(2,1)S(1)} all-gather(bf16[3,256]{1,0:T(4,128)(2,1)S(1)} %pad_maximum_fusion.16), channel_id=1, replica_groups=mesh['dp'=8,'tensor'=4] {'dp'}, dimensions={1}, use_global_device_ids=true | all-gather | bytes 13824 | tf_op jit(solution)/shard_map/all_gather | solution.py:714
  41.3 54.3 %all-gather.4.cloned.1.call-done.wq_ref.wk_ref.wv_ref.refs_2_.wo_ref.refs_16_.refs_17_.refs_18_.refs_19_ = bf16[2048,2048]{1,0:T(8,128)(2,1)} async-done(((bf16[256,2048]{1,0:T(8,128)(2,1)}), bf16[2048,2048]{1,0:T(8,128)(2,1)}) %all-gather.4.cloned.1.call-update) | async-done | bytes 8388624 | tf_op jit(solution)/shard_map/all_gather | solution.py:713
  95.6 24.8 %shard_map.237 = (bf16[1024,512]{1,0:T(8,128)(2,1)}, bf16[1024,512]{1,0:T(8,128)(2,1)}, bf16[1024,512]{1,0:T(8,128)(2,1)}, bf16[1024,512]{1,0:T(8,128)(2,1)}, bf16[512,1024]{1,0:T(8,128)(2,1)}) custom-call(s32[3]{0:T(128)} %pad_add_fusion.place_ref.shift_ref, bf16[1024,2048]{1,0:T(8,128)(2,1)} %get-tuple-element.235.normed_ref.refs_7_, ...), custom_call_target="tpu_custom_call" | custom-call | flops 8053063680 | bytes 18874368 | tf_op jit(solution)/shard_map/pallas_call | solution.py:114
  135.7 15.6 %collective-permute-done.1 = bf16[2,256,1024]{2,1,0:T(8,128)(2,1)S(1)} collective-permute-done((bf16[2,256,1024]{2,1,0:T(8,128)(2,1)}, bf16[2,256,1024]{2,1,0:T(8,128)(2,1)S(1)}, u32[]{:S(2)}, u32[]{:S(2)}) %collective-permute-start.1) | collective-permute-done | bytes 1048608 | tf_op jit(solution)/shard_map/ppermute | solution.py:451
  159.5 9.3 %collective-permute-done.2 = bf16[256,1024]{1,0:T(8,128)(2,1)} collective-permute-done((bf16[256,1024]{1,0:T(8,128)(2,1)}, bf16[256,1024]{1,0:T(8,128)(2,1)}, u32[]{:S(2)}, u32[]{:S(2)}) %collective-permute-start.2) | collective-permute-done | bytes 524320 | tf_op jit(solution)/shard_map/ppermute | solution.py:451
  177.0 8.8 %collective-permute-done.4.refs_2_ = bf16[1,256,1024]{2,1,0:T(8,128)(2,1)S(1)} collective-permute-done((bf16[1,256,1024]{2,1,0:T(8,128)(2,1)S(1)}, bf16[1,256,1024]{2,1,0:T(8,128)(2,1)S(1)}, u32[]{:S(2)}, u32[]{:S(2)}) %collective-permute-start.4) | collective-permute-done | bytes 524320 | tf_op jit(solution)/shard_map/ppermute | solution.py:451
  197.0 13.6 %collective-permute-done.7.refs_5_ = bf16[2,256,1024]{2,1,0:T(8,128)(2,1)} collective-permute-done((bf16[2,256,1024]{2,1,0:T(8,128)(2,1)}, bf16[2,256,1024]{2,1,0:T(8,128)(2,1)}, u32[]{:S(2)}, u32[]{:S(2)}) %collective-permute-start.7) | collective-permute-done | bytes 1048608 | tf_op jit(solution)/shard_map/ppermute | solution.py:451
  227.9 21.6 %shard_map.241 = (bf16[1024,1024]{1,0:T(8,128)(2,1)}, bf16[1024,1024]{1,0:T(8,128)(2,1)}, bf16[1024,1024]{1,0:T(8,128)(2,1)}, bf16[3,1024,1024]{2,1,0:T(8,128)(2,1)}) custom-call(bf16[1024,2048]{1,0:T(8,128)(2,1)} %shard_map.240.x_ref.refs_3_, bf16[1024,2048]{1,0:T(8,128)(2,1)} %bitcast.161, ...), custom_call_target="tpu_custom_call" | custom-call | flops 12884901888 | bytes 33554432 | tf_op jit(solution)/shard_map/pallas_call | solution.py:275
  249.5 21.1 %shard_map.242 = bf16[3072,2048]{1,0:T(8,128)(2,1)} custom-call(bf16[3,1024,1024]{2,1,0:T(8,128)(2,1)} %get-tuple-element.143.refs_0_.refs_1_.refs_2_, bf16[3,1024,1024]{2,1,0:T(8,128)(2,1)} %get-tuple-element.143.refs_0_.refs_1_.refs_2_, bf16[3,1024,1024]{2,1,0:T(8,128)(2,1)} %get-tuple-element.143.refs_0_.refs_1_.refs_2_, ...), custom_call_target="tpu_custom_call" | custom-call | flops 12884901888 | bytes 27262976 | tf_op jit(solution)/shard_map/pallas_call | solution.py:350
  270.7 14.6 %shard_map.243 = (bf16[1024,384]{1,0:T(8,128)(2,1)}, bf16[1024,384]{1,0:T(8,128)(2,1)}, bf16[1024,384]{1,0:T(8,128)(2,1)}, bf16[3,384,1024]{2,1,0:T(8,128)(2,1)}) custom-call(bf16[1024,2048]{1,0:T(8,128)(2,1)} %shard_map.240.x_ref.refs_3_, bf16[1024,2048]{1,0:T(8,128)(2,1)} %bitcast.163, ...), custom_call_target="tpu_custom_call" | custom-call | flops 4831838208 | bytes 17825792 | tf_op jit(solution)/shard_map/pallas_call | solution.py:275
  285.3 11.9 %shard_map.244 = (bf16[2,256,1024]{2,1,0:T(8,128)(2,1)}, bf16[2,256,1024]{2,1,0:T(8,128)(2,1)}) custom-call(bf16[1024,1024]{1,0:T(8,128)(2,1)} %get-tuple-element.152.refs_0_.refs_1_, bf16[1024,1024]{1,0:T(8,128)(2,1)} %get-tuple-element.152.refs_0_.refs_1_, bf16[1024,1024]{1,0:T(8,128)(2,1)} %get-tuple-element.153.refs_2_.refs_3_, ...), custom_call_target="tpu_custom_call" | custom-call | flops 5905580032 | bytes 19398656 | tf_op jit(solution)/shard_map/pallas_call | solution.py:407
  298.2 12.1 %shard_map.245 = (bf16[2,256,1024]{2,1,0:T(8,128)(2,1)}, bf16[2,256,1024]{2,1,0:T(8,128)(2,1)}) custom-call(bf16[1024,1024]{1,0:T(8,128)(2,1)} %get-tuple-element.152.refs_0_.refs_1_, bf16[1024,1024]{1,0:T(8,128)(2,1)} %get-tuple-element.152.refs_0_.refs_1_, bf16[1024,1024]{1,0:T(8,128)(2,1)} %get-tuple-element.153.refs_2_.refs_3_, ...), custom_call_target="tpu_custom_call" | custom-call | flops 5905580032 | bytes 19398656 | tf_op jit(solution)/shard_map/pallas_call | solution.py:407
  310.4 6.9 %collective-permute-done.9 = bf16[2,256,1024]{2,1,0:T(8,128)(2,1)S(1)} collective-permute-done((bf16[2,256,1024]{2,1,0:T(8,128)(2,1)}, bf16[2,256,1024]{2,1,0:T(8,128)(2,1)S(1)}, u32[]{:S(2)}, u32[]{:S(2)}) %collective-permute-start.9) | collective-permute-done | bytes 1048608 | tf_op jit(solution)/shard_map/ppermute | solution.py:451
  337.9 12.7 %shard_map.248 = bf16[1152,2048]{1,0:T(8,128)(2,1)} custom-call(bf16[3,384,1024]{2,1,0:T(8,128)(2,1)} %get-tuple-element.174.refs_0_.refs_1_.refs_2_, bf16[3,384,1024]{2,1,0:T(8,128)(2,1)} %get-tuple-element.174.refs_0_.refs_1_.refs_2_, bf16[3,384,1024]{2,1,0:T(8,128)(2,1)} %get-tuple-element.174.refs_0_.refs_1_.refs_2_, ...), custom_call_target="tpu_custom_call" | custom-call | flops 4831838208 | bytes 15466496 | tf_op jit(solution)/shard_map/pallas_call | solution.py:350
  355.6 7.8 %shard_map.246 = (bf16[2,256,1024]{2,1,0:T(8,128)(2,1)}, bf16[2,256,1024]{2,1,0:T(8,128)(2,1)}) custom-call(bf16[1024,1024]{1,0:T(8,128)(2,1)} %get-tuple-element.164.refs_0_.refs_1_, bf16[1024,1024]{1,0:T(8,128)(2,1)} %get-tuple-element.164.refs_0_.refs_1_, bf16[1024,384]{1,0:T(8,128)(2,1)} %get-tuple-element.165.refs_2_.refs_3_, ...), custom_call_target="tpu_custom_call" | custom-call | flops 2952790016 | bytes 10747904 | tf_op jit(solution)/shard_map/pallas_call | solution.py:407
  363.4 8.3 %shard_map.247 = (bf16[2,256,1024]{2,1,0:T(8,128)(2,1)}, bf16[2,256,1024]{2,1,0:T(8,128)(2,1)}) custom-call(bf16[1024,1024]{1,0:T(8,128)(2,1)} %get-tuple-element.164.refs_0_.refs_1_, bf16[1024,1024]{1,0:T(8,128)(2,1)} %get-tuple-element.164.refs_0_.refs_1_, bf16[1024,384]{1,0:T(8,128)(2,1)} %get-tuple-element.165.refs_2_.refs_3_, ...), custom_call_target="tpu_custom_call" | custom-call | flops 2952790016 | bytes 10747904 | tf_op jit(solution)/shard_map/pallas_call | solution.py:407
  377.3 12.7 %shard_map.249 = (bf16[1024,256]{1,0:T(8,128)(2,1)}, bf16[1024,256]{1,0:T(8,128)(2,1)}, bf16[1024,256]{1,0:T(8,128)(2,1)}, bf16[3,256,1024]{2,1,0:T(8,128)(2,1)}) custom-call(s32[3]{0:T(128)} %pad_add_fusion.place_ref.shift_ref, bf16[2048,2048]{1,0:T(8,128)(2,1)} %all-gather.4.cloned.1.call-done.wq_ref.wk_ref.wv_ref.refs_2_.wo_ref.refs_16_.refs_17_.refs_18_.refs_19_, ...), custom_call_target="tpu_custom_call" | custom-call | flops 3758096384 | bytes 9961472 | tf_op jit(solution)/shard_map/pallas_call | solution.py:221
  391.9 13.0 %shard_map.250 = (bf16[1024,256]{1,0:T(8,128)(2,1)}, bf16[1024,256]{1,0:T(8,128)(2,1)}, bf16[1024,256]{1,0:T(8,128)(2,1)}, bf16[3,256,1024]{2,1,0:T(8,128)(2,1)}) custom-call(s32[3]{0:T(128)} %pad_add_fusion.place_ref.shift_ref, bf16[2048,2048]{1,0:T(8,128)(2,1)} %all-gather.4.cloned.1.call-done.wq_ref.wk_ref.wv_ref.refs_2_.wo_ref.refs_16_.refs_17_.refs_18_.refs_19_, ...), custom_call_target="tpu_custom_call" | custom-call | flops 3758096384 | bytes 9961472 | tf_op jit(solution)/shard_map/pallas_call | solution.py:221
  405.0 9.4 %shard_map.251 = (bf16[2,256,1024]{2,1,0:T(8,128)(2,1)}, bf16[2,256,1024]{2,1,0:T(8,128)(2,1)}, bf16[2,256,1024]{2,1,0:T(8,128)(2,1)}, bf16[2,256,1024]{2,1,0:T(8,128)(2,1)}) custom-call(bf16[1024,256]{1,0:T(8,128)(2,1)} %get-tuple-element.196.refs_0_.refs_1_.refs_2_.refs_3_, bf16[1024,256]{1,0:T(8,128)(2,1)} %get-tuple-element.196.refs_0_.refs_1_.refs_2_.refs_3_, ...), custom_call_target="tpu_custom_call" | custom-call | flops 4294967296 | bytes 10485760 | tf_op jit(solution)/shard_map/pallas_call | solution.py:407
  430.8 17.9 %shard_map.255 = bf16[2048,2048]{1,0:T(8,128)(2,1)} custom-call(bf16[3,256,1024]{2,1,0:T(8,128)(2,1)} %get-tuple-element.231.refs_0_.refs_2_.refs_4_, bf16[3,256,1024]{2,1,0:T(8,128)(2,1)} %get-tuple-element.232.refs_1_.refs_3_.refs_5_, bf16[3,256,1024]{2,1,0:T(8,128)(2,1)} %get-tuple-element.231.refs_0_.refs_2_.refs_4_, ...), custom_call_target="tpu_custom_call" | custom-call | flops 8589934592 | bytes 25165824 | tf_op jit(solution)/shard_map/pallas_call | solution.py:350
  450.4 11.6 %collective-permute-done.21 = bf16[2,256,1024]{2,1,0:T(8,128)(2,1)} collective-permute-done((bf16[2,256,1024]{2,1,0:T(8,128)(2,1)}, bf16[2,256,1024]{2,1,0:T(8,128)(2,1)}, u32[]{:S(2)}, u32[]{:S(2)}) %collective-permute-start.21) | collective-permute-done | bytes 1048608 | tf_op jit(solution)/shard_map/ppermute | solution.py:451
  486.1 7.7 %collective-permute-done.25.refs_2_ = bf16[1,256,1024]{2,1,0:T(8,128)(2,1)S(1)} collective-permute-done((bf16[1,256,1024]{2,1,0:T(8,128)(2,1)S(1)}, bf16[1,256,1024]{2,1,0:T(8,128)(2,1)S(1)}, u32[]{:S(2)}, u32[]{:S(2)}) %collective-permute-start.25) | collective-permute-done | bytes 524320 | tf_op jit(solution)/shard_map/ppermute | solution.py:451
  503.1 18.6 %shard_map.254 = f32[1024,2048]{1,0:T(8,128)} custom-call(s32[3]{0:T(128)} %pad_add_fusion.place_ref.shift_ref, bf16[1024,2048]{1,0:T(8,128)(2,1)} %hidden_ref, bf16[1024,2048]{1,0:T(8,128)(2,1)} %shard_map.253.mid_ref, f32[1,2048]{1,0:T(1,128)} %copy-done.43, bf16[1,1024,256]{2,1,0:T(8,128)(2,1)} %bitcast.197, ...), custom_call_target="tpu_custom_call" | custom-call | flops 8589934592 | bytes 29360128 | tf_op jit(solution)/shard_map/pallas_call | solution.py:651
  525.5 10.8 %collective-permute-done.28.refs_5_ = bf16[2,256,1024]{2,1,0:T(8,128)(2,1)} collective-permute-done((bf16[2,256,1024]{2,1,0:T(8,128)(2,1)}, bf16[2,256,1024]{2,1,0:T(8,128)(2,1)}, u32[]{:S(2)}, u32[]{:S(2)}) %collective-permute-start.28) | collective-permute-done | bytes 1048608 | tf_op jit(solution)/shard_map/ppermute | solution.py:451
  (339 shorter events, 196.6 us)
Async XLA Ops:
  7.2 88.4 %all-gather.4.cloned.1.call-start = ((), (), s32[]{:S(2)}) async-start(), calls=%async_computation.3 | async-start | bytes 9437184 | tf_op jit(solution)/shard_map/all_gather | solution.py:713
  10.6 217.3 %all-gather.6.cloned.1.call-start = ((), (), s32[]{:S(2)}) async-start(), calls=%async_computation.4 | async-start | bytes 14155776 | tf_op jit(solution)/shard_map/all_gather | solution.py:713
  13.6 257.0 %all-gather.8.cloned.1.call-start = ((), (), s32[]{:S(2)}) async-start(), calls=%async_computation.5 | async-start | bytes 5308416 | tf_op jit(solution)/shard_map/all_gather | solution.py:713
  125.8 25.5 %collective-permute-start.1 = (bf16[2,256,1024]{2,1,0:T(8,128)(2,1)}, bf16[2,256,1024]{2,1,0:T(8,128)(2,1)S(1)}, u32[]{:S(2)}, u32[]{:S(2)}) collective-permute-start(bf16[2,256,1024]{2,1,0:T(8,128)(2,1)} %get-tuple-element.132), channel_id=1, source_target_pairs={{0,2},{1,3},{2,0},{3,1},{4,6},{5,7},{6,4},{7,5},{8,10},{9,11},{10,... | collective-permute-start | bytes 3145736 | tf_op jit(solution)/shard_map/ppermute | solution.py:451
  127.3 25.3 %collective-permute-start = (bf16[2,256,1024]{2,1,0:T(8,128)(2,1)}, bf16[2,256,1024]{2,1,0:T(8,128)(2,1)}, u32[]{:S(2)}, u32[]{:S(2)}) collective-permute-start(bf16[2,256,1024]{2,1,0:T(8,128)(2,1)} %get-tuple-element.131), channel_id=1, source_target_pairs={{0,1},{1,0},{2,3},{3,2},{4,5},{5,4},{6,7},{7,6},{8,9},{9,8},{10,11... | collective-permute-start | bytes 3145736 | tf_op jit(solution)/shard_map/ppermute | solution.py:451
  130.1 300.7 %reduce-scatter.4.cloned.1.call-start = ((), (), s32[]{:S(2)}) async-start(), calls=%async_computation.6 | async-start | bytes 14155776 | tf_op jit(solution)/shard_map/reduce_scatter | solution.py:760
  225.3 45.3 %collective-permute-start.37 = (bf16[2,1024,256]{2,1,0:T(8,128)(2,1)S(1)}, bf16[2,1024,256]{2,1,0:T(8,128)(2,1)}, u32[]{:S(2)}, u32[]{:S(2)}) collective-permute-start(bf16[2,1024,256]{2,1,0:T(8,128)(2,1)S(1)} %pad_maximum_fusion.10), channel_id=1, source_target_pairs={{0,2},{1,3},{2,0},{3,1},{4,6},{5,7},{6,4},{7,5},{8,10},{9,11},{10,... | collective-permute-start | bytes 3145736 | tf_op jit(solution)/shard_map/ppermute | solution.py:451
  226.2 44.5 %collective-permute-start.35 = (bf16[2,1024,256]{2,1,0:T(8,128)(2,1)S(1)}, bf16[2,1024,256]{2,1,0:T(8,128)(2,1)}, u32[]{:S(2)}, u32[]{:S(2)}) collective-permute-start(bf16[2,1024,256]{2,1,0:T(8,128)(2,1)S(1)} %pad_maximum_fusion.9), channel_id=1, source_target_pairs={{0,1},{1,0},{2,3},{3,2},{4,5},{5,4},{6,7},{7,6},{8,9},{9,8},{10,11... | collective-permute-start | bytes 3145736 | tf_op jit(solution)/shard_map/ppermute | solution.py:451
  270.7 271.7 %reduce-scatter.8.cloned.1.call-start = ((), (), s32[]{:S(2)}) async-start(), calls=%async_computation.8 | async-start | bytes 5308416 | tf_op jit(solution)/shard_map/reduce_scatter | solution.py:785
  350.7 196.9 %reduce-scatter.6.cloned.1.call-start = ((), (), s32[]{:S(2)}) async-start(), calls=%async_computation.7 | async-start | bytes 9437184 | tf_op jit(solution)/shard_map/reduce_scatter | solution.py:830
  350.7 25.8 %collective-permute-start.19 = (bf16[256,1024]{1,0:T(8,128)(2,1)}, bf16[256,1024]{1,0:T(8,128)(2,1)S(1)}, u32[]{:S(2)}, u32[]{:S(2)}) collective-permute-start(bf16[256,1024]{1,0:T(8,128)(2,1)} %get-tuple-element.306), channel_id=1, source_target_pairs={{0,2},{1,3},{2,0},{3,1},{4,6},{5,7},{6,4},{7,5},{8,10},{9,11},{10,... | collective-permute-start | bytes 1572872 | tf_op jit(solution)/shard_map/ppermute | solution.py:451
  352.1 24.4 %collective-permute-start.18 = (bf16[256,1024]{1,0:T(8,128)(2,1)}, bf16[256,1024]{1,0:T(8,128)(2,1)}, u32[]{:S(2)}, u32[]{:S(2)}) collective-permute-start(bf16[256,1024]{1,0:T(8,128)(2,1)} %get-tuple-element.307), channel_id=1, source_target_pairs={{0,1},{1,0},{2,3},{3,2},{4,5},{5,4},{6,7},{7,6},{8,9},{9,8},{10,11... | collective-permute-start | bytes 1572872 | tf_op jit(solution)/shard_map/ppermute | solution.py:451
  374.1 30.9 %collective-permute-start.16 = (bf16[2,256,1024]{2,1,0:T(8,128)(2,1)}, bf16[2,256,1024]{2,1,0:T(8,128)(2,1)}, u32[]{:S(2)}, u32[]{:S(2)}) collective-permute-start(bf16[2,256,1024]{2,1,0:T(8,128)(2,1)} %get-tuple-element.168), channel_id=1, source_target_pairs={{0,1},{1,0},{2,3},{3,2},{4,5},{5,4},{6,7},{7,6},{8,9},{9,8},{10,11... | collective-permute-start | bytes 3145736 | tf_op jit(solution)/shard_map/ppermute | solution.py:451
  376.4 28.6 %collective-permute-start.17 = (bf16[2,256,1024]{2,1,0:T(8,128)(2,1)}, bf16[2,256,1024]{2,1,0:T(8,128)(2,1)S(1)}, u32[]{:S(2)}, u32[]{:S(2)}) collective-permute-start(bf16[2,256,1024]{2,1,0:T(8,128)(2,1)} %get-tuple-element.169), channel_id=1, source_target_pairs={{0,2},{1,3},{2,0},{3,1},{4,6},{5,7},{6,4},{7,5},{8,10},{9,11},{10,... | collective-permute-start | bytes 3145736 | tf_op jit(solution)/shard_map/ppermute | solution.py:451
  420.9 27.8 %collective-permute-start.33 = (bf16[2,1024,256]{2,1,0:T(8,128)(2,1)S(1)}, bf16[2,1024,256]{2,1,0:T(8,128)(2,1)}, u32[]{:S(2)}, u32[]{:S(2)}) collective-permute-start(bf16[2,1024,256]{2,1,0:T(8,128)(2,1)S(1)} %pad_maximum_fusion.8), channel_id=1, source_target_pairs={{0,2},{1,3},{2,0},{3,1},{4,6},{5,7},{6,4},{7,5},{8,10},{9,11},{10,... | collective-permute-start | bytes 3145736 | tf_op jit(solution)/shard_map/ppermute | solution.py:451
  422.1 26.6 %collective-permute-start.31 = (bf16[2,1024,256]{2,1,0:T(8,128)(2,1)}, bf16[2,1024,256]{2,1,0:T(8,128)(2,1)}, u32[]{:S(2)}, u32[]{:S(2)}) collective-permute-start(bf16[2,1024,256]{2,1,0:T(8,128)(2,1)} %pad_maximum_fusion.7), channel_id=1, source_target_pairs={{0,1},{1,0},{2,3},{3,2},{4,5},{5,4},{6,7},{7,6},{8,9},{9,8},{10,11... | collective-permute-start | bytes 3145736 | tf_op jit(solution)/shard_map/ppermute | solution.py:451
  422.1 28.3 %collective-permute-start.22 = (bf16[2,256,1024]{2,1,0:T(8,128)(2,1)}, bf16[2,256,1024]{2,1,0:T(8,128)(2,1)}, u32[]{:S(2)}, u32[]{:S(2)}) collective-permute-start(bf16[2,256,1024]{2,1,0:T(8,128)(2,1)} %get-tuple-element.202), channel_id=1, source_target_pairs={{0,2},{1,3},{2,0},{3,1},{4,6},{5,7},{6,4},{7,5},{8,10},{9,11},{10,... | collective-permute-start | bytes 3145736 | tf_op jit(solution)/shard_map/ppermute | solution.py:451
  424.1 37.9 %collective-permute-start.21 = (bf16[2,256,1024]{2,1,0:T(8,128)(2,1)}, bf16[2,256,1024]{2,1,0:T(8,128)(2,1)}, u32[]{:S(2)}, u32[]{:S(2)}) collective-permute-start(bf16[2,256,1024]{2,1,0:T(8,128)(2,1)} %get-tuple-element.201), channel_id=1, source_target_pairs={{0,1},{1,0},{2,3},{3,2},{4,5},{5,4},{6,7},{7,6},{8,9},{9,8},{10,11... | collective-permute-start | bytes 3145736 | tf_op jit(solution)/shard_map/ppermute | solution.py:451
  476.8 24.9 %collective-permute-start.39 = (bf16[2,1024,256]{2,1,0:T(8,128)(2,1)}, bf16[2,1024,256]{2,1,0:T(8,128)(2,1)}, u32[]{:S(2)}, u32[]{:S(2)}) collective-permute-start(bf16[2,1024,256]{2,1,0:T(8,128)(2,1)} %collective-permute-done.35.refs_7_), channel_id=1, source_target_pairs={{0,4},{4,0},{8,12},{12,8},{16,20},{20,16},{24,28},{28,24},{1,5},{5... | collective-permute-start | bytes 3145736 | tf_op jit(solution)/shard_map/ppermute | solution.py:853
  477.4 25.7 %collective-permute-start.43 = (bf16[2,1024,256]{2,1,0:T(8,128)(2,1)}, bf16[2,1024,256]{2,1,0:T(8,128)(2,1)}, u32[]{:S(2)}, u32[]{:S(2)}) collective-permute-start(bf16[2,1024,256]{2,1,0:T(8,128)(2,1)} %collective-permute-done.37.refs_11_), channel_id=1, source_target_pairs={{0,4},{4,0},{8,12},{12,8},{16,20},{20,16},{24,28},{28,24},{1,5},{5... | collective-permute-start | bytes 3145736 | tf_op jit(solution)/shard_map/ppermute | solution.py:853
  500.5 35.8 %collective-permute-start.28 = (bf16[2,256,1024]{2,1,0:T(8,128)(2,1)}, bf16[2,256,1024]{2,1,0:T(8,128)(2,1)}, u32[]{:S(2)}, u32[]{:S(2)}) collective-permute-start(bf16[2,256,1024]{2,1,0:T(8,128)(2,1)} %pad_maximum_fusion.6), channel_id=1, source_target_pairs={{0,2},{1,3},{2,0},{3,1},{4,6},{5,7},{6,4},{7,5},{8,10},{9,11},{10,... | collective-permute-start | bytes 3145736 | tf_op jit(solution)/shard_map/ppermute | solution.py:451
  501.8 35.2 %collective-permute-start.26 = (bf16[2,256,1024]{2,1,0:T(8,128)(2,1)}, bf16[2,256,1024]{2,1,0:T(8,128)(2,1)}, u32[]{:S(2)}, u32[]{:S(2)}) collective-permute-start(bf16[2,256,1024]{2,1,0:T(8,128)(2,1)} %pad_maximum_fusion.5), channel_id=1, source_target_pairs={{0,1},{1,0},{2,3},{3,2},{4,5},{5,4},{6,7},{7,6},{8,9},{9,8},{10,11... | collective-permute-start | bytes 3145736 | tf_op jit(solution)/shard_map/ppermute | solution.py:451
  522.9 35.5 %collective-permute-start.47 = (bf16[2,256,1024]{2,1,0:T(8,128)(2,1)}, bf16[2,256,1024]{2,1,0:T(8,128)(2,1)}, u32[]{:S(2)}, u32[]{:S(2)}) collective-permute-start(bf16[2,256,1024]{2,1,0:T(8,128)(2,1)} %pad_maximum_fusion.12), channel_id=1, source_target_pairs={{0,2},{1,3},{2,0},{3,1},{4,6},{5,7},{6,4},{7,5},{8,10},{9,11},{10,... | collective-permute-start | bytes 3145736 | tf_op jit(solution)/shard_map/ppermute | solution.py:451
  524.7 34.1 %collective-permute-start.45 = (bf16[2,256,1024]{2,1,0:T(8,128)(2,1)}, bf16[2,256,1024]{2,1,0:T(8,128)(2,1)}, u32[]{:S(2)}, u32[]{:S(2)}) collective-permute-start(bf16[2,256,1024]{2,1,0:T(8,128)(2,1)} %pad_maximum_fusion.11), channel_id=1, source_target_pairs={{0,1},{1,0},{2,3},{3,2},{4,5},{5,4},{6,7},{7,6},{8,9},{9,8},{10,11... | collective-permute-start | bytes 3145736 | tf_op jit(solution)/shard_map/ppermute | solution.py:451
  (93 other events, 757.2 us)
Sparse Core Ops, SparseCore 0:
  10.7 84.7 all-gather.3
  97.2 115.2 all-gather.5
  214.2 49.9 all-gather.7
  270.8 127.1 reduce-scatter.3
  400.1 53.3 reduce-scatter.7
  462.1 85.4 reduce-scatter.5
